TPU v7x, 32 devices: a whole 2x2x4 slice. The times are simulated.
32 devices in a mesh: grp: 2 (over y), cand: 8 (over z, x), head: 2 (over core).
Axes of the slice: x: 2, y: 2, z: 4, core: 2. Of those that a mesh axis runs over, the one named last changes fastest.
Arguments:
- queries: bfloat16 [8192, 2560], P(('grp', 'cand'), 'head'), parts along dimension 0, may hold values from -130 to 130
- keys: bfloat16 [8192, 512], P(('grp', 'cand'), 'head'), parts along dimension 0, may hold values from -5 to 5
- values: bfloat16 [8192, 512], P(('grp', 'cand'), 'head'), parts along dimension 0, may hold values from -6 to 6
- lengths: int32 [16], P('grp'), parts along dimension 0, may hold values from 257 to 512, as said below
- winners: int32 [8], P('grp'), parts along dimension 0, may hold values from 0 to 1
- score_weight: float32 [2560], P('head'), may hold values from -16 to 16
Outputs:
- first_round: bfloat16 [8192, 2560], P(('grp', 'cand'), 'head'), parts along dimension 0
- second_round: bfloat16 [4096, 2560], P(('grp', 'cand'), 'head'), parts along dimension 0
- first_score: float32 [16], P(('grp', 'cand')), parts along dimension 0
- final_round_score: float32 [16], P(('grp', 'cand')), parts along dimension 0
There are 2 independent parts, one for each index of `grp`. A program takes and returns all parts, laid end to end along the dimension named above; an argument that names none is the same for every part. Nothing has to cross between parts.
Inputs may be any that keep to these rules, and one draw needn't show every extreme that they name: lengths of all candidates lie in this range; some candidate uses all 512 slots. `winners`: 0 picks the even member 2 j of pair j, 1 the odd one.
All inputs are finite; a program needn't handle non-finite values.
Results may differ from a plain program's by a relative error of at most 0.0049.
Values may be sent and summed in bfloat16 or wider, within the bound.
No kernel may reach another device: no remote copies, remote signals or barrier semaphores. Data moves between devices by JAX's collectives and lax.ppermute only.
A program may use at most 128 MiB of HBM per device.

v0:
```python
import jax
import jax.numpy as jnp
from jax import lax
from jax.sharding import PartitionSpec as P

HD = 128


def from_partner(value, axis, stride):
    return lax.ppermute(value, axis, [(i, i ^ 1 << stride) for i in range(lax.axis_size(axis))])


def attend_spans(query_rows, key_rows, value_rows, key_valid, valid_row_mask):
    row_count = query_rows.shape[0]
    group_count = key_rows.shape[1] // HD
    ratio = query_rows.shape[1] // HD // group_count
    pieces = []
    for group_index in range(group_count):
        queries_g = query_rows[
            :, group_index * ratio * HD : (group_index + 1) * ratio * HD
        ].reshape(row_count, ratio, HD)
        keys_g = key_rows[:, group_index * HD : (group_index + 1) * HD]
        values_g = value_rows[:, group_index * HD : (group_index + 1) * HD]
        scores = jnp.einsum(
            "qrd,kd->rqk", queries_g, keys_g, preferred_element_type=jnp.float32
        ) * HD ** (-0.5)
        scores = jnp.where(key_valid[None, None, :], scores, -jnp.inf)
        peak = jnp.max(scores, axis=2, keepdims=True)
        exps = jnp.exp(scores - peak)
        weights = (exps / jnp.sum(exps, axis=2, keepdims=True)).astype(jnp.bfloat16)
        output = jnp.einsum("rqk,kd->qrd", weights, values_g, preferred_element_type=jnp.float32)
        pieces.append(output.reshape(row_count, ratio * HD))
    merged = jnp.concatenate(pieces, axis=1)
    return (merged * valid_row_mask[:, None].astype(jnp.float32)).astype(jnp.bfloat16)


def body(queries, keys, values, lengths, winners, score_weight):
    span_rows = queries.shape[0]
    half_rows = span_rows // 2
    device = lax.axis_index("cand")
    device_bit = device % 2
    pairing_index = device // 2
    partner = jnp.bitwise_xor(device, 1)
    span_positions = jnp.arange(span_rows, dtype=jnp.int32)
    own_valid = span_positions < lengths[device]
    partner_valid = span_positions < lengths[partner]
    sent_rows = lax.dynamic_slice_in_dim(queries, (1 - device_bit) * half_rows, half_rows, 0)
    paired_span_rows = from_partner(sent_rows, "cand", 0)
    companion_keys, companion_values = from_partner((keys, values), "cand", 0)
    first = attend_spans(
        queries,
        jnp.concatenate([keys, companion_keys], axis=0),
        jnp.concatenate([values, companion_values], axis=0),
        jnp.concatenate([own_valid, partner_valid], axis=0),
        own_valid,
    )
    victory_flag = winners[pairing_index]
    pair_victor_mask = device_bit == victory_flag
    remaining_candidate = 2 * pairing_index + victory_flag
    remaining_keys = jnp.where(pair_victor_mask, keys, companion_keys)
    remaining_values = jnp.where(pair_victor_mask, values, companion_values)
    rival_pair = jnp.bitwise_xor(pairing_index, 1)
    rival = 2 * rival_pair + winners[rival_pair]
    challenger_keys, challenger_values = from_partner((remaining_keys, remaining_values), "cand", 1)
    remaining_valid = span_positions < lengths[remaining_candidate]
    challenger_valid = span_positions < lengths[rival]
    bout_key_rows = jnp.concatenate([remaining_keys, challenger_keys], axis=0)
    bout_value_rows = jnp.concatenate([remaining_values, challenger_values], axis=0)
    bout_valid_mask = jnp.concatenate([remaining_valid, challenger_valid], axis=0)
    local_span_rows = lax.dynamic_slice_in_dim(queries, device_bit * half_rows, half_rows, 0)
    advancing_rows = jnp.where(pair_victor_mask, local_span_rows, paired_span_rows)
    valid_row_mask = lax.dynamic_slice_in_dim(remaining_valid, device_bit * half_rows, half_rows, 0)
    later_round = attend_spans(
        advancing_rows, bout_key_rows, bout_value_rows, bout_valid_mask, valid_row_mask
    )
    first_part = jnp.sum(first.astype(jnp.float32) * score_weight[None, :]).reshape(1)
    second_part = jnp.sum(later_round.astype(jnp.float32) * score_weight[None, :]).reshape(1)
    first_total, latter_half = lax.psum((first_part, second_part), "head")
    opposite_half = from_partner(latter_half, "cand", 0)
    first_score = first_total / lengths[device].astype(jnp.float32)
    final_round_score = (latter_half + opposite_half) / lengths[remaining_candidate].astype(
        jnp.float32
    )
    return (first, later_round, first_score, final_round_score)


def solution(mesh):
    in_specs = (
        P(("grp", "cand"), "head"),
        P(("grp", "cand"), "head"),
        P(("grp", "cand"), "head"),
        P("grp"),
        P("grp"),
        P("head"),
    )
    out_specs = (
        P(("grp", "cand"), "head"),
        P(("grp", "cand"), "head"),
        P(("grp", "cand")),
        P(("grp", "cand")),
    )
    return jax.shard_map(body, mesh=mesh, in_specs=in_specs, out_specs=out_specs, check_vma=False)
```

profile of v0, /device:TPU:0, one launch (start us, length us, event | category | flops | bytes accessed | tf_op | source)
XLA Modules:
  0.0 85.4 jit_solution(17797963077633017307)
XLA Ops:
  0.6 3.0 %collective-permute-start.1 = (bf16[512,256]{1,0:T(8,128)(2,1)}, bf16[512,256]{1,0:T(8,128)(2,1)}, u32[]{:S(2)}, u32[]{:S(2)}) collective-permute-start(bf16[512,256]{1,0:T(8,128)(2,1)} %param.7), channel_id=1, source_target_pairs={{0,2},{2,0},{4,6},{6,4},{8,10},{10,8},{12,14},{14,12},{1,3},{3,1},... | collective-permute-start | bytes 786440 | tf_op jit(solution)/shard_map/ppermute | solution.py:10
  3.7 1.4 %constant_dynamic-slice_fusion = (bf16[256,1280]{1,0:T(8,128)(2,1)S(1)}, bf16[256,1280]{1,0:T(8,128)(2,1)S(1)}) fusion(bf16[512,1280]{1,0:T(8,128)(2,1)} %param.6, s32[]{:T(128)S(6)} %select_n.101, s32[]{:T(128)S(6)} %select_n.100), kind=kLoop, calls=%fused_computation.93 | loop fusion | bytes 2621448 | tf_op jit(solution)/shard_map/dynamic_slice | solution.py:47
  5.2 1.1 %copy.61 = bf16[256,1280]{0,1:T(8,128)(2,1)} copy(bf16[256,1280]{1,0:T(8,128)(2,1)S(1)} %get-tuple-element.10) | data formatting | bytes 1310720
  6.2 1.9 %collective-permute-start.4 = (bf16[256,1280]{0,1:T(8,128)(2,1)}, bf16[256,1280]{0,1:T(8,128)(2,1)}, u32[]{:S(2)}, u32[]{:S(2)}) collective-permute-start(bf16[256,1280]{0,1:T(8,128)(2,1)} %copy.61), channel_id=1, source_target_pairs={{0,2},{2,0},{4,6},{6,4},{8,10},{10,8},{12,14},{14,12},{1,3},{3,1},... | collective-permute-start | bytes 1966088 | tf_op jit(solution)/shard_map/ppermute | solution.py:10
  8.2 1.3 %fusion.95 = (s32[1]{0:T(128)}, s32[1]{0:T(128)}) fusion(s32[4]{0:T(128)} %param.10, s32[]{:T(128)S(6)} %select_n.96, s32[]{:T(128)S(6)} %select_n.92), kind=kLoop, calls=%fused_computation.109 | loop fusion | bytes 24 | tf_op jit(solution)/shard_map/dynamic_slice | solution.py:63
  10.8 1.4 %fusion.92 = (bf16[512,640]{1,0:T(8,128)(2,1)S(1)}, bf16[512,640]{1,0:T(8,128)(2,1)S(1)}) fusion(bf16[512,1280]{1,0:T(8,128)(2,1)} %param.6), kind=kLoop, calls=%fused_computation.106 | loop fusion | bytes 2621440 | tf_op jit(solution)/shard_map/slice | solution.py:19
  13.5 1.3 %iota_compare_fusion.2 = (pred[512]{0:T(512)(128)(4,1)S(1)}, pred[512]{0:T(512)(128)(4,1)S(1)}) fusion(s32[]{:T(128)} %bitcast.2, s32[]{:T(128)} %bitcast.1), kind=kLoop, calls=%fused_computation.86 | loop fusion | flops 1024 | bytes 1032 | tf_op jit(solution)/shard_map/lt | solution.py:46
  18.6 1.1 %copy.59 = bf16[512,640]{0,1:T(8,128)(2,1)} copy(bf16[512,640]{1,0:T(8,128)(2,1)S(1)} %get-tuple-element.13) | data formatting | bytes 1310720
  20.2 1.7 %broadcast_select_fusion.1 = (bf16[512,256]{1,0:T(8,128)(2,1)}, bf16[1024,256]{1,0:T(8,128)(2,1)S(1)}) fusion(bf16[512,256]{1,0:T(8,128)(2,1)S(1)} %copy-done, bf16[512,256]{1,0:T(8,128)(2,1)} %collective-permute-done.1, pred[]{:T(512)S(6)} %eq.5, bf16[1024,256]{1,0:T(8,128)(2,1)S(1)} %constant_dynamic-update-slice_fusion.3), kind=kLoop, calls=%fused_computation.72 | loop fusion | flops 131072 | bytes 1048577 | tf_op jit(solution)/shard_map/jit(_where)/select_n | solution.py:60
  22.0 8.5 %fusion.96 = (f32[5,512]{1,0:T(8,128)S(1)}, f32[5,512,1024]{1,2,0:T(8,128)}) fusion(pred[1024]{0:T(1024)(128)(4,1)S(1)} %pad_add_fusion, bf16[512,5,128]{0,2,1:T(8,128)(2,1)} %bitcast.141, bf16[1024,256]{1,0:T(8,128)(2,1)S(1)} %get-tuple-element.19), kind=kOutput, calls=%fused_computation.110 | convolution fusion | flops 681575424 | bytes 11414528 | tf_op jit(solution)/shard_map/sub | solution.py:29
  30.5 5.8 %fusion.97 = (f32[5,512]{1,0:T(8,128)S(1)}, f32[5,512,1024]{1,2,0:T(8,128)}) fusion(pred[1024]{0:T(1024)(128)(4,1)S(1)} %pad_add_fusion, bf16[512,5,128]{0,2,1:T(8,128)(2,1)S(1)} %bitcast.140, bf16[1024,256]{1,0:T(8,128)(2,1)S(1)} %get-tuple-element.19), kind=kOutput, calls=%fused_computation.111 | convolution fusion | flops 681575424 | bytes 11414528 | tf_op jit(solution)/shard_map/sub | solution.py:29
  37.1 5.3 %fusion.23 = f32[128,5,512]{2,0,1:T(8,128)S(1)} fusion(f32[5,512,1024]{1,2,0:T(8,128)} %get-tuple-element.27, f32[5,512]{1,0:T(8,128)S(1)} %get-tuple-element.26, bf16[1024,256]{1,0:T(8,128)(2,1)S(1)} %get-tuple-element.17), kind=kOutput, calls=%fused_computation.35 | convolution fusion | flops 676331520 | bytes 12075008 | tf_op jit(solution)/shard_map/rqk,kd->qrd/dot_general | solution.py:31
  43.6 1.9 %fusion.22 = f32[128,5,512]{2,0,1:T(8,128)} fusion(f32[5,512,1024]{1,2,0:T(8,128)S(1)} %bitcast.147, f32[5,512]{1,0:T(8,128)S(1)} %get-tuple-element.28, bf16[1024,256]{1,0:T(8,128)(2,1)S(1)} %get-tuple-element.17), kind=kOutput, calls=%fused_computation.34 | convolution fusion | flops 676331520 | bytes 12075008 | tf_op jit(solution)/shard_map/rqk,kd->qrd/dot_general | solution.py:31
  46.0 1.7 %copy.30 = f32[512,640]{1,0:T(8,128)S(1)} copy(f32[512,640]{0,1:T(8,128)} %bitcast.139) | data formatting | bytes 2621440 | tf_op jit(solution)/shard_map/reshape | solution.py:32
  47.7 1.7 %collective-permute-start.3 = (bf16[512,256]{1,0:T(8,128)(2,1)S(1)}, bf16[512,256]{1,0:T(8,128)(2,1)S(1)}, u32[]{:S(2)}, u32[]{:S(2)}) collective-permute-start(bf16[512,256]{1,0:T(8,128)(2,1)S(1)} %copy-done.2), channel_id=1, source_target_pairs={{0,4},{2,6},{4,0},{6,2},{8,12},{10,14},{12,8},{14,10},{1,5},{3,7},... | collective-permute-start | bytes 786440 | tf_op jit(solution)/shard_map/ppermute | solution.py:10
  49.8 2.5 %multiply_reduce_fusion = (f32[]{:T(128)}, bf16[512,1280]{1,0:T(8,128)(2,1)}) fusion(f32[1280]{0:T(1024)S(1)} %copy-done.4, f32[512]{0:T(512)S(1)} %fusion.89, f32[512,640]{1,0:T(8,128)S(1)} %copy.31, f32[512,640]{1,0:T(8,128)S(1)} %copy.30), kind=kLoop, calls=%fused_computation.40 | loop fusion | flops 3932159 | bytes 3939332 | tf_op jit(solution)/shard_map/reduce_sum | solution.py:76
  52.4 4.6 %collective-permute-done.3 = bf16[512,256]{1,0:T(8,128)(2,1)S(1)} collective-permute-done((bf16[512,256]{1,0:T(8,128)(2,1)S(1)}, bf16[512,256]{1,0:T(8,128)(2,1)S(1)}, u32[]{:S(2)}, u32[]{:S(2)}) %collective-permute-start.3) | collective-permute-done | bytes 262176 | tf_op jit(solution)/shard_map/ppermute | solution.py:10
  57.8 4.9 %fusion.98 = (f32[5,256]{1,0:T(8,128)S(1)}, f32[5,256,1024]{1,2,0:T(8,128)}) fusion(pred[1024]{0:T(1024)(128)(4,1)} %pad_add_fusion.1, bf16[256,5,128]{0,2,1:T(8,128)(2,1)S(1)} %bitcast.145, bf16[512,256]{1,0:T(8,128)(2,1)} %copy-done.7, bf16[512,256]{1,0:T(8,128)(2,1)S(1)} %copy-done.2), kind=kOutput, calls=%fused_computation.112 | convolution fusion | flops 341312512 | bytes 6100992 | tf_op jit(solution)/shard_map/sub | solution.py:29
  62.7 3.1 %fusion.40 = f32[128,5,256]{2,0,1:T(8,128)S(1)} fusion(f32[5,256,1024]{1,2,0:T(8,128)} %get-tuple-element.31, f32[5,256]{1,0:T(8,128)S(1)} %get-tuple-element.30, bf16[512,256]{1,0:T(8,128)(2,1)} %collective-permute-done.2, bf16[512,256]{1,0:T(8,128)(2,1)S(1)} %copy-done.3), kind=kOutput, calls=%fused_computation.48 | convolution fusion | flops 338690048 | bytes 6427648 | tf_op jit(solution)/shard_map/rqk,kd->qrd/dot_general | solution.py:31
  66.1 4.0 %fusion.103 = (f32[5,256]{1,0:T(8,128)S(1)}, f32[5,256,1024]{1,2,0:T(8,128)}) fusion(pred[1024]{0:T(1024)(128)(4,1)S(1)} %copy-done.6, bf16[256,5,128]{0,2,1:T(8,128)(2,1)S(1)} %bitcast.144, bf16[512,256]{1,0:T(8,128)(2,1)S(1)} %copy-done.2, bf16[512,256]{1,0:T(8,128)(2,1)S(1)} %copy-done.8), kind=kOutput, calls=%fused_computation.113 | convolution fusion | flops 341312512 | bytes 6100992 | tf_op jit(solution)/shard_map/sub | solution.py:29
  70.0 3.1 %fusion.39 = f32[128,5,256]{2,0,1:T(8,128)S(1)} fusion(f32[5,256,1024]{1,2,0:T(8,128)} %get-tuple-element.33, f32[5,256]{1,0:T(8,128)S(1)} %get-tuple-element.32, bf16[512,256]{1,0:T(8,128)(2,1)S(1)} %copy-done.3, bf16[512,256]{1,0:T(8,128)(2,1)} %collective-permute-done.2), kind=kOutput, calls=%fused_computation.47 | convolution fusion | flops 338690048 | bytes 6427648 | tf_op jit(solution)/shard_map/rqk,kd->qrd/dot_general | solution.py:31
  73.4 1.6 %multiply_reduce_fusion.1 = (f32[]{:T(128)}, bf16[256,1280]{1,0:T(8,128)(2,1)}) fusion(f32[1280]{0:T(1024)S(1)} %copy-done.4, f32[256]{0:T(256)S(1)} %dynamic-slice_convert_fusion, f32[256,640]{1,0:T(8,128)S(1)} %copy.41, f32[256,640]{1,0:T(8,128)S(1)} %copy.40), kind=kLoop, calls=%fused_computation.51 | loop fusion | flops 1966079 | bytes 1972228 | tf_op jit(solution)/shard_map/reduce_sum | solution.py:77
  75.0 3.1 %all-reduce = (f32[1]{0:T(128)}, f32[1]{0:T(128)}) all-reduce(f32[1]{0:T(128)} %bitcast.30, f32[1]{0:T(128)} %bitcast.32), channel_id=1, replica_groups=mesh['grp'=2,'cand'=8,'head'=2] {'head'}, use_global_device_ids=true, to_apply=%region_9.10 | all-reduce | flops 2 | bytes 16 | tf_op jit(solution)/shard_map/psum | solution.py:78
  78.9 3.0 %collective-permute-done.5 = f32[1]{0:T(128)} collective-permute-done((f32[1]{0:T(128)}, f32[1]{0:T(128)}, u32[]{:S(2)}, u32[]{:S(2)}) %collective-permute-start.5) | collective-permute-done | bytes 36 | tf_op jit(solution)/shard_map/ppermute | solution.py:10
  (49 shorter events, 8.0 us)
Async XLA Ops:
  0.6 11.6 %copy-start.5 = (s32[8]{0:T(128)S(1)}, s32[8]{0:T(128)}, u32[]{:S(2)}) copy-start(s32[8]{0:T(128)} %param.9) | copy-start | bytes 100
  0.6 19.6 %collective-permute-start.1 = (bf16[512,256]{1,0:T(8,128)(2,1)}, bf16[512,256]{1,0:T(8,128)(2,1)}, u32[]{:S(2)}, u32[]{:S(2)}) collective-permute-start(bf16[512,256]{1,0:T(8,128)(2,1)} %param.7), channel_id=1, source_target_pairs={{0,2},{2,0},{4,6},{6,4},{8,10},{10,8},{12,14},{14,12},{1,3},{3,1},... | collective-permute-start | bytes 786440 | tf_op jit(solution)/shard_map/ppermute | solution.py:10
  3.6 32.7 %collective-permute-start = (bf16[512,256]{1,0:T(8,128)(2,1)}, bf16[512,256]{1,0:T(8,128)(2,1)S(1)}, u32[]{:S(2)}, u32[]{:S(2)}) collective-permute-start(bf16[512,256]{1,0:T(8,128)(2,1)} %param.8), channel_id=1, source_target_pairs={{0,2},{2,0},{4,6},{6,4},{8,10},{10,8},{12,14},{14,12},{1,3},{3,1},... | collective-permute-start | bytes 786440 | tf_op jit(solution)/shard_map/ppermute | solution.py:10
  3.7 16.4 %copy-start = (bf16[512,256]{1,0:T(8,128)(2,1)S(1)}, bf16[512,256]{1,0:T(8,128)(2,1)}, u32[]{:S(2)}) copy-start(bf16[512,256]{1,0:T(8,128)(2,1)} %param.7) | copy-start | bytes 786436
  3.7 16.5 %copy-start.1 = (bf16[512,256]{1,0:T(8,128)(2,1)S(1)}, bf16[512,256]{1,0:T(8,128)(2,1)}, u32[]{:S(2)}) copy-start(bf16[512,256]{1,0:T(8,128)(2,1)} %param.8) | copy-start | bytes 786436
  6.2 46.0 %collective-permute-start.4 = (bf16[256,1280]{0,1:T(8,128)(2,1)}, bf16[256,1280]{0,1:T(8,128)(2,1)}, u32[]{:S(2)}, u32[]{:S(2)}) collective-permute-start(bf16[256,1280]{0,1:T(8,128)(2,1)} %copy.61), channel_id=1, source_target_pairs={{0,2},{2,0},{4,6},{6,4},{8,10},{10,8},{12,14},{14,12},{1,3},{3,1},... | collective-permute-start | bytes 1966088 | tf_op jit(solution)/shard_map/ppermute | solution.py:10
  36.3 6.1 %slice-start = ((s8[10485760]{0:T(1024)(128)(4,1)}), s8[4194304]{0:T(1024)(128)(4,1)S(1)}, s32[]{:S(2)}) async-start(s8[10485760]{0:T(1024)(128)(4,1)} %bitcast.146), calls=%async_computation | async-start | bytes 8388608
  37.1 5.9 %slice-start.1 = ((s8[10485760]{0:T(1024)(128)(4,1)}), s8[4194304]{0:T(1024)(128)(4,1)S(1)}, s32[]{:S(2)}) async-start(s8[10485760]{0:T(1024)(128)(4,1)} %bitcast.146), calls=%async_computation.1 | async-start | bytes 8388608
  37.1 6.5 %slice-start.2 = ((s8[10485760]{0:T(1024)(128)(4,1)}), s8[2097152]{0:T(1024)(128)(4,1)S(1)}, s32[]{:S(2)}) async-start(s8[10485760]{0:T(1024)(128)(4,1)} %bitcast.146), calls=%async_computation.2 | async-start | bytes 4194304
  45.6 2.1 %copy-start.2 = (bf16[512,256]{1,0:T(8,128)(2,1)S(1)}, bf16[512,256]{1,0:T(8,128)(2,1)}, u32[]{:S(2)}) copy-start(bf16[512,256]{1,0:T(8,128)(2,1)} %get-tuple-element.18) | copy-start | bytes 786436
  45.6 4.2 %copy-start.4 = (f32[1280]{0:T(1024)S(1)}, f32[1280]{0:T(1024)}, u32[]{:S(2)}) copy-start(f32[1280]{0:T(1024)} %param.11) | copy-start | bytes 15364
  47.7 9.3 %collective-permute-start.3 = (bf16[512,256]{1,0:T(8,128)(2,1)S(1)}, bf16[512,256]{1,0:T(8,128)(2,1)S(1)}, u32[]{:S(2)}, u32[]{:S(2)}) collective-permute-start(bf16[512,256]{1,0:T(8,128)(2,1)S(1)} %copy-done.2), channel_id=1, source_target_pairs={{0,4},{2,6},{4,0},{6,2},{8,12},{10,14},{12,8},{14,10},{1,5},{3,7},... | collective-permute-start | bytes 786440 | tf_op jit(solution)/shard_map/ppermute | solution.py:10
  49.4 13.3 %collective-permute-start.2 = (bf16[512,256]{1,0:T(8,128)(2,1)}, bf16[512,256]{1,0:T(8,128)(2,1)}, u32[]{:S(2)}, u32[]{:S(2)}) collective-permute-start(bf16[512,256]{1,0:T(8,128)(2,1)} %get-tuple-element.16), channel_id=1, source_target_pairs={{0,4},{2,6},{4,0},{6,2},{8,12},{10,14},{12,8},{14,10},{1,5},{3,7},... | collective-permute-start | bytes 786440 | tf_op jit(solution)/shard_map/ppermute | solution.py:10
  52.4 10.3 %copy-start.3 = (bf16[512,256]{1,0:T(8,128)(2,1)S(1)}, bf16[512,256]{1,0:T(8,128)(2,1)}, u32[]{:S(2)}) copy-start(bf16[512,256]{1,0:T(8,128)(2,1)} %get-tuple-element.16) | copy-start | bytes 786436
  57.0 0.7 copy-start.7
  62.6 3.4 %copy-start.6 = (pred[1024]{0:T(1024)(128)(4,1)S(1)}, pred[1024]{0:T(1024)(128)(4,1)}, u32[]{:S(2)}) copy-start(pred[1024]{0:T(1024)(128)(4,1)} %pad_add_fusion.1) | copy-start | bytes 3076
  62.7 3.4 %copy-start.8 = (bf16[512,256]{1,0:T(8,128)(2,1)S(1)}, bf16[512,256]{1,0:T(8,128)(2,1)}, u32[]{:S(2)}) copy-start(bf16[512,256]{1,0:T(8,128)(2,1)} %copy-done.7) | copy-start | bytes 786436
  78.1 3.7 %collective-permute-start.5 = (f32[1]{0:T(128)}, f32[1]{0:T(128)}, u32[]{:S(2)}, u32[]{:S(2)}) collective-permute-start(f32[1]{0:T(128)} %get-tuple-element.5), channel_id=1, source_target_pairs={{0,2},{2,0},{4,6},{6,4},{8,10},{10,8},{12,14},{14,12},{1,3},{3,1},... | collective-permute-start | bytes 20 | tf_op jit(solution)/shard_map/ppermute | solution.py:10
where the time goes:
time: 85.8 us; the launch traced here: 85.4 us
  matrix products  36.7 us (43%)
  local copies, waits for them, and re-layouts  12 us (14%)
  other arithmetic  10.5 us (12%)
  between operations  8.24 us (10%)
  waiting for transfers between devices  7.57 us (9%)
  starting transfers between devices  7.21 us (8%)
  blocking collectives  3.11 us (4%)
    sub x4, matrix products, attend_spans(): exps = jnp.exp(scores - peak)  23.2 us
    dot_general x4, matrix products, attend_spans(): jnp.einsum('rqk,kd->qrd', weights, values_g, preferred_element_type=jnp.f...  13.5 us
    ppermute x6, waiting for transfers between devices, from_partner(): lax.ppermute(value, axis, [(i, i ^ 1 << stride) for i in range(lax.axis_s...  7.57 us
    ppermute x6, starting transfers between devices, from_partner(): lax.ppermute(value, axis, [(i, i ^ 1 << stride) for i in range(lax.axis_s...  7.21 us
    unnamed x30, local copies, waits for them, and re-layouts  4.66 us
    psum x1, blocking collectives, body(): first_total, latter_half = lax.psum((first_part, second_part), 'head')  3.11 us
    reshape x4, local copies, waits for them, and re-layouts, attend_spans(): pieces.append(output.reshape(row_count, ratio * HD))  2.57 us
    reduce_sum x1, other arithmetic, body(): jnp.sum(first.astype(jnp.float32) * score_weight[None, :]).reshape(1)  2.46 us
  transfers between devices with their start and end apart: 6, of which 2 were waited for; matrix products, arithmetic and copies ran while one was open for 53% of the time, Pallas kernels for 0%

commit v1 on v0

v1 whole, which is shorter than its diff:
```python
import functools

import jax
import jax.numpy as jnp
from jax import lax
from jax.experimental import pallas as pl
from jax.experimental.pallas import tpu as pltpu
from jax.sharding import PartitionSpec as P

HD = 128
LANES = 128
FACTOR = HD ** (-0.5) * 1.4426950408889634
BARRED = -1e30
VMEM_LIMIT = 40 * 1024 * 1024
ANY = pl.BlockSpec(memory_space=pl.ANY)
SMEM = pl.BlockSpec(memory_space=pltpu.SMEM)


def from_partner(value, axis, stride):
    return lax.ppermute(value, axis, [(i, i ^ 1 << stride) for i in range(lax.axis_size(axis))])


def fill_constant_columns(k_buf, v_buf, valid_a, valid_b):
    span = k_buf.shape[0] // 2
    row = lax.broadcasted_iota(jnp.int32, (span, LANES), 0)
    first_lane = lax.broadcasted_iota(jnp.int32, (span, LANES), 1) == 0
    for place, valid in ((0, valid_a), (1, valid_b)):
        bar = jnp.where(first_lane & (row >= valid), BARRED, 0.0)
        k_buf[place * span : (place + 1) * span, HD:] = bar.astype(k_buf.dtype)
    v_buf[:, HD:] = jnp.ones((2 * span, LANES), v_buf.dtype)


def attend_rows(q, k_buf, v_buf, valid_rows, first_row):
    rows = q.shape[0]
    lane = lax.broadcasted_iota(jnp.int32, (rows, LANES), 1)
    one_lane = jnp.where(lane == 0, 1.0, 0.0).astype(q.dtype)
    wide_q = jnp.concatenate([q, one_lane], axis=1)
    scores = lax.dot_general(
        wide_q, k_buf[...], (((1,), (1,)), ((), ())), preferred_element_type=jnp.float32
    )
    peak = jnp.max(scores, axis=1, keepdims=True)
    exps = jnp.exp2((scores - peak) * FACTOR).astype(v_buf.dtype)
    both = jnp.dot(exps, v_buf[...], preferred_element_type=jnp.float32)
    output = both[:, :HD] / both[:, HD:]
    row = lax.broadcasted_iota(jnp.int32, (rows, LANES), 0) + first_row
    return jnp.where(row < valid_rows, output, 0.0).astype(q.dtype)


def attend_kernel(
    group, ratio, row_block, picked,
    info_ref, weight_ref, q_ref, other_q_ref, ka_ref, va_ref, kb_ref, vb_ref, prior_ref,
    out_ref, part_ref,
    q_buf, k_buf, v_buf, out_buf, q_sems, k_sems, out_sems,
):
    rows = q_buf.shape[0]
    span = k_buf.shape[0] // 2
    first_row = pl.multiple_of(info_ref[2], 16)
    columns = [pl.ds((group * ratio + h) * HD, HD) for h in range(ratio)]
    near = [pl.ds(h * HD, HD) for h in range(ratio)]
    kv_columns = pl.ds(group * HD, HD)

    def kv_copy(index):
        ref, buf, place = ((ka_ref, k_buf, 0), (kb_ref, k_buf, 1), (va_ref, v_buf, 0), (vb_ref, v_buf, 1))[index]
        source = ref if ref.shape[1] == HD else ref.at[:, kv_columns]
        return pltpu.make_async_copy(source, buf.at[pl.ds(place * span, span), pl.ds(0, HD)], k_sems.at[index])

    def own_q(h):
        return pltpu.make_async_copy(
            q_ref.at[pl.ds(first_row, rows), columns[h]], q_buf.at[:, near[h]], q_sems.at[h]
        )

    def other_q(h):
        return pltpu.make_async_copy(other_q_ref.at[:, near[h]], q_buf.at[:, near[h]], q_sems.at[h])

    kv_copy(0).start()
    kv_copy(1).start()
    if picked:
        @pl.when(info_ref[3] == 1)
        def _():
            for h in range(ratio):
                own_q(h).start()

        @pl.when(info_ref[3] != 1)
        def _():
            for h in range(ratio):
                other_q(h).start()
    else:
        for h in range(ratio):
            own_q(h).start()
    kv_copy(2).start()
    kv_copy(3).start()
    fill_constant_columns(k_buf, v_buf, info_ref[0], info_ref[1])
    for index in range(4):
        kv_copy(index).wait()

    total = jnp.zeros((8, LANES), jnp.float32)
    for h in range(ratio):
        own_q(h).wait()
        weight = weight_ref[:, (group * ratio + h) * HD : (group * ratio + h + 1) * HD]
        head_total = jnp.zeros((8, LANES), jnp.float32)
        for start in range(0, rows, row_block):
            output = attend_rows(
                q_buf[start : start + row_block, h * HD : (h + 1) * HD], k_buf, v_buf, info_ref[0], first_row + start
            )
            out_buf[start : start + row_block, h * HD : (h + 1) * HD] = output
            head_total += jnp.sum(output.astype(jnp.float32).reshape(row_block // 8, 8, LANES), axis=0)
        total += head_total * weight
        pltpu.make_async_copy(out_buf.at[:, near[h]], out_ref.at[:, columns[h]], out_sems.at[h]).start()
    part_ref[...] = jnp.full(part_ref.shape, jnp.sum(total), jnp.float32)
    for h in range(ratio):
        pltpu.make_async_copy(out_buf.at[:, near[h]], out_ref.at[:, columns[h]], out_sems.at[h]).wait()


def attend(group, rows, info, weight, q, other_q, ka, va, kb, vb, prior):
    span = ka.shape[0]
    groups = ka.shape[1] // HD
    ratio = q.shape[1] // HD // groups
    row_block = min(rows, 256)
    picked = other_q is not None
    out_shape = (jax.ShapeDtypeStruct((rows, q.shape[1]), q.dtype), jax.ShapeDtypeStruct((8, LANES), jnp.float32))
    if not picked:
        other_q = q
    aliased = prior is not None
    if not aliased:
        prior = jnp.zeros((8, LANES), jnp.float32)
    flops = 4 * rows * ratio * HD * 2 * span
    return pl.pallas_call(
        functools.partial(attend_kernel, group, ratio, row_block, picked),
        out_shape=out_shape,
        in_specs=[SMEM, pl.BlockSpec(memory_space=pltpu.VMEM)] + [ANY] * 7,
        out_specs=(ANY, pl.BlockSpec(memory_space=pltpu.VMEM)),
        input_output_aliases={8: 0} if aliased else {},
        scratch_shapes=[
            pltpu.VMEM((rows, ratio * HD), q.dtype),
            pltpu.VMEM((2 * span, HD + LANES), ka.dtype),
            pltpu.VMEM((2 * span, HD + LANES), va.dtype),
            pltpu.VMEM((rows, ratio * HD), q.dtype),
            pltpu.SemaphoreType.DMA((ratio,)),
            pltpu.SemaphoreType.DMA((4,)),
            pltpu.SemaphoreType.DMA((ratio,)),
        ],
        compiler_params=pltpu.CompilerParams(vmem_limit_bytes=VMEM_LIMIT),
        cost_estimate=pl.CostEstimate(
            flops=flops, bytes_accessed=4 * rows * ratio * HD, transcendentals=rows * ratio * 2 * span
        ),
    )(info, weight, q, other_q, ka, va, kb, vb, prior)


def body(queries, keys, values, lengths, winners, score_weight):
    span = queries.shape[0]
    half = span // 2
    groups = keys.shape[1] // HD
    width = queries.shape[1] // groups
    device = lax.axis_index("cand")
    bit = device % 2
    pair = device // 2
    partner = jnp.bitwise_xor(device, 1)
    winner = winners[pair]
    survivor = 2 * pair + winner
    rival_pair = jnp.bitwise_xor(pair, 1)
    rival = 2 * rival_pair + winners[rival_pair]
    won = bit == winner
    weight = score_weight.reshape(1, -1)
    first_info = jnp.stack([lengths[device], lengths[partner], jnp.int32(0), jnp.int32(1)])
    second_info = jnp.stack([lengths[survivor], lengths[rival], bit * half, won.astype(jnp.int32)])

    def group_part(array, g, size):
        return array[:, g * size : (g + 1) * size]

    companion_keys = from_partner(keys, "cand", 0)
    companion_values = [from_partner(group_part(values, g, HD), "cand", 0) for g in range(groups)]
    sent_rows = lax.dynamic_slice_in_dim(queries, (1 - bit) * half, half, 0)
    partner_queries = [from_partner(group_part(sent_rows, g, width), "cand", 0) for g in range(groups)]

    survivor_keys = jnp.where(won, keys, companion_keys)
    rival_keys = from_partner(survivor_keys, "cand", 1)
    survivor_values, rival_values = [], []
    for g in range(groups):
        survivor_values.append(jnp.where(won, group_part(values, g, HD), companion_values[g]))
        rival_values.append(from_partner(survivor_values[g], "cand", 1))

    first, first_part = None, 0.0
    for g in range(groups):
        first, part = attend(
            g, span, first_info, weight, queries, None, keys, values, companion_keys, companion_values[g], first
        )
        first_part += part[0, 0]
    second, second_part = None, 0.0
    for g in range(groups):
        second, part = attend(
            g, half, second_info, weight, queries, partner_queries[g],
            survivor_keys, survivor_values[g], rival_keys, rival_values[g], second,
        )
        second_part += part[0, 0]

    first_total, second_total = lax.psum((first_part.reshape(1), second_part.reshape(1)), "head")
    other_half = from_partner(second_total, "cand", 0)
    first_score = first_total / lengths[device].astype(jnp.float32)
    final_round_score = (second_total + other_half) / lengths[survivor].astype(jnp.float32)
    return first, second, first_score, final_round_score


def solution(mesh):
    in_specs = (
        P(("grp", "cand"), "head"),
        P(("grp", "cand"), "head"),
        P(("grp", "cand"), "head"),
        P("grp"),
        P("grp"),
        P("head"),
    )
    out_specs = (
        P(("grp", "cand"), "head"),
        P(("grp", "cand"), "head"),
        P(("grp", "cand")),
        P(("grp", "cand")),
    )
    return jax.shard_map(body, mesh=mesh, in_specs=in_specs, out_specs=out_specs, check_vma=False)
```

time: 85.8 us -> 76.9 us (0.90)
  matrix products: 36.7 us -> 0 us
  Pallas kernels: 0 us -> 27.1 us
  other arithmetic: 10.5 us -> 2.78 us
  local copies, waits for them, and re-layouts: 12 us -> 6.07 us
  waiting for transfers between devices: 7.57 us -> 13 us
  starting transfers between devices: 7.21 us -> 12.6 us
  between operations: 8.24 us -> 10.9 us
  blocking collectives: 3.11 us -> 4.12 us
    pallas_call x0 -> x4, Pallas kernels: none -> 27.1 us  [attend(): pl.pallas_call(functools.partial(attend_kernel, group, ratio, row_block,...]
    sub x4 -> x0, matrix products: 23.2 us -> none  [attend_spans(): exps = jnp.exp(scores - peak)]
    dot_general x4 -> x0, matrix products: 13.5 us -> none  [attend_spans(): jnp.einsum('rqk,kd->qrd', weights, values_g, preferred_element_type=jnp.f...]
    ppermute x6 -> x9, waiting for transfers between devices: 7.57 us -> 13 us  [from_partner(): lax.ppermute(value, axis, [(i, i ^ 1 << stride) for i in range(lax.axis_s...]
    ppermute x6 -> x9, starting transfers between devices: 7.21 us -> 12.6 us  [from_partner(): lax.ppermute(value, axis, [(i, i ^ 1 << stride) for i in range(lax.axis_s...]
    unnamed x30 -> x12, local copies, waits for them, and re-layouts: 4.66 us -> 0.03 us
    reduce_sum x2 -> x0, other arithmetic: 4.07 us -> none  [the longest x1 2.46 us: body(): jnp.sum(first.astype(jnp.float32) * score_weight[None, :]).reshape(1)]
    slice x2 -> x6, local copies, waits for them, and re-layouts: 1.45 us -> 4.83 us  [the longest x2 2.77 us: group_part(): return array[:, g * size:(g + 1) * size]]
  transfers between devices with their start and end apart: 6 -> 9, of which waited for: 2 -> 2; matrix products, arithmetic and copies ran while one was open for 53% -> 9% of each run, Pallas kernels for 0% -> 28%
where the time goes in v1:
time: 76.9 us; the launch traced here: 76.6 us
  Pallas kernels  27.1 us (35%)
  waiting for transfers between devices  13 us (17%)
  starting transfers between devices  12.6 us (16%)
  between operations  10.9 us (14%)
  local copies, waits for them, and re-layouts  6.07 us (8%)
  blocking collectives  4.12 us (5%)
  other arithmetic  2.78 us (4%)
    pallas_call x4, Pallas kernels, attend(): pl.pallas_call(functools.partial(attend_kernel, group, ratio, row_block,...  27.1 us
    ppermute x9, waiting for transfers between devices, from_partner(): lax.ppermute(value, axis, [(i, i ^ 1 << stride) for i in range(lax.axis_s...  13 us
    ppermute x9, starting transfers between devices, from_partner(): lax.ppermute(value, axis, [(i, i ^ 1 << stride) for i in range(lax.axis_s...  12.6 us
    psum x1, blocking collectives, body(): lax.psum((first_part.reshape(1), second_part.reshape(1)), 'head')  4.12 us
    slice x2, local copies, waits for them, and re-layouts, group_part(): return array[:, g * size:(g + 1) * size]  2.77 us
  transfers between devices with their start and end apart: 9, of which 2 were waited for; matrix products, arithmetic and copies ran while one was open for 9% of the time, Pallas kernels for 28%

profile of v1, /device:TPU:0, one launch (start us, length us, event | category | flops | bytes accessed | tf_op | source)
XLA Modules:
  0.0 76.6 jit_solution(8508205890506722369)
XLA Ops:
  0.7 1.6 %slice.27 = bf16[512,128]{1,0:T(8,128)(2,1)} slice(bf16[512,256]{1,0:T(8,128)(2,1)} %va_ref.3), slice={[0:512], [0:128]} | slice | bytes 262144 | tf_op jit(solution)/shard_map/slice | solution.py:168
  2.3 2.9 %collective-permute-start.2 = (bf16[512,128]{1,0:T(8,128)(2,1)}, bf16[512,128]{1,0:T(8,128)(2,1)S(1)}, u32[]{:S(2)}, u32[]{:S(2)}) collective-permute-start(bf16[512,128]{1,0:T(8,128)(2,1)} %slice.27), channel_id=1, source_target_pairs={{0,2},{2,0},{4,6},{6,4},{8,10},{10,8},{12,14},{14,12},{1,3},{3,1},... | collective-permute-start | bytes 393224 | tf_op jit(solution)/shard_map/ppermute | solution.py:20
  5.3 1.1 %constant_dynamic-slice_fusion = (bf16[256,640]{1,0:T(8,128)(2,1)S(1)}, bf16[256,640]{1,0:T(8,128)(2,1)S(1)}) fusion(bf16[512,1280]{1,0:T(8,128)(2,1)} %q_ref.7, s32[]{:T(128)S(6)} %select_n.62, s32[]{:T(128)S(6)} %add.68), kind=kLoop, calls=%fused_computation.5 | loop fusion | bytes 1310728 | tf_op jit(solution)/shard_map/slice | solution.py:168
  6.4 2.1 %collective-permute-start.6 = (bf16[256,640]{1,0:T(8,128)(2,1)S(1)}, bf16[256,640]{1,0:T(8,128)(2,1)S(1)}, u32[]{:S(2)}, u32[]{:S(2)}) collective-permute-start(bf16[256,640]{1,0:T(8,128)(2,1)S(1)} %get-tuple-element.22), channel_id=1, source_target_pairs={{0,2},{2,0},{4,6},{6,4},{8,10},{10,8},{12,14},{14,12},{1,3},{3,1},... | collective-permute-start | bytes 983048 | tf_op jit(solution)/shard_map/ppermute | solution.py:20
  8.6 0.6 fusion.1
  11.1 0.6 fusion
  11.8 1.3 %pad_add_fusion.1.info_ref = s32[4]{0:T(128)S(1)} fusion(s32[1]{0:T(128)} %bitcast.3, s32[1]{0:T(128)} %bitcast.2, s32[1]{0:T(128)} %get-tuple-element.29, s32[1]{0:T(128)} %get-tuple-element.26), kind=kLoop, calls=%fused_computation.4 | loop fusion | flops 12 | bytes 32 | tf_op jit(solution)/shard_map/stack | solution.py:165
  13.1 1.4 %pad_add_fusion.info_ref = s32[4]{0:T(128)S(1)} fusion(s32[1]{0:T(128)} %constant.39.clone.1, s32[1]{0:T(128)} %constant.38.clone.1, s32[1]{0:T(128)} %get-tuple-element.27, s32[1]{0:T(128)} %get-tuple-element.28), kind=kLoop, calls=%fused_computation.3 | loop fusion | flops 12 | bytes 32 | tf_op jit(solution)/shard_map/stack | solution.py:164
  15.8 2.0 %collective-permute-start.1 = (bf16[512,128]{1,0:T(8,128)(2,1)S(1)}, bf16[512,128]{1,0:T(8,128)(2,1)S(1)}, u32[]{:S(2)}, u32[]{:S(2)}) collective-permute-start(bf16[512,128]{1,0:T(8,128)(2,1)S(1)} %get-tuple-element.25), channel_id=1, source_target_pairs={{0,2},{2,0},{4,6},{6,4},{8,10},{10,8},{12,14},{14,12},{1,3},{3,1},... | collective-permute-start | bytes 393224 | tf_op jit(solution)/shard_map/ppermute | solution.py:20
  17.9 1.6 %collective-permute-start.7 = (bf16[512,128]{1,0:T(8,128)(2,1)S(1)}, bf16[512,128]{1,0:T(8,128)(2,1)S(1)}, u32[]{:S(2)}, u32[]{:S(2)}) collective-permute-start(bf16[512,128]{1,0:T(8,128)(2,1)S(1)} %get-tuple-element.24.va_ref), channel_id=1, source_target_pairs={{0,4},{2,6},{4,0},{6,2},{8,12},{10,14},{12,8},{14,10},{1,5},{3,7},... | collective-permute-start | bytes 393224 | tf_op jit(solution)/shard_map/ppermute | solution.py:20
  19.5 0.5 collective-permute-start.4
  20.0 11.4 %collective-permute-done.1.vb_ref = bf16[512,128]{1,0:T(8,128)(2,1)S(1)} collective-permute-done((bf16[512,128]{1,0:T(8,128)(2,1)S(1)}, bf16[512,128]{1,0:T(8,128)(2,1)S(1)}, u32[]{:S(2)}, u32[]{:S(2)}) %collective-permute-start.1) | collective-permute-done | bytes 131104 | tf_op jit(solution)/shard_map/ppermute | solution.py:20
  31.5 1.9 %collective-permute-start.5 = (bf16[512,128]{1,0:T(8,128)(2,1)S(1)}, bf16[512,128]{1,0:T(8,128)(2,1)S(1)}, u32[]{:S(2)}, u32[]{:S(2)}) collective-permute-start(bf16[512,128]{1,0:T(8,128)(2,1)S(1)} %broadcast_select_fusion.2.va_ref), channel_id=1, source_target_pairs={{0,4},{2,6},{4,0},{6,2},{8,12},{10,14},{12,8},{14,10},{1,5},{3,7},... | collective-permute-start | bytes 393224 | tf_op jit(solution)/shard_map/ppermute | solution.py:20
  33.4 7.5 %shard_map.93 = (bf16[512,1280]{1,0:T(8,128)(2,1)}, f32[8,128]{1,0:T(8,128)S(1)}) custom-call(s32[4]{0:T(128)S(1)} %pad_add_fusion.info_ref, f32[1,1280]{1,0:T(1,128)S(1)} %reshape.25.weight_ref, bf16[512,1280]{1,0:T(8,128)(2,1)S(1)} %copy-done, bf16[512,1280]{1,0:T(8,128)(2,1)S(1)} %copy-done, bf16[512,256]{1,0:T(8,128)(2,1)S(1)} %copy-done.2, ...), custom_call_target="tpu_custom_call" | custom-call | flops 1342177280 | bytes 1310720 | tf_op jit(solution)/shard_map/pallas_call | solution.py:127
  40.9 0.5 slice.30
  41.4 7.5 %shard_map.94 = (bf16[512,1280]{1,0:T(8,128)(2,1)}, f32[8,128]{1,0:T(8,128)S(1)}) custom-call(s32[4]{0:T(128)S(1)} %pad_add_fusion.info_ref, f32[1,1280]{1,0:T(1,128)S(1)} %reshape.25.weight_ref, bf16[512,1280]{1,0:T(8,128)(2,1)S(1)} %copy-done, bf16[512,1280]{1,0:T(8,128)(2,1)S(1)} %copy-done, ...), custom_call_target="tpu_custom_call", output_to_operand_aliasing={{0}: (8, {})} | custom-call | flops 1342177280 | bytes 1310720 | tf_op jit(solution)/shard_map/pallas_call | solution.py:127
  48.9 0.5 slice.31
  50.7 6.2 %shard_map.95 = (bf16[256,1280]{1,0:T(8,128)(2,1)}, f32[8,128]{1,0:T(8,128)S(1)}) custom-call(s32[4]{0:T(128)S(1)} %pad_add_fusion.1.info_ref, f32[1,1280]{1,0:T(1,128)S(1)} %reshape.25.weight_ref, bf16[512,1280]{1,0:T(8,128)(2,1)S(1)} %copy-done, bf16[256,640]{1,0:T(8,128)(2,1)S(1)} %collective-permute-done.6.other_q_ref, ...), custom_call_target="tpu_custom_call" | custom-call | flops 671088640 | bytes 655360 | tf_op jit(solution)/shard_map/pallas_call | solution.py:127
  56.9 0.5 slice.32
  57.4 6.0 %shard_map.96 = (bf16[256,1280]{1,0:T(8,128)(2,1)}, f32[8,128]{1,0:T(8,128)S(1)}) custom-call(s32[4]{0:T(128)S(1)} %pad_add_fusion.1.info_ref, f32[1,1280]{1,0:T(1,128)S(1)} %reshape.25.weight_ref, bf16[512,1280]{1,0:T(8,128)(2,1)S(1)} %copy-done, bf16[256,640]{1,0:T(8,128)(2,1)S(1)} %collective-permute-done.3.other_q_ref, ...), custom_call_target="tpu_custom_call", output_to_operand_aliasing={{0}: (8, {})} | custom-call | flops 671088640 | bytes 655360 | tf_op jit(solution)/shard_map/pallas_call | solution.py:127
  63.4 0.5 slice.33
  65.2 4.1 %all-reduce = (f32[1]{0:T(128)}, f32[1]{0:T(128)}) all-reduce(f32[1]{0:T(128)} %bitcast.4, f32[1]{0:T(128)} %bitcast.5), channel_id=1, replica_groups=mesh['grp'=2,'cand'=8,'head'=2] {'head'}, use_global_device_ids=true, to_apply=%region_0.1 | all-reduce | flops 2 | bytes 16 | tf_op jit(solution)/shard_map/psum | solution.py:196
  69.3 1.5 %collective-permute-start.8 = (f32[1]{0:T(128)}, f32[1]{0:T(128)}, u32[]{:S(2)}, u32[]{:S(2)}) collective-permute-start(f32[1]{0:T(128)} %get-tuple-element.21), channel_id=1, source_target_pairs={{0,2},{2,0},{4,6},{6,4},{8,10},{10,8},{12,14},{14,12},{1,3},{3,1},... | collective-permute-start | bytes 20 | tf_op jit(solution)/shard_map/ppermute | solution.py:20
  71.5 1.5 %collective-permute-done.8 = f32[1]{0:T(128)} collective-permute-done((f32[1]{0:T(128)}, f32[1]{0:T(128)}, u32[]{:S(2)}, u32[]{:S(2)}) %collective-permute-start.8) | collective-permute-done | bytes 36 | tf_op jit(solution)/shard_map/ppermute | solution.py:20
  (26 shorter events, 0.2 us)
Async XLA Ops:
  0.6 15.2 %copy-start.1 = (bf16[512,256]{1,0:T(8,128)(2,1)S(1)}, bf16[512,256]{1,0:T(8,128)(2,1)}, u32[]{:S(2)}) copy-start(bf16[512,256]{1,0:T(8,128)(2,1)} %va_ref.3) | copy-start | bytes 786436
  0.6 18.8 %copy-start.2 = (bf16[512,256]{1,0:T(8,128)(2,1)S(1)}, bf16[512,256]{1,0:T(8,128)(2,1)}, u32[]{:S(2)}) copy-start(bf16[512,256]{1,0:T(8,128)(2,1)} %ka_ref.3) | copy-start | bytes 786436
  0.7 7.9 %copy-start.5 = (s32[4]{0:T(128)S(1)}, s32[4]{0:T(128)}, u32[]{:S(2)}) copy-start(s32[4]{0:T(128)} %param.10) | copy-start | bytes 52
  0.7 10.5 %copy-start.3 = (s32[8]{0:T(128)S(1)}, s32[8]{0:T(128)}, u32[]{:S(2)}) copy-start(s32[8]{0:T(128)} %param.9) | copy-start | bytes 100
  0.7 15.1 %copy-start.4 = (f32[1280]{0:T(1024)S(1)}, f32[1280]{0:T(1024)}, u32[]{:S(2)}) copy-start(f32[1280]{0:T(1024)} %param.11) | copy-start | bytes 15364
  2.3 13.5 %collective-permute-start.2 = (bf16[512,128]{1,0:T(8,128)(2,1)}, bf16[512,128]{1,0:T(8,128)(2,1)S(1)}, u32[]{:S(2)}, u32[]{:S(2)}) collective-permute-start(bf16[512,128]{1,0:T(8,128)(2,1)} %slice.27), channel_id=1, source_target_pairs={{0,2},{2,0},{4,6},{6,4},{8,10},{10,8},{12,14},{14,12},{1,3},{3,1},... | collective-permute-start | bytes 393224 | tf_op jit(solution)/shard_map/ppermute | solution.py:20
  5.3 14.2 %collective-permute-start = (bf16[512,256]{1,0:T(8,128)(2,1)}, bf16[512,256]{1,0:T(8,128)(2,1)S(1)}, u32[]{:S(2)}, u32[]{:S(2)}) collective-permute-start(bf16[512,256]{1,0:T(8,128)(2,1)} %ka_ref.3), channel_id=1, source_target_pairs={{0,2},{2,0},{4,6},{6,4},{8,10},{10,8},{12,14},{14,12},{1,3},{3,1},... | collective-permute-start | bytes 786440 | tf_op jit(solution)/shard_map/ppermute | solution.py:20
  6.4 26.9 %copy-start = (bf16[512,1280]{1,0:T(8,128)(2,1)S(1)}, bf16[512,1280]{1,0:T(8,128)(2,1)}, u32[]{:S(2)}) copy-start(bf16[512,1280]{1,0:T(8,128)(2,1)} %q_ref.7) | copy-start | bytes 3932164
  6.4 44.2 %collective-permute-start.6 = (bf16[256,640]{1,0:T(8,128)(2,1)S(1)}, bf16[256,640]{1,0:T(8,128)(2,1)S(1)}, u32[]{:S(2)}, u32[]{:S(2)}) collective-permute-start(bf16[256,640]{1,0:T(8,128)(2,1)S(1)} %get-tuple-element.22), channel_id=1, source_target_pairs={{0,2},{2,0},{4,6},{6,4},{8,10},{10,8},{12,14},{14,12},{1,3},{3,1},... | collective-permute-start | bytes 983048 | tf_op jit(solution)/shard_map/ppermute | solution.py:20
  8.5 48.9 %collective-permute-start.3 = (bf16[256,640]{1,0:T(8,128)(2,1)S(1)}, bf16[256,640]{1,0:T(8,128)(2,1)S(1)}, u32[]{:S(2)}, u32[]{:S(2)}) collective-permute-start(bf16[256,640]{1,0:T(8,128)(2,1)S(1)} %get-tuple-element.23), channel_id=1, source_target_pairs={{0,2},{2,0},{4,6},{6,4},{8,10},{10,8},{12,14},{14,12},{1,3},{3,1},... | collective-permute-start | bytes 983048 | tf_op jit(solution)/shard_map/ppermute | solution.py:20
  15.8 15.6 %collective-permute-start.1 = (bf16[512,128]{1,0:T(8,128)(2,1)S(1)}, bf16[512,128]{1,0:T(8,128)(2,1)S(1)}, u32[]{:S(2)}, u32[]{:S(2)}) collective-permute-start(bf16[512,128]{1,0:T(8,128)(2,1)S(1)} %get-tuple-element.25), channel_id=1, source_target_pairs={{0,2},{2,0},{4,6},{6,4},{8,10},{10,8},{12,14},{14,12},{1,3},{3,1},... | collective-permute-start | bytes 393224 | tf_op jit(solution)/shard_map/ppermute | solution.py:20
  17.9 32.8 %collective-permute-start.7 = (bf16[512,128]{1,0:T(8,128)(2,1)S(1)}, bf16[512,128]{1,0:T(8,128)(2,1)S(1)}, u32[]{:S(2)}, u32[]{:S(2)}) collective-permute-start(bf16[512,128]{1,0:T(8,128)(2,1)S(1)} %get-tuple-element.24.va_ref), channel_id=1, source_target_pairs={{0,4},{2,6},{4,0},{6,2},{8,12},{10,14},{12,8},{14,10},{1,5},{3,7},... | collective-permute-start | bytes 393224 | tf_op jit(solution)/shard_map/ppermute | solution.py:20
  19.5 31.2 %collective-permute-start.4 = (bf16[512,256]{1,0:T(8,128)(2,1)S(1)}, bf16[512,256]{1,0:T(8,128)(2,1)S(1)}, u32[]{:S(2)}, u32[]{:S(2)}) collective-permute-start(bf16[512,256]{1,0:T(8,128)(2,1)S(1)} %broadcast_select_fusion.ka_ref), channel_id=1, source_target_pairs={{0,4},{2,6},{4,0},{6,2},{8,12},{10,14},{12,8},{14,10},{1,5},{3,7},... | collective-permute-start | bytes 786440 | tf_op jit(solution)/shard_map/ppermute | solution.py:20
  31.5 26.0 %collective-permute-start.5 = (bf16[512,128]{1,0:T(8,128)(2,1)S(1)}, bf16[512,128]{1,0:T(8,128)(2,1)S(1)}, u32[]{:S(2)}, u32[]{:S(2)}) collective-permute-start(bf16[512,128]{1,0:T(8,128)(2,1)S(1)} %broadcast_select_fusion.2.va_ref), channel_id=1, source_target_pairs={{0,4},{2,6},{4,0},{6,2},{8,12},{10,14},{12,8},{14,10},{1,5},{3,7},... | collective-permute-start | bytes 393224 | tf_op jit(solution)/shard_map/ppermute | solution.py:20
  69.3 3.7 %collective-permute-start.8 = (f32[1]{0:T(128)}, f32[1]{0:T(128)}, u32[]{:S(2)}, u32[]{:S(2)}) collective-permute-start(f32[1]{0:T(128)} %get-tuple-element.21), channel_id=1, source_target_pairs={{0,2},{2,0},{4,6},{6,4},{8,10},{10,8},{12,14},{14,12},{1,3},{3,1},... | collective-permute-start | bytes 20 | tf_op jit(solution)/shard_map/ppermute | solution.py:20

commit v2 on v0

v2 whole, which is shorter than its diff:
```python
import functools

import jax
import jax.numpy as jnp
from jax import lax
from jax.experimental import pallas as pl
from jax.experimental.pallas import tpu as pltpu
from jax.sharding import PartitionSpec as P

HD = 128
LANES = 128
LOG2E = 1.4426950408889634
FACTOR = HD ** (-0.5) * LOG2E
BARRED = -1e30
VMEM_LIMIT = 12 * 1024 * 1024
ANY = pl.BlockSpec(memory_space=pl.ANY)
VMEM = pl.BlockSpec(memory_space=pltpu.VMEM)
SMEM = pl.BlockSpec(memory_space=pltpu.SMEM)


def from_partner(value, axis, stride):
    return lax.ppermute(value, axis, [(i, i ^ 1 << stride) for i in range(lax.axis_size(axis))])


class Place:
    def __init__(self, lengths_ref, winners_ref):
        device = lax.axis_index("cand")
        self.bit = device & 1
        pair = device >> 1
        self.winner = winners_ref[pair]
        self.won = self.bit == self.winner
        rival_pair = pair ^ 1
        self.own_valid = lengths_ref[device]
        self.partner_valid = lengths_ref[device ^ 1]
        self.survivor_valid = lengths_ref[2 * pair + self.winner]
        self.rival_valid = lengths_ref[2 * rival_pair + winners_ref[rival_pair]]


def load_span(k_buf, v_buf, k_ref, v_ref, group, valid, start):
    span = k_ref.shape[0]
    k_columns = slice(group * HD, (group + 1) * HD)
    v_columns = k_columns if v_ref.shape[1] == k_ref.shape[1] else slice(0, HD)
    rows = slice(start, start + span)
    row = lax.broadcasted_iota(jnp.int32, (span, LANES), 0)
    first_lane = lax.broadcasted_iota(jnp.int32, (span, LANES), 1) == 0
    k_buf[rows, :HD] = k_ref[:, k_columns]
    k_buf[rows, HD:] = jnp.where(first_lane & (row >= valid), BARRED, 0.0).astype(k_buf.dtype)
    v_buf[rows, :HD] = v_ref[:, v_columns]
    v_buf[rows, HD:] = jnp.ones((span, LANES), v_buf.dtype)


def score_rows(q, k_buf):
    lane = lax.broadcasted_iota(jnp.int32, (q.shape[0], LANES), 1)
    one_lane = jnp.where(lane == 0, 1.0, 0.0).astype(q.dtype)
    wide_q = jnp.concatenate([q, one_lane], axis=1)
    return lax.dot_general(wide_q, k_buf[...], (((1,), (1,)), ((), ())), preferred_element_type=jnp.float32)


def weigh(scores, peak, v_buf):
    wide_peak = jnp.concatenate([peak] * (scores.shape[1] // LANES), axis=1)
    exps = jnp.exp2(scores * FACTOR - wide_peak).astype(v_buf.dtype)
    both = jnp.dot(exps, v_buf[...], preferred_element_type=jnp.float32)
    return both[:, :HD], both[:, HD:]


def peak_of(scores):
    peak = jnp.max(scores, axis=1, keepdims=True) * FACTOR
    return jnp.broadcast_to(peak, (scores.shape[0], LANES))


def finish(above, below, valid_rows, first_row, dtype):
    row = lax.broadcasted_iota(jnp.int32, above.shape, 0) + first_row
    return jnp.where(row < valid_rows, above / below, 0.0).astype(dtype)


def own_kernel(ratio, block, cuts, lengths_ref, q_ref, k_ref, v_ref, o_ref, mass_ref, *rest):
    piece_refs, (k_buf, v_buf) = rest[: len(cuts)], rest[len(cuts) :]
    device = lax.axis_index("cand")
    half = q_ref.shape[0] // 2
    sent = pl.ds(pl.multiple_of((1 - (device & 1)) * half, half), half)
    for piece_ref, (_, low, high) in zip(piece_refs, cuts):
        piece_ref[...] = q_ref[sent, low * HD : high * HD]
    for group in range(k_ref.shape[1] // HD):
        load_span(k_buf, v_buf, k_ref, v_ref, group, lengths_ref[device], 0)
        for head in range(group * ratio, (group + 1) * ratio):
            columns = slice(head * HD, (head + 1) * HD)
            for start in range(0, q_ref.shape[0], block):
                rows = slice(start, start + block)
                scores = score_rows(q_ref[rows, columns], k_buf)
                peak = peak_of(scores)
                above, below = weigh(scores, peak, v_buf)
                o_ref[rows, columns] = above / below
                mass_ref[rows, columns] = peak + jnp.log(below) * LOG2E


def choose_kernel(lengths_ref, winners_ref, own_ref, companion_ref, *out_refs):
    place = Place(lengths_ref, winners_ref)
    for won, ref in ((True, own_ref), (False, companion_ref)):
        @pl.when(place.won == won)
        def _():
            start = 0
            for out_ref in out_refs:
                out_ref[...] = ref[:, start : start + out_ref.shape[1]]
                start += out_ref.shape[1]


def join_head(columns, block, valid_rows, q_ref, o_ref, mass_ref, weight_ref, k_buf, v_buf, out_buf, out_columns):
    total = jnp.zeros((8, LANES), jnp.float32)
    for start in range(0, q_ref.shape[0], block):
        rows = slice(start, start + block)
        scores = score_rows(q_ref[rows, columns], k_buf)
        mass = mass_ref[rows, columns]
        peak = jnp.maximum(mass, peak_of(scores))
        above, below = weigh(scores, peak, v_buf)
        keep = jnp.exp2(mass - peak)
        output = finish(above + o_ref[rows, columns] * keep, below + keep, valid_rows, start, out_buf.dtype)
        out_buf[rows, out_columns] = output
        total += jnp.sum(output.astype(jnp.float32).reshape(block // 8, 8, LANES), axis=0)
    return total * weight_ref[:, columns]


def first_kernel(
    ratio, block, lengths_ref, weight_ref, q_ref, o_ref, mass_ref, k_ref, v_ref,
    out_ref, part_ref, k_buf, v_buf, out_buf, out_sems,
):
    device = lax.axis_index("cand")
    heads = q_ref.shape[1] // HD

    def out_copy(head):
        columns = pl.ds(head * HD, HD)
        return pltpu.make_async_copy(out_buf.at[:, columns], out_ref.at[:, columns], out_sems.at[head])

    total = jnp.zeros((8, LANES), jnp.float32)
    for group in range(heads // ratio):
        load_span(k_buf, v_buf, k_ref, v_ref, group, lengths_ref[device ^ 1], 0)
        for head in range(group * ratio, (group + 1) * ratio):
            columns = slice(head * HD, (head + 1) * HD)
            total += join_head(
                columns, block, lengths_ref[device], q_ref, o_ref, mass_ref, weight_ref, k_buf, v_buf, out_buf, columns
            )
            out_copy(head).start()
    part_ref[...] = jnp.full(part_ref.shape, jnp.sum(total), jnp.float32)
    for head in range(heads):
        out_copy(head).wait()


def winner_kernel(
    group, ratio, block, lengths_ref, winners_ref, weight_ref, q_ref, o_ref, mass_ref, k_ref, v_ref, before_ref, prior_ref,
    out_ref, part_ref, k_buf, v_buf, out_buf, out_sems,
):
    place = Place(lengths_ref, winners_ref)
    half = out_buf.shape[0] // 2
    kept = pl.ds(pl.multiple_of(place.bit * half, half), half)

    def out_copy(h):
        return pltpu.make_async_copy(
            out_buf.at[kept, pl.ds(h * HD, HD)], out_ref.at[:, pl.ds((group * ratio + h) * HD, HD)], out_sems.at[h]
        )

    @pl.when(place.won)
    def _():
        load_span(k_buf, v_buf, k_ref, v_ref, group, place.rival_valid, 0)
        total = jnp.zeros((8, LANES), jnp.float32)
        for h in range(ratio):
            columns = slice((group * ratio + h) * HD, (group * ratio + h + 1) * HD)
            total += join_head(
                columns, block, place.own_valid, q_ref, o_ref, mass_ref, weight_ref, k_buf, v_buf,
                out_buf, slice(h * HD, (h + 1) * HD),
            )
            out_copy(h).start()
        part = jnp.full(part_ref.shape, jnp.sum(total), jnp.float32)
        part_ref[...] = part + before_ref[...] if group else part
        for h in range(ratio):
            out_copy(h).wait()

    @pl.when(jnp.logical_not(place.won))
    def _():
        part_ref[...] = jnp.zeros(part_ref.shape, jnp.float32)


def loser_kernel(
    group, first_head, lengths_ref, winners_ref, q_ref, ka_ref, va_ref, kb_ref, vb_ref, prior_ref,
    out_ref, k_buf, v_buf, out_buf, out_sems,
):
    place = Place(lengths_ref, winners_ref)
    rows, span = q_ref.shape[0], ka_ref.shape[0]
    heads = q_ref.shape[1] // HD

    def out_copy(h):
        return pltpu.make_async_copy(
            out_buf.at[:, pl.ds(h * HD, HD)], out_ref.at[:, pl.ds((first_head + h) * HD, HD)], out_sems.at[h]
        )

    @pl.when(jnp.logical_not(place.won))
    def _():
        load_span(k_buf, v_buf, ka_ref, va_ref, group, place.partner_valid, 0)
        load_span(k_buf, v_buf, kb_ref, vb_ref, group, place.rival_valid, span)
        for h in range(heads):
            columns = slice(h * HD, (h + 1) * HD)
            scores = score_rows(q_ref[:, columns], k_buf)
            above, below = weigh(scores, peak_of(scores), v_buf)
            out_buf[:, columns] = finish(above, below, place.partner_valid, place.bit * rows, out_buf.dtype)
            out_copy(h).start()
        for h in range(heads):
            out_copy(h).wait()


def total_kernel(
    lengths_ref, winners_ref, first_ref, first_beside_ref, part_ref, beside_ref, across_ref, across_beside_ref,
    first_score_ref, final_score_ref,
):
    place = Place(lengths_ref, winners_ref)
    first = (first_ref[...] + first_beside_ref[...]) / place.own_valid.astype(jnp.float32)
    own = part_ref[...] + beside_ref[...]
    partner = across_ref[...] + across_beside_ref[...]
    final = jnp.where(place.won, own, partner) / place.survivor_valid.astype(jnp.float32)
    first_score_ref[0] = jnp.max(first)
    final_score_ref[0] = jnp.max(final)


def kernel_call(kernel, operands, in_specs, out_shape, out_specs, scratch=(), flops=0, aliases=None):
    return pl.pallas_call(
        kernel,
        out_shape=out_shape,
        in_specs=in_specs,
        out_specs=out_specs,
        scratch_shapes=scratch,
        input_output_aliases=aliases or {},
        compiler_params=pltpu.CompilerParams(vmem_limit_bytes=VMEM_LIMIT),
        cost_estimate=pl.CostEstimate(flops=flops, bytes_accessed=flops // 256, transcendentals=flops // 512),
    )(*operands)


def body(queries, keys, values, lengths, winners, score_weight):
    span, width = queries.shape
    half = span // 2
    heads = width // HD
    groups = keys.shape[1] // HD
    ratio = heads // groups
    block = min(span, 256)
    dtype = queries.dtype
    weight = score_weight.reshape(1, -1)
    share = 4 * span * span * HD
    part_shape = jax.ShapeDtypeStruct((8, LANES), jnp.float32)
    second_shape = jax.ShapeDtypeStruct((half, width), dtype)

    def buffers(spans):
        return [pltpu.VMEM((spans * span, HD + LANES), dtype)] * 2

    companion_keys = from_partner(keys, "cand", 0)
    companion_values = from_partner(values, "cand", 0)

    cuts = []
    for g in range(groups):
        middle = ratio if g < groups - 1 else (ratio + 1) // 2
        cuts.append((g, g * ratio, g * ratio + middle))
        if middle < ratio:
            cuts.append((g, g * ratio + middle, (g + 1) * ratio))
    piece_shapes = tuple(jax.ShapeDtypeStruct((half, (high - low) * HD), dtype) for _, low, high in cuts)
    partial = jax.ShapeDtypeStruct((span, width), jnp.float32)
    own_output, own_mass, *sent = kernel_call(
        functools.partial(own_kernel, ratio, block, cuts),
        (lengths, queries, keys, values),
        [SMEM, VMEM, VMEM, VMEM],
        (partial, partial) + piece_shapes,
        (VMEM,) * (2 + len(cuts)),
        buffers(1),
        share * heads,
    )
    pieces = [from_partner(piece, "cand", 0) for piece in sent]

    def choose(own, companion, parts):
        shape = jax.ShapeDtypeStruct((span, own.shape[1] // parts), dtype)
        return kernel_call(
            choose_kernel, (lengths, winners, own, companion), [SMEM, SMEM, VMEM, VMEM], (shape,) * parts, (VMEM,) * parts
        )

    rival_keys = from_partner(choose(keys, companion_keys, 1)[0], "cand", 1)
    rival_values = [from_partner(part, "cand", 1) for part in choose(values, companion_values, groups)]

    first, first_part = kernel_call(
        functools.partial(first_kernel, ratio, block),
        (lengths, weight, queries, own_output, own_mass, companion_keys, companion_values),
        [SMEM] + [VMEM] * 6,
        (jax.ShapeDtypeStruct((span, width), dtype), part_shape),
        (ANY, VMEM),
        buffers(1) + [pltpu.VMEM((span, width), dtype), pltpu.SemaphoreType.DMA((heads,))],
        share * heads,
    )

    def winner_part(g, part, second):
        return kernel_call(
            functools.partial(winner_kernel, g, ratio, block),
            (lengths, winners, weight, queries, own_output, own_mass, rival_keys, rival_values[g], part, second),
            [SMEM] * 2 + [VMEM] * 7 + [ANY],
            (second_shape, part_shape),
            (ANY, VMEM),
            buffers(1) + [pltpu.VMEM((span, ratio * HD), dtype), pltpu.SemaphoreType.DMA((ratio,))],
            share * ratio,
            {9: 0} if g else {},
        )

    def loser_part(index, second):
        g, low, high = cuts[index]
        return kernel_call(
            functools.partial(loser_kernel, g, low),
            (lengths, winners, pieces[index], companion_keys, companion_values, rival_keys, rival_values[g], second),
            [SMEM] * 2 + [VMEM] * 5 + [ANY],
            second_shape,
            ANY,
            buffers(2) + [pltpu.VMEM((half, (high - low) * HD), dtype), pltpu.SemaphoreType.DMA((high - low,))],
            share * (high - low),
            {7: 0},
        )

    part, second = first_part, first_part
    for g in range(groups):
        second, part = winner_part(g, part, second)
        if g < groups - 1:
            for index, cut in enumerate(cuts):
                second = loser_part(index, second) if cut[0] == g else second
    for index, cut in enumerate(cuts):
        second = loser_part(index, second) if cut[0] == groups - 1 else second

    cores = lax.axis_size("head")
    devices = lax.axis_size("cand") * cores
    diagonal = [(i, i ^ (cores + 1)) for i in range(devices)]
    score = jax.ShapeDtypeStruct((1,), jnp.float32)
    first_score, final_round_score = kernel_call(
        total_kernel,
        (
            lengths, winners, first_part, from_partner(first_part, "head", 0),
            part, from_partner(part, "head", 0), from_partner(part, "cand", 0), lax.ppermute(part, ("cand", "head"), diagonal),
        ),
        [SMEM] * 2 + [VMEM] * 6,
        (score, score),
        (SMEM, SMEM),
    )
    return first, second, first_score, final_round_score


def solution(mesh):
    in_specs = (
        P(("grp", "cand"), "head"),
        P(("grp", "cand"), "head"),
        P(("grp", "cand"), "head"),
        P("grp"),
        P("grp"),
        P("head"),
    )
    out_specs = (
        P(("grp", "cand"), "head"),
        P(("grp", "cand"), "head"),
        P(("grp", "cand")),
        P(("grp", "cand")),
    )
    return jax.shard_map(body, mesh=mesh, in_specs=in_specs, out_specs=out_specs, check_vma=False)
```

time: 85.8 us -> 44.6 us (0.52)
  matrix products: 36.7 us -> 0 us
  Pallas kernels: 0 us -> 22.6 us
  other arithmetic: 10.5 us -> 0 us
  starting transfers between devices: 7.21 us -> 16.5 us
  local copies, waits for them, and re-layouts: 12 us -> 3.89 us
  between operations: 8.24 us -> 0.96 us
  waiting for transfers between devices: 7.57 us -> 0.47 us
  blocking collectives: 3.11 us -> 0 us
    sub x4 -> x0, matrix products: 23.2 us -> none  [attend_spans(): exps = jnp.exp(scores - peak)]
    pallas_call x0 -> x10, Pallas kernels: none -> 22.6 us  [kernel_call(): pl.pallas_call(kernel, out_shape=out_shape, in_specs=in_specs, out_specs=...]
    dot_general x4 -> x0, matrix products: 13.5 us -> none  [attend_spans(): jnp.einsum('rqk,kd->qrd', weights, values_g, preferred_element_type=jnp.f...]
    ppermute x6 -> x11, starting transfers between devices: 7.21 us -> 16.5 us  [from_partner(): lax.ppermute(value, axis, [(i, i ^ 1 << stride) for i in range(lax.axis_s...]
    ppermute x6 -> x11, waiting for transfers between devices: 7.57 us -> 0.47 us  [from_partner(): lax.ppermute(value, axis, [(i, i ^ 1 << stride) for i in range(lax.axis_s...]
    reduce_sum x2 -> x0, other arithmetic: 4.07 us -> none  [the longest x1 2.46 us: body(): jnp.sum(first.astype(jnp.float32) * score_weight[None, :]).reshape(1)]
    dynamic_slice x3 -> x0, local copies, waits for them, and re-layouts: 3.35 us -> none  [the longest x1 1.43 us: body(): lax.dynamic_slice_in_dim(queries, (1 - device_bit) * half_rows, half_rows...]
    psum x1 -> x0, blocking collectives: 3.11 us -> none  [body(): first_total, latter_half = lax.psum((first_part, second_part), 'head')]
  transfers between devices with their start and end apart: 6 -> 12, of which waited for: 2 -> 1; matrix products, arithmetic and copies ran while one was open for 53% -> 0% of each run, Pallas kernels for 0% -> 48%
where the time goes in v2:
time: 44.6 us; the launch traced here: 44.4 us
  Pallas kernels  22.6 us (51%)
  starting transfers between devices  16.5 us (37%)
  local copies, waits for them, and re-layouts  3.89 us (9%)
  between operations  0.96 us (2%)
  waiting for transfers between devices  0.47 us (1%)
    pallas_call x10, Pallas kernels, kernel_call(): pl.pallas_call(kernel, out_shape=out_shape, in_specs=in_specs, out_specs=...  22.6 us
    ppermute x11, starting transfers between devices, from_partner(): lax.ppermute(value, axis, [(i, i ^ 1 << stride) for i in range(lax.axis_s...  16.5 us
    unnamed x18, local copies, waits for them, and re-layouts  3.89 us
  transfers between devices with their start and end apart: 12, of which 1 were waited for; matrix products, arithmetic and copies ran while one was open for 0% of the time, Pallas kernels for 48%

profile of v2, /device:TPU:0, one launch (start us, length us, event | category | flops | bytes accessed | tf_op | source)
XLA Modules:
  0.0 44.4 jit_solution(82607147425006896)
XLA Ops:
  0.6 3.0 %collective-permute-start = (bf16[512,256]{1,0:T(8,128)(2,1)}, bf16[512,256]{1,0:T(8,128)(2,1)S(1)}, u32[]{:S(2)}, u32[]{:S(2)}) collective-permute-start(bf16[512,256]{1,0:T(8,128)(2,1)} %own_ref.2), channel_id=1, source_target_pairs={{0,2},{2,0},{4,6},{6,4},{8,10},{10,8},{12,14},{14,12},{1,3},{3,1},... | collective-permute-start | bytes 786440 | tf_op jit(solution)/shard_map/ppermute | solution.py:22
  3.7 1.3 %copy-done = bf16[512,1280]{1,0:T(8,128)(2,1)S(1)} copy-done((bf16[512,1280]{1,0:T(8,128)(2,1)S(1)}, bf16[512,1280]{1,0:T(8,128)(2,1)}, u32[]{:S(2)}) %copy-start) | copy-done | bytes 1310744
  5.0 0.9 %copy-done.2 = bf16[512,256]{1,0:T(8,128)(2,1)S(1)} copy-done((bf16[512,256]{1,0:T(8,128)(2,1)S(1)}, bf16[512,256]{1,0:T(8,128)(2,1)}, u32[]{:S(2)}) %copy-start.2) | copy-done | bytes 262168
  6.0 0.9 %copy-done.4 = bf16[512,256]{1,0:T(8,128)(2,1)S(1)} copy-done((bf16[512,256]{1,0:T(8,128)(2,1)S(1)}, bf16[512,256]{1,0:T(8,128)(2,1)}, u32[]{:S(2)}) %copy-start.4) | copy-done | bytes 262168
  6.9 0.7 %copy-done.6 = s32[8]{0:T(128)S(1)} copy-done((s32[8]{0:T(128)S(1)}, s32[8]{0:T(128)}, u32[]{:S(2)}) %copy-start.6) | copy-done | bytes 56
  7.6 4.3 %shard_map.93 = (f32[512,1280]{1,0:T(8,128)S(1)}, f32[512,1280]{1,0:T(8,128)S(1)}, bf16[256,640]{1,0:T(8,128)(2,1)S(1)}, bf16[256,384]{1,0:T(8,128)(2,1)S(1)}, bf16[256,256]{1,0:T(8,128)(2,1)S(1)}) custom-call(s32[8]{0:T(128)S(1)} %copy-done.6, bf16[512,1280]{1,0:T(8,128)(2,1)S(1)} %copy-done, bf16[512,256]{1,0:T(8,128)(2,1)S(1)} %copy-done.2, ...), custom_call_target="tpu_custom_call" | custom-call | flops 1342177280 | bytes 5242880 | tf_op jit(solution)/shard_map/pallas_call | solution.py:222
  11.9 2.0 %collective-permute-start.7 = (bf16[256,640]{1,0:T(8,128)(2,1)S(1)}, bf16[256,640]{1,0:T(8,128)(2,1)S(1)}, u32[]{:S(2)}, u32[]{:S(2)}) collective-permute-start(bf16[256,640]{1,0:T(8,128)(2,1)S(1)} %get-tuple-element.28), channel_id=1, source_target_pairs={{0,2},{2,0},{4,6},{6,4},{8,10},{10,8},{12,14},{14,12},{1,3},{3,1},... | collective-permute-start | bytes 983048 | tf_op jit(solution)/shard_map/ppermute | solution.py:22
  13.9 0.6 %shard_map.95 = bf16[512,256]{1,0:T(8,128)(2,1)S(1)} custom-call(s32[8]{0:T(128)S(1)} %copy-done.6, s32[4]{0:T(128)S(1)} %copy-done.7, bf16[512,256]{1,0:T(8,128)(2,1)S(1)} %copy-done.3, bf16[512,256]{1,0:T(8,128)(2,1)S(1)} %collective-permute-done.k_ref.companion_ref.ka_ref), custom_call_target="tpu_custom_call" | custom-call | tf_op jit(solution)/shard_map/pallas_call | solution.py:222
  14.5 1.6 %collective-permute-start.3 = (bf16[512,256]{1,0:T(8,128)(2,1)S(1)}, bf16[512,256]{1,0:T(8,128)(2,1)S(1)}, u32[]{:S(2)}, u32[]{:S(2)}) collective-permute-start(bf16[512,256]{1,0:T(8,128)(2,1)S(1)} %shard_map.95), channel_id=1, source_target_pairs={{0,4},{2,6},{4,0},{6,2},{8,12},{10,14},{12,8},{14,10},{1,5},{3,7},... | collective-permute-start | bytes 786440 | tf_op jit(solution)/shard_map/ppermute | solution.py:22
  16.2 0.4 collective-permute-done.1.v_ref.companion_ref.va_ref
  16.6 0.6 %shard_map.96 = (bf16[512,128]{1,0:T(8,128)(2,1)S(1)}, bf16[512,128]{1,0:T(8,128)(2,1)S(1)}) custom-call(s32[8]{0:T(128)S(1)} %copy-done.6, s32[4]{0:T(128)S(1)} %copy-done.7, bf16[512,256]{1,0:T(8,128)(2,1)S(1)} %copy-done.5, bf16[512,256]{1,0:T(8,128)(2,1)S(1)} %collective-permute-done.1.v_ref.companion_ref.va_ref), custom_call_target="tpu_custom_call" | custom-call | tf_op jit(solution)/shard_map/pallas_call | solution.py:222
  17.2 2.2 %collective-permute-start.6 = (bf16[512,128]{1,0:T(8,128)(2,1)S(1)}, bf16[512,128]{1,0:T(8,128)(2,1)S(1)}, u32[]{:S(2)}, u32[]{:S(2)}) collective-permute-start(bf16[512,128]{1,0:T(8,128)(2,1)S(1)} %get-tuple-element.25), channel_id=1, source_target_pairs={{0,4},{2,6},{4,0},{6,2},{8,12},{10,14},{12,8},{14,10},{1,5},{3,7},... | collective-permute-start | bytes 393224 | tf_op jit(solution)/shard_map/ppermute | solution.py:22
  19.4 1.5 %collective-permute-start.5 = (bf16[256,384]{1,0:T(8,128)(2,1)S(1)}, bf16[256,384]{1,0:T(8,128)(2,1)S(1)}, u32[]{:S(2)}, u32[]{:S(2)}) collective-permute-start(bf16[256,384]{1,0:T(8,128)(2,1)S(1)} %get-tuple-element.24), channel_id=1, source_target_pairs={{0,2},{2,0},{4,6},{6,4},{8,10},{10,8},{12,14},{14,12},{1,3},{3,1},... | collective-permute-start | bytes 589832 | tf_op jit(solution)/shard_map/ppermute | solution.py:22
  20.9 0.4 %collective-permute-start.4 = (bf16[512,128]{1,0:T(8,128)(2,1)S(1)}, bf16[512,128]{1,0:T(8,128)(2,1)S(1)}, u32[]{:S(2)}, u32[]{:S(2)}) collective-permute-start(bf16[512,128]{1,0:T(8,128)(2,1)S(1)} %get-tuple-element.23), channel_id=1, source_target_pairs={{0,4},{2,6},{4,0},{6,2},{8,12},{10,14},{12,8},{14,10},{1,5},{3,7},... | collective-permute-start | bytes 393224 | tf_op jit(solution)/shard_map/ppermute | solution.py:22
  21.4 5.6 %shard_map.94 = (bf16[512,1280]{1,0:T(8,128)(2,1)}, f32[8,128]{1,0:T(8,128)S(1)}) custom-call(s32[8]{0:T(128)S(1)} %copy-done.6, f32[1,1280]{1,0:T(1,128)S(1)} %reshape.11.weight_ref, bf16[512,1280]{1,0:T(8,128)(2,1)S(1)} %copy-done.1, f32[512,1280]{1,0:T(8,128)S(1)} %get-tuple-element.19.o_ref, f32[512,1280]{1,0:T(8,128)S(1)} %get-tuple-element.20.mass_ref, ...), custom_call_target="tpu_custom_call" | custom-call | flops 1342177280 | bytes 5242880 | tf_op jit(solution)/shard_map/pallas_call | solution.py:222
  27.0 0.2 collective-permute-start.2
  27.3 0.6 %shard_map.97 = (bf16[256,1280]{1,0:T(8,128)(2,1)}, f32[8,128]{1,0:T(8,128)S(1)}) custom-call(s32[8]{0:T(128)S(1)} %copy-done.6, s32[4]{0:T(128)S(1)} %copy-done.7, f32[1,1280]{1,0:T(1,128)S(1)} %reshape.11.weight_ref, bf16[512,1280]{1,0:T(8,128)(2,1)S(1)} %copy-done.1, f32[512,1280]{1,0:T(8,128)S(1)} %get-tuple-element.19.o_ref, ...), custom_call_target="tpu_custom_call" | custom-call | flops 671088640 | bytes 2621440 | tf_op jit(solution)/shard_map/pallas_call | solution.py:222
  27.9 3.8 %shard_map.98.prior_ref = bf16[256,1280]{1,0:T(8,128)(2,1)} custom-call(s32[8]{0:T(128)S(1)} %copy-done.6, s32[4]{0:T(128)S(1)} %copy-done.7, bf16[256,640]{1,0:T(8,128)(2,1)S(1)} %collective-permute-done.7.q_ref, bf16[512,256]{1,0:T(8,128)(2,1)S(1)} %collective-permute-done.k_ref.companion_ref.ka_ref, ...), custom_call_target="tpu_custom_call", output_to_operand_aliasing={{}: (7, {})} | custom-call | flops 671088640 | bytes 2621440 | tf_op jit(solution)/shard_map/pallas_call | solution.py:222
  31.7 0.6 %shard_map.99 = (bf16[256,1280]{1,0:T(8,128)(2,1)}, f32[8,128]{1,0:T(8,128)S(1)}) custom-call(s32[8]{0:T(128)S(1)} %copy-done.6, s32[4]{0:T(128)S(1)} %copy-done.7, f32[1,1280]{1,0:T(1,128)S(1)} %reshape.11.weight_ref, bf16[512,1280]{1,0:T(8,128)(2,1)S(1)} %copy-done.1, f32[512,1280]{1,0:T(8,128)S(1)} %get-tuple-element.19.o_ref, ...), custom_call_target="tpu_custom_call", output_to_operand_aliasing={{0}: (9, {})} | custom-call | flops 671088640 | bytes 2621440 | tf_op jit(solution)/shard_map/pallas_call | solution.py:222
  32.3 0.6 %collective-permute-start.9 = (f32[8,128]{1,0:T(8,128)S(1)}, f32[8,128]{1,0:T(8,128)S(1)}, u32[]{:S(2)}, u32[]{:S(2)}) collective-permute-start(f32[8,128]{1,0:T(8,128)S(1)} %get-tuple-element.31.part_ref), channel_id=1, source_target_pairs={{0,1},{1,0},{2,3},{3,2},{4,5},{5,4},{6,7},{7,6},{8,9},{9,8},{10,11... | collective-permute-start | bytes 12296 | tf_op jit(solution)/shard_map/ppermute | solution.py:22
  32.9 4.8 %collective-permute-start.10 = (f32[8,128]{1,0:T(8,128)S(1)}, f32[8,128]{1,0:T(8,128)S(1)}, u32[]{:S(2)}, u32[]{:S(2)}) collective-permute-start(f32[8,128]{1,0:T(8,128)S(1)} %get-tuple-element.31.part_ref), channel_id=1, source_target_pairs={{0,2},{2,0},{4,6},{6,4},{8,10},{10,8},{12,14},{14,12},{1,3},{3,1},... | collective-permute-start | bytes 12296 | tf_op jit(solution)/shard_map/ppermute | solution.py:22
  37.6 2.8 %shard_map.100.prior_ref = bf16[256,1280]{1,0:T(8,128)(2,1)} custom-call(s32[8]{0:T(128)S(1)} %copy-done.6, s32[4]{0:T(128)S(1)} %copy-done.7, bf16[256,384]{1,0:T(8,128)(2,1)S(1)} %collective-permute-done.5.q_ref, bf16[512,256]{1,0:T(8,128)(2,1)S(1)} %collective-permute-done.k_ref.companion_ref.ka_ref, ...), custom_call_target="tpu_custom_call", output_to_operand_aliasing={{}: (7, {})} | custom-call | flops 402653184 | bytes 1572864 | tf_op jit(solution)/shard_map/pallas_call | solution.py:222
  40.5 2.5 %shard_map.101 = bf16[256,1280]{1,0:T(8,128)(2,1)} custom-call(s32[8]{0:T(128)S(1)} %copy-done.6, s32[4]{0:T(128)S(1)} %copy-done.7, bf16[256,256]{1,0:T(8,128)(2,1)S(1)} %collective-permute-done.2.q_ref, bf16[512,256]{1,0:T(8,128)(2,1)S(1)} %collective-permute-done.k_ref.companion_ref.ka_ref, ...), custom_call_target="tpu_custom_call", output_to_operand_aliasing={{}: (7, {})} | custom-call | flops 268435456 | bytes 1048576 | tf_op jit(solution)/shard_map/pallas_call | solution.py:222
  43.0 1.2 %shard_map.102 = (f32[1]{0:T(128)}, f32[1]{0:T(128)}) custom-call(s32[8]{0:T(128)S(1)} %copy-done.6, s32[4]{0:T(128)S(1)} %copy-done.7, f32[8,128]{1,0:T(8,128)S(1)} %get-tuple-element.26.before_ref.prior_ref.first_ref, f32[8,128]{1,0:T(8,128)S(1)} %collective-permute-done.8.first_beside_ref, f32[8,128]{1,0:T(8,128)S(1)} %get-tuple-element.31.part_ref, ...), custom_call_target="tpu_custom_call" | custom-call | tf_op jit(solution)/shard_map/pallas_call | solution.py:222
  (29 shorter events, 0.1 us)
Async XLA Ops:
  0.6 13.3 %collective-permute-start = (bf16[512,256]{1,0:T(8,128)(2,1)}, bf16[512,256]{1,0:T(8,128)(2,1)S(1)}, u32[]{:S(2)}, u32[]{:S(2)}) collective-permute-start(bf16[512,256]{1,0:T(8,128)(2,1)} %own_ref.2), channel_id=1, source_target_pairs={{0,2},{2,0},{4,6},{6,4},{8,10},{10,8},{12,14},{14,12},{1,3},{3,1},... | collective-permute-start | bytes 786440 | tf_op jit(solution)/shard_map/ppermute | solution.py:22
  3.6 13.0 %collective-permute-start.1 = (bf16[512,256]{1,0:T(8,128)(2,1)}, bf16[512,256]{1,0:T(8,128)(2,1)S(1)}, u32[]{:S(2)}, u32[]{:S(2)}) collective-permute-start(bf16[512,256]{1,0:T(8,128)(2,1)} %own_ref.3), channel_id=1, source_target_pairs={{0,2},{2,0},{4,6},{6,4},{8,10},{10,8},{12,14},{14,12},{1,3},{3,1},... | collective-permute-start | bytes 786440 | tf_op jit(solution)/shard_map/ppermute | solution.py:22
  3.7 1.3 %copy-start = (bf16[512,1280]{1,0:T(8,128)(2,1)S(1)}, bf16[512,1280]{1,0:T(8,128)(2,1)}, u32[]{:S(2)}) copy-start(bf16[512,1280]{1,0:T(8,128)(2,1)} %q_ref.7) | copy-start | bytes 3932164
  5.0 0.9 %copy-start.2 = (bf16[512,256]{1,0:T(8,128)(2,1)S(1)}, bf16[512,256]{1,0:T(8,128)(2,1)}, u32[]{:S(2)}) copy-start(bf16[512,256]{1,0:T(8,128)(2,1)} %own_ref.2) | copy-start | bytes 786436
  6.0 0.9 %copy-start.4 = (bf16[512,256]{1,0:T(8,128)(2,1)S(1)}, bf16[512,256]{1,0:T(8,128)(2,1)}, u32[]{:S(2)}) copy-start(bf16[512,256]{1,0:T(8,128)(2,1)} %own_ref.3) | copy-start | bytes 786436
  6.9 0.7 %copy-start.6 = (s32[8]{0:T(128)S(1)}, s32[8]{0:T(128)}, u32[]{:S(2)}) copy-start(s32[8]{0:T(128)} %lengths_ref.19) | copy-start | bytes 100
  7.6 6.3 %copy-start.3 = (bf16[512,256]{1,0:T(8,128)(2,1)S(1)}, bf16[512,256]{1,0:T(8,128)(2,1)}, u32[]{:S(2)}) copy-start(bf16[512,256]{1,0:T(8,128)(2,1)} %own_ref.2) | copy-start | bytes 786436
  7.6 6.3 %copy-start.7 = (s32[4]{0:T(128)S(1)}, s32[4]{0:T(128)}, u32[]{:S(2)}) copy-start(s32[4]{0:T(128)} %winners_ref.15) | copy-start | bytes 52
  7.6 9.0 %copy-start.5 = (bf16[512,256]{1,0:T(8,128)(2,1)S(1)}, bf16[512,256]{1,0:T(8,128)(2,1)}, u32[]{:S(2)}) copy-start(bf16[512,256]{1,0:T(8,128)(2,1)} %own_ref.3) | copy-start | bytes 786436
  7.6 13.3 %copy-start.8 = (f32[1280]{0:T(1024)S(1)}, f32[1280]{0:T(1024)}, u32[]{:S(2)}) copy-start(f32[1280]{0:T(1024)} %param.11) | copy-start | bytes 15364
  7.6 13.8 %copy-start.1 = (bf16[512,1280]{1,0:T(8,128)(2,1)S(1)}, bf16[512,1280]{1,0:T(8,128)(2,1)}, u32[]{:S(2)}) copy-start(bf16[512,1280]{1,0:T(8,128)(2,1)} %q_ref.7) | copy-start | bytes 3932164
  11.9 16.0 %collective-permute-start.7 = (bf16[256,640]{1,0:T(8,128)(2,1)S(1)}, bf16[256,640]{1,0:T(8,128)(2,1)S(1)}, u32[]{:S(2)}, u32[]{:S(2)}) collective-permute-start(bf16[256,640]{1,0:T(8,128)(2,1)S(1)} %get-tuple-element.28), channel_id=1, source_target_pairs={{0,2},{2,0},{4,6},{6,4},{8,10},{10,8},{12,14},{14,12},{1,3},{3,1},... | collective-permute-start | bytes 983048 | tf_op jit(solution)/shard_map/ppermute | solution.py:22
  14.5 12.7 %collective-permute-start.3 = (bf16[512,256]{1,0:T(8,128)(2,1)S(1)}, bf16[512,256]{1,0:T(8,128)(2,1)S(1)}, u32[]{:S(2)}, u32[]{:S(2)}) collective-permute-start(bf16[512,256]{1,0:T(8,128)(2,1)S(1)} %shard_map.95), channel_id=1, source_target_pairs={{0,4},{2,6},{4,0},{6,2},{8,12},{10,14},{12,8},{14,10},{1,5},{3,7},... | collective-permute-start | bytes 786440 | tf_op jit(solution)/shard_map/ppermute | solution.py:22
  17.2 9.8 %collective-permute-start.6 = (bf16[512,128]{1,0:T(8,128)(2,1)S(1)}, bf16[512,128]{1,0:T(8,128)(2,1)S(1)}, u32[]{:S(2)}, u32[]{:S(2)}) collective-permute-start(bf16[512,128]{1,0:T(8,128)(2,1)S(1)} %get-tuple-element.25), channel_id=1, source_target_pairs={{0,4},{2,6},{4,0},{6,2},{8,12},{10,14},{12,8},{14,10},{1,5},{3,7},... | collective-permute-start | bytes 393224 | tf_op jit(solution)/shard_map/ppermute | solution.py:22
  19.4 18.2 %collective-permute-start.5 = (bf16[256,384]{1,0:T(8,128)(2,1)S(1)}, bf16[256,384]{1,0:T(8,128)(2,1)S(1)}, u32[]{:S(2)}, u32[]{:S(2)}) collective-permute-start(bf16[256,384]{1,0:T(8,128)(2,1)S(1)} %get-tuple-element.24), channel_id=1, source_target_pairs={{0,2},{2,0},{4,6},{6,4},{8,10},{10,8},{12,14},{14,12},{1,3},{3,1},... | collective-permute-start | bytes 589832 | tf_op jit(solution)/shard_map/ppermute | solution.py:22
  20.9 10.7 %collective-permute-start.4 = (bf16[512,128]{1,0:T(8,128)(2,1)S(1)}, bf16[512,128]{1,0:T(8,128)(2,1)S(1)}, u32[]{:S(2)}, u32[]{:S(2)}) collective-permute-start(bf16[512,128]{1,0:T(8,128)(2,1)S(1)} %get-tuple-element.23), channel_id=1, source_target_pairs={{0,4},{2,6},{4,0},{6,2},{8,12},{10,14},{12,8},{14,10},{1,5},{3,7},... | collective-permute-start | bytes 393224 | tf_op jit(solution)/shard_map/ppermute | solution.py:22
  27.0 13.5 %collective-permute-start.2 = (bf16[256,256]{1,0:T(8,128)(2,1)S(1)}, bf16[256,256]{1,0:T(8,128)(2,1)S(1)}, u32[]{:S(2)}, u32[]{:S(2)}) collective-permute-start(bf16[256,256]{1,0:T(8,128)(2,1)S(1)} %get-tuple-element.22), channel_id=1, source_target_pairs={{0,2},{2,0},{4,6},{6,4},{8,10},{10,8},{12,14},{14,12},{1,3},{3,1},... | collective-permute-start | bytes 393224 | tf_op jit(solution)/shard_map/ppermute | solution.py:22
  27.3 15.7 %collective-permute-start.8 = (f32[8,128]{1,0:T(8,128)S(1)}, f32[8,128]{1,0:T(8,128)S(1)}, u32[]{:S(2)}, u32[]{:S(2)}) collective-permute-start(f32[8,128]{1,0:T(8,128)S(1)} %get-tuple-element.26.before_ref.prior_ref.first_ref), channel_id=1, source_target_pairs={{0,1},{1,0},{2,3},{3,2},{4,5},{5,4},{6,7},{7,6},{8,9},{9,8},{10,11... | collective-permute-start | bytes 12296 | tf_op jit(solution)/shard_map/ppermute | solution.py:22
  32.3 10.7 %collective-permute-start.9 = (f32[8,128]{1,0:T(8,128)S(1)}, f32[8,128]{1,0:T(8,128)S(1)}, u32[]{:S(2)}, u32[]{:S(2)}) collective-permute-start(f32[8,128]{1,0:T(8,128)S(1)} %get-tuple-element.31.part_ref), channel_id=1, source_target_pairs={{0,1},{1,0},{2,3},{3,2},{4,5},{5,4},{6,7},{7,6},{8,9},{9,8},{10,11... | collective-permute-start | bytes 12296 | tf_op jit(solution)/shard_map/ppermute | solution.py:22
  32.9 10.1 %collective-permute-start.10 = (f32[8,128]{1,0:T(8,128)S(1)}, f32[8,128]{1,0:T(8,128)S(1)}, u32[]{:S(2)}, u32[]{:S(2)}) collective-permute-start(f32[8,128]{1,0:T(8,128)S(1)} %get-tuple-element.31.part_ref), channel_id=1, source_target_pairs={{0,2},{2,0},{4,6},{6,4},{8,10},{10,8},{12,14},{14,12},{1,3},{3,1},... | collective-permute-start | bytes 12296 | tf_op jit(solution)/shard_map/ppermute | solution.py:22
  37.6 5.4 %collective-permute-start.11 = (f32[8,128]{1,0:T(8,128)S(1)}, f32[8,128]{1,0:T(8,128)S(1)}, u32[]{:S(2)}, u32[]{:S(2)}) collective-permute-start(f32[8,128]{1,0:T(8,128)S(1)} %get-tuple-element.31.part_ref), channel_id=1, source_target_pairs={{0,3},{1,2},{2,1},{3,0},{4,7},{5,6},{6,5},{7,4},{8,11},{9,10},{10,... | collective-permute-start | bytes 12296 | tf_op jit(solution)/shard_map/ppermute | solution.py:333

commit v3 on v2

v3 whole, which is shorter than its diff:
```python
import functools

import jax
import jax.numpy as jnp
from jax import lax
from jax.experimental import pallas as pl
from jax.experimental.pallas import tpu as pltpu
from jax.sharding import PartitionSpec as P

HD = 128
LANES = 128
LOG2E = 1.4426950408889634
FACTOR = HD ** (-0.5) * LOG2E
BARRED = -1e30
LAST_HEADS = 4
COST = 10
VMEM_LIMIT = 12 * 1024 * 1024
ANY = pl.BlockSpec(memory_space=pl.ANY)
HBM = pl.BlockSpec(memory_space=pltpu.HBM)
VMEM = pl.BlockSpec(memory_space=pltpu.VMEM)
SMEM = pl.BlockSpec(memory_space=pltpu.SMEM)


def from_partner(value, axis, stride):
    return lax.ppermute(value, axis, [(i, i ^ 1 << stride) for i in range(lax.axis_size(axis))])


class Place:
    def __init__(self, lengths_ref, winners_ref):
        device = lax.axis_index("cand")
        self.bit = device & 1
        pair = device >> 1
        self.winner = winners_ref[pair]
        self.won = self.bit == self.winner
        rival_pair = pair ^ 1
        self.own_valid = lengths_ref[device]
        self.partner_valid = lengths_ref[device ^ 1]
        self.rival_valid = lengths_ref[2 * rival_pair + winners_ref[rival_pair]]


def load_span(k_buf, v_buf, k_ref, v_ref, group, valid, start):
    span = k_ref.shape[0]
    k_columns = slice(group * HD, (group + 1) * HD)
    v_columns = k_columns if v_ref.shape[1] == k_ref.shape[1] else slice(0, HD)
    rows = slice(start, start + span)
    row = lax.broadcasted_iota(jnp.int32, (span, LANES), 0)
    first_lane = lax.broadcasted_iota(jnp.int32, (span, LANES), 1) == 0
    k_buf[rows, :HD] = k_ref[:, k_columns]
    k_buf[rows, HD:] = jnp.where(first_lane & (row >= valid), BARRED, 0.0).astype(k_buf.dtype)
    v_buf[rows, :HD] = v_ref[:, v_columns]
    v_buf[rows, HD:] = jnp.ones((span, LANES), v_buf.dtype)


def score_rows(q, k_buf):
    lane = lax.broadcasted_iota(jnp.int32, (q.shape[0], LANES), 1)
    one_lane = jnp.where(lane == 0, 1.0, 0.0).astype(q.dtype)
    wide_q = jnp.concatenate([q, one_lane], axis=1)
    return lax.dot_general(wide_q, k_buf[...], (((1,), (1,)), ((), ())), preferred_element_type=jnp.float32)


def weigh(scores, peak, v_buf):
    wide_peak = jnp.concatenate([peak] * (scores.shape[1] // LANES), axis=1)
    exps = jnp.exp2(scores * FACTOR - wide_peak).astype(v_buf.dtype)
    both = jnp.dot(exps, v_buf[...], preferred_element_type=jnp.float32)
    return both[:, :HD], both[:, HD:]


def peak_of(scores):
    peak = jnp.max(scores, axis=1, keepdims=True) * FACTOR
    return jnp.broadcast_to(peak, (scores.shape[0], LANES))


def finish(above, below, valid_rows, first_row, dtype):
    row = lax.broadcasted_iota(jnp.int32, above.shape, 0) + first_row
    return jnp.where(row < valid_rows, above / below, 0.0).astype(dtype)


def in_turn(works):
    scores = works[0][0]()
    for index, (_, finish_work) in enumerate(works):
        later = works[index + 1][0]() if index + 1 < len(works) else None
        finish_work(scores)
        scores = later


def own_kernel(ratio, block, cuts, lengths_ref, q_hbm, k_hbm, v_hbm, o_ref, sum_ref, peak_ref, *rest):
    piece_refs, (q_ref, k_ref, v_ref, k_buf, v_buf, sems) = rest[: len(cuts)], rest[len(cuts) :]
    groups = k_ref.shape[1] // HD
    copies = [pltpu.make_async_copy(k_hbm, k_ref, sems.at[0]), pltpu.make_async_copy(v_hbm, v_ref, sems.at[1])]
    for group in range(groups):
        columns = pl.ds(group * ratio * HD, ratio * HD)
        copies.append(pltpu.make_async_copy(q_hbm.at[:, columns], q_ref.at[:, columns], sems.at[2 + group]))
    for copy in copies:
        copy.start()
    copies[0].wait()
    copies[1].wait()
    device = lax.axis_index("cand")
    half = q_ref.shape[0] // 2
    sent = pl.ds(pl.multiple_of((1 - (device & 1)) * half, half), half)
    for group in range(groups):
        load_span(k_buf.at[group], v_buf.at[group], k_ref, v_ref, group, lengths_ref[device], 0)

    def score(rows, columns, group):
        if rows.start == 0 and columns.start == group * ratio * HD:
            copies[2 + group].wait()
        return score_rows(q_ref[rows, columns], k_buf.at[group])

    def weigh_own(rows, columns, group, scores):
        peak = peak_of(scores)
        o_ref[rows, columns], sum_ref[rows, columns] = weigh(scores, peak, v_buf.at[group])
        peak_ref[rows, columns] = peak

    works = []
    for head in range(groups * ratio):
        for start in range(0, q_ref.shape[0], block):
            place = (slice(start, start + block), slice(head * HD, (head + 1) * HD), head // ratio)
            works.append((functools.partial(score, *place), functools.partial(weigh_own, *place)))
    in_turn(works)
    for piece_ref, (low, high) in zip(piece_refs, cuts):
        piece_ref[...] = q_ref[sent, low * HD : high * HD]


def choose_kernel(lengths_ref, winners_ref, own_ref, companion_ref, *out_refs):
    place = Place(lengths_ref, winners_ref)
    for won, ref in ((True, own_ref), (False, companion_ref)):
        @pl.when(place.won == won)
        def _():
            start = 0
            for out_ref in out_refs:
                out_ref[...] = ref[:, start : start + out_ref.shape[1]]
                start += out_ref.shape[1]


def join_work(rows, first_row, columns, valid_rows, q_ref, own_refs, k_buf, v_buf, totals, keep_output):
    o_ref, sum_ref, peak_ref = own_refs

    def score():
        return score_rows(q_ref[rows, columns], k_buf)

    def join(scores):
        own_peak = peak_ref[rows, columns]
        peak = jnp.maximum(own_peak, peak_of(scores))
        above, below = weigh(scores, peak, v_buf)
        keep = jnp.exp2(own_peak - peak)
        above += o_ref[rows, columns] * keep
        below += sum_ref[rows, columns] * keep
        output = finish(above, below, valid_rows, first_row, q_ref.dtype)
        totals.append((columns, sum_rows(output)))
        keep_output(output)

    return score, join


def sum_rows(output):
    return jnp.sum(output.astype(jnp.float32).reshape(output.shape[0] // 8, 8, LANES), axis=0)


def weigh_totals(totals, weight_ref, valid):
    score = jnp.zeros((8, LANES), jnp.float32)
    for columns, total in totals:
        score += total * weight_ref[:, columns]
    return jnp.full((8, LANES), jnp.sum(score), jnp.float32) / valid.astype(jnp.float32)


def first_kernel(
    ratio, block, lengths_ref, weight_ref, q_ref, o_ref, sum_ref, peak_ref, k_ref, v_ref, out_ref, part_ref, k_buf, v_buf
):
    device = lax.axis_index("cand")
    span, heads = q_ref.shape[0], q_ref.shape[1] // HD
    valid = lengths_ref[device]
    for group in range(heads // ratio):
        load_span(k_buf.at[group], v_buf.at[group], k_ref, v_ref, group, lengths_ref[device ^ 1], 0)

    def keep(rows, columns, output):
        out_ref[rows, columns] = output

    works, totals = [], []
    for head in range(heads):
        for start in range(0, span, block):
            rows, columns = slice(start, start + block), slice(head * HD, (head + 1) * HD)
            works.append(
                join_work(
                    rows, start, columns, valid, q_ref, (o_ref, sum_ref, peak_ref), k_buf.at[head // ratio],
                    v_buf.at[head // ratio], totals, functools.partial(keep, rows, columns),
                )
            )
    in_turn(works)
    part_ref[...] = weigh_totals(totals, weight_ref, valid)


def lose_works(place, low, high, ratio, q_ref, k_buf, v_buf, totals, out_ref):
    def score(head):
        return score_rows(q_ref[:, (head - low) * HD : (head - low + 1) * HD], k_buf.at[head // ratio])

    def attend(head, scores):
        columns = slice(head * HD, (head + 1) * HD)
        above, below = weigh(scores, peak_of(scores), v_buf.at[head // ratio])
        first_row = place.bit * q_ref.shape[0]
        output = finish(above, below, place.partner_valid, first_row, out_ref.dtype)
        totals.append((columns, sum_rows(output)))
        out_ref[:, columns] = output

    return [(functools.partial(score, head), functools.partial(attend, head)) for head in range(low, high)]


def second_kernel(
    ratio, high, lengths_ref, winners_ref, weight_ref, q_ref, o_ref, sum_ref, peak_ref,
    ka_ref, va_ref, kb_ref, vb_ref, piece_ref, first_ref, out_ref, part_ref, k_buf, v_buf,
):
    place = Place(lengths_ref, winners_ref)
    half, span, heads = piece_ref.shape[0], q_ref.shape[0], q_ref.shape[1] // HD

    def give_part(part):
        row = lax.broadcasted_iota(jnp.int32, part.shape, 0)
        part_ref[...] = jnp.where(row == 0, part, first_ref[...])

    @pl.when(place.won)
    def _():
        for group in range(heads // ratio):
            load_span(k_buf.at[group, :span], v_buf.at[group, :span], kb_ref, vb_ref, group, place.rival_valid, 0)
        works, totals = [], []

        def keep(head, output):
            out_ref[:, head * HD : (head + 1) * HD] = output

        def work(head, start, keep_output):
            return join_work(
                pl.ds(start, half), start, slice(head * HD, (head + 1) * HD), place.own_valid, q_ref,
                (o_ref, sum_ref, peak_ref), k_buf.at[head // ratio, :span], v_buf.at[head // ratio, :span], totals,
                keep_output,
            )

        own_row = pl.multiple_of(place.bit * half, half)
        other_row = pl.multiple_of(half - own_row, half)
        works = [work(head, own_row, functools.partial(keep, head)) for head in range(heads)]
        works += [work(head, other_row, lambda output: None) for head in range(high, heads)]
        in_turn(works)
        give_part(weigh_totals(totals, weight_ref, place.own_valid))

    @pl.when(jnp.logical_not(place.won))
    def _():
        for group in range((high - 1) // ratio + 1):
            load_span(k_buf.at[group], v_buf.at[group], ka_ref, va_ref, group, place.partner_valid, 0)
            load_span(k_buf.at[group], v_buf.at[group], kb_ref, vb_ref, group, place.rival_valid, span)
        totals = []
        in_turn(lose_works(place, 0, high, ratio, piece_ref, k_buf, v_buf, totals, out_ref))
        give_part(weigh_totals(totals, weight_ref, place.partner_valid))


def last_kernel(
    ratio, low, lengths_ref, winners_ref, ka_ref, va_ref, kb_ref, vb_ref, piece_ref, first_ref, second_ref,
    first_out, second_out, k_buf, v_buf, out_buf, sems,
):
    place = Place(lengths_ref, winners_ref)
    heads, span = second_ref.shape[1] // HD, ka_ref.shape[0]
    before, after = pl.ds(0, low * HD), pl.ds(low * HD, (heads - low) * HD)
    first_copy = pltpu.make_async_copy(first_ref, first_out, sems.at[0])
    before_copy = pltpu.make_async_copy(second_ref.at[:, before], second_out.at[:, before], sems.at[1])
    won_copy = pltpu.make_async_copy(second_ref.at[:, after], second_out.at[:, after], sems.at[2])

    def lost_copy(head):
        columns = pl.ds(head * HD, HD)
        return pltpu.make_async_copy(out_buf.at[:, columns], second_out.at[:, columns], sems.at[3 + head - low])

    first_copy.start()
    before_copy.start()

    @pl.when(place.won)
    def _():
        won_copy.start()
        won_copy.wait()

    @pl.when(jnp.logical_not(place.won))
    def _():
        for group in range(low // ratio, heads // ratio):
            load_span(k_buf.at[group], v_buf.at[group], ka_ref, va_ref, group, place.partner_valid, 0)
            load_span(k_buf.at[group], v_buf.at[group], kb_ref, vb_ref, group, place.rival_valid, span)
        works = []
        for head, (score, attend) in zip(
            range(low, heads), lose_works(place, low, heads, ratio, piece_ref, k_buf, v_buf, [], out_buf)
        ):

            def attend_and_copy(scores, head=head, attend=attend):
                attend(scores)
                lost_copy(head).start()

            works.append((score, attend_and_copy))
        in_turn(works)
        for head in range(low, heads):
            lost_copy(head).wait()

    first_copy.wait()
    before_copy.wait()


def kernel_call(kernel, operands, in_specs, out_shape, out_specs, scratch=(), flops=0, aliases=None):
    return pl.pallas_call(
        kernel,
        out_shape=out_shape,
        in_specs=in_specs,
        out_specs=out_specs,
        scratch_shapes=scratch,
        input_output_aliases=aliases or {},
        compiler_params=pltpu.CompilerParams(vmem_limit_bytes=VMEM_LIMIT),
        cost_estimate=pl.CostEstimate(flops=COST * flops, bytes_accessed=COST * flops // 256, transcendentals=flops // 512),
    )(*operands)


def body(queries, keys, values, lengths, winners, score_weight):
    span, width = queries.shape
    half = span // 2
    heads = width // HD
    groups = keys.shape[1] // HD
    ratio = heads // groups
    block = min(span, 256)
    dtype = queries.dtype
    weight = score_weight.reshape(1, -1)
    share = 4 * span * span * HD
    part_shape = jax.ShapeDtypeStruct((8, LANES), jnp.float32)
    second_shape = jax.ShapeDtypeStruct((half, width), dtype)

    def buffers(spans):
        return [pltpu.VMEM((groups, spans * span, HD + LANES), dtype)] * 2

    companion_keys = from_partner(keys, "cand", 0)
    companion_values = from_partner(values, "cand", 0)

    middle = heads - LAST_HEADS
    cuts = [(0, middle), (middle, heads)]
    piece_shapes = tuple(jax.ShapeDtypeStruct((half, (high - low) * HD), dtype) for low, high in cuts)
    partial = jax.ShapeDtypeStruct((span, width), jnp.float32)
    *own, sent = kernel_call(
        functools.partial(own_kernel, ratio, block, cuts),
        (lengths, *[pltpu.with_memory_space_constraint(array, pltpu.HBM) for array in (queries, keys, values)]),
        [SMEM, HBM, HBM, HBM],
        (partial,) * 3 + piece_shapes,
        (VMEM,) * (3 + len(cuts)),
        [pltpu.VMEM(array.shape, dtype) for array in (queries, keys, values)]
        + buffers(1)
        + [pltpu.SemaphoreType.DMA((2 + groups,))],
        share * heads,
    )
    own, sent = own[:3], own[3:] + [sent]

    pieces = [from_partner(piece, "cand", 0) for piece in sent]

    def choose(own, companion, parts):
        shape = jax.ShapeDtypeStruct((span, own.shape[1] // parts), dtype)
        return kernel_call(
            choose_kernel, (lengths, winners, own, companion), [SMEM, SMEM, VMEM, VMEM], (shape,) * parts, (VMEM,) * parts
        )

    chosen_keys = choose(keys, companion_keys, 1)[0]
    rival_keys = from_partner(chosen_keys, "cand", 1)
    companion_values, _ = lax.optimization_barrier((companion_values, chosen_keys))
    rival_values = from_partner(choose(values, companion_values, 1)[0], "cand", 1)

    first_shape = jax.ShapeDtypeStruct((span, width), dtype)
    first, first_part = kernel_call(
        functools.partial(first_kernel, ratio, block),
        (lengths, weight, queries, *own, companion_keys, companion_values),
        [SMEM] + [VMEM] * 7,
        (first_shape, part_shape),
        (VMEM, VMEM),
        buffers(1),
        share * heads // 5,
    )
    second, part = kernel_call(
        functools.partial(second_kernel, ratio, middle),
        (
            lengths, winners, weight, queries, *own, companion_keys, companion_values, rival_keys, rival_values,
            pieces[0], first_part,
        ),
        [SMEM] * 2 + [VMEM] * 11,
        (second_shape, part_shape),
        (VMEM, VMEM),
        buffers(2),
        share * middle,
    )
    first, second = kernel_call(
        functools.partial(last_kernel, ratio, middle),
        (lengths, winners, companion_keys, companion_values, rival_keys, rival_values, pieces[1], first, second),
        [SMEM] * 2 + [VMEM] * 7,
        (first_shape, second_shape),
        (ANY, ANY),
        buffers(2) + [pltpu.VMEM((half, width), dtype), pltpu.SemaphoreType.DMA((3 + LAST_HEADS,))],
        share // 16,
    )

    cores = lax.axis_size("head")
    devices = lax.axis_size("cand") * cores
    diagonal = [(i, i ^ (cores + 1)) for i in range(devices)]
    beside = from_partner(part, "head", 0)
    across = from_partner(part, "cand", 0) + lax.ppermute(part, ("cand", "head"), diagonal)
    row = lax.broadcasted_iota(jnp.int32, part.shape, 0)
    sums = lax.optimization_barrier(part + beside + jnp.where(row == 0, across, 0.0))
    final_round_score, first_score = sums[0, :1], sums[1, :1]
    return first, second, first_score, final_round_score


def solution(mesh):
    in_specs = (
        P(("grp", "cand"), "head"),
        P(("grp", "cand"), "head"),
        P(("grp", "cand"), "head"),
        P("grp"),
        P("grp"),
        P("head"),
    )
    out_specs = (
        P(("grp", "cand"), "head"),
        P(("grp", "cand"), "head"),
        P(("grp", "cand")),
        P(("grp", "cand")),
    )
    return jax.shard_map(body, mesh=mesh, in_specs=in_specs, out_specs=out_specs, check_vma=False)
```

time: 44.6 us -> 35.1 us (0.79)
  Pallas kernels: 22.6 us -> 17.8 us
  starting transfers between devices: 16.5 us -> 11.7 us
  local copies, waits for them, and re-layouts: 3.89 us -> 1.2 us
  waiting for transfers between devices: 0.47 us -> 3.03 us
    pallas_call x10 -> x6, Pallas kernels: 22.6 us -> 17.8 us  [kernel_call(): pl.pallas_call(kernel, out_shape=out_shape, in_specs=in_specs, out_specs=...]
    ppermute x11 -> x8, starting transfers between devices: 16.5 us -> 11.7 us  [from_partner(): lax.ppermute(value, axis, [(i, i ^ 1 << stride) for i in range(lax.axis_s...]
    unnamed x18 -> x12, local copies, waits for them, and re-layouts: 3.89 us -> 0.67 us
    ppermute x11 -> x8, waiting for transfers between devices: 0.47 us -> 2.89 us  [from_partner(): lax.ppermute(value, axis, [(i, i ^ 1 << stride) for i in range(lax.axis_s...]
    slice x0 -> x1, local copies, waits for them, and re-layouts: none -> 0.52 us  [body(): final_round_score, first_score = (sums[0, :1], sums[1, :1])]
  transfers between devices with their start and end apart: 12 -> 9, of which waited for: 1 -> 4; matrix products, arithmetic and copies ran while one was open for 0% -> 0% of each run, Pallas kernels for 48% -> 52%
where the time goes in v3:
time: 35.1 us; the launch traced here: 34.5 us
  Pallas kernels  17.8 us (51%)
  starting transfers between devices  11.7 us (33%)
  waiting for transfers between devices  3.03 us (9%)
  local copies, waits for them, and re-layouts  1.2 us (3%)
  between operations  0.73 us (2%)
    pallas_call x6, Pallas kernels, kernel_call(): pl.pallas_call(kernel, out_shape=out_shape, in_specs=in_specs, out_specs=...  17.8 us
    ppermute x8, starting transfers between devices, from_partner(): lax.ppermute(value, axis, [(i, i ^ 1 << stride) for i in range(lax.axis_s...  11.7 us
    ppermute x8, waiting for transfers between devices, from_partner(): lax.ppermute(value, axis, [(i, i ^ 1 << stride) for i in range(lax.axis_s...  2.89 us
  transfers between devices with their start and end apart: 9, of which 4 were waited for; matrix products, arithmetic and copies ran while one was open for 0% of the time, Pallas kernels for 52%

profile of v3, /device:TPU:0, one launch (start us, length us, event | category | flops | bytes accessed | tf_op | source)
XLA Modules:
  0.0 34.5 jit_solution(1551595073516846923)
XLA Ops:
  0.7 3.0 %collective-permute-start = (bf16[512,256]{1,0:T(8,128)(2,1)}, bf16[512,256]{1,0:T(8,128)(2,1)S(1)}, u32[]{:S(2)}, u32[]{:S(2)}) collective-permute-start(bf16[512,256]{1,0:T(8,128)(2,1)} %k_hbm.1), channel_id=1, source_target_pairs={{0,2},{2,0},{4,6},{6,4},{8,10},{10,8},{12,14},{14,12},{1,3},{3,1},... | collective-permute-start | bytes 786440 | tf_op jit(solution)/shard_map/ppermute | solution.py:25
  3.7 0.1 collective-permute-start.1
  3.7 0.7 %copy-done.2 = s32[8]{0:T(128)S(1)} copy-done((s32[8]{0:T(128)S(1)}, s32[8]{0:T(128)}, u32[]{:S(2)}) %copy-start.2) | copy-done | bytes 56
  4.4 5.6 %shard_map.95 = (f32[512,1280]{1,0:T(8,128)S(1)}, f32[512,1280]{1,0:T(8,128)S(1)}, f32[512,1280]{1,0:T(8,128)S(1)}, bf16[256,768]{1,0:T(8,128)(2,1)S(1)}, bf16[256,512]{1,0:T(8,128)(2,1)S(1)}) custom-call(s32[8]{0:T(128)S(1)} %copy-done.2, bf16[512,1280]{1,0:T(8,128)(2,1)} %q_ref.3, bf16[512,256]{1,0:T(8,128)(2,1)} %k_hbm.1, bf16[512,256]{1,0:T(8,128)(2,1)} %v_hbm.1), custom_call_target="tpu_custom_call" | custom-call | flops 13421772800 | bytes 52428800 | tf_op jit(solution)/shard_map/pallas_call | solution.py:297
  10.0 2.0 %collective-permute-start.5 = (bf16[256,768]{1,0:T(8,128)(2,1)S(1)}, bf16[256,768]{1,0:T(8,128)(2,1)S(1)}, u32[]{:S(2)}, u32[]{:S(2)}) collective-permute-start(bf16[256,768]{1,0:T(8,128)(2,1)S(1)} %get-tuple-element.22), channel_id=1, source_target_pairs={{0,2},{2,0},{4,6},{6,4},{8,10},{10,8},{12,14},{14,12},{1,3},{3,1},... | collective-permute-start | bytes 1179656 | tf_op jit(solution)/shard_map/ppermute | solution.py:25
  12.0 0.1 collective-permute-start.4
  12.1 0.0 collective-permute-done.companion_ref.k_ref.ka_ref
  12.1 0.6 %shard_map.93 = bf16[512,256]{1,0:T(8,128)(2,1)S(1)} custom-call(s32[8]{0:T(128)S(1)} %copy-done.2, s32[4]{0:T(128)S(1)} %copy-done.3, bf16[512,256]{1,0:T(8,128)(2,1)S(1)} %copy-done, bf16[512,256]{1,0:T(8,128)(2,1)S(1)} %collective-permute-done.companion_ref.k_ref.ka_ref), custom_call_target="tpu_custom_call" | custom-call | tf_op jit(solution)/shard_map/pallas_call | solution.py:297
  12.7 2.1 %collective-permute-start.2 = (bf16[512,256]{1,0:T(8,128)(2,1)S(1)}, bf16[512,256]{1,0:T(8,128)(2,1)S(1)}, u32[]{:S(2)}, u32[]{:S(2)}) collective-permute-start(bf16[512,256]{1,0:T(8,128)(2,1)S(1)} %shard_map.93), channel_id=1, source_target_pairs={{0,4},{2,6},{4,0},{6,2},{8,12},{10,14},{12,8},{14,10},{1,5},{3,7},... | collective-permute-start | bytes 786440 | tf_op jit(solution)/shard_map/ppermute | solution.py:25
  14.8 1.8 %collective-permute-done.1.companion_ref.v_ref.va_ref = bf16[512,256]{1,0:T(8,128)(2,1)S(1)} collective-permute-done((bf16[512,256]{1,0:T(8,128)(2,1)}, bf16[512,256]{1,0:T(8,128)(2,1)S(1)}, u32[]{:S(2)}, u32[]{:S(2)}) %collective-permute-start.1) | collective-permute-done | bytes 262176 | tf_op jit(solution)/shard_map/ppermute | solution.py:25
  16.6 0.6 %shard_map.94 = bf16[512,256]{1,0:T(8,128)(2,1)S(1)} custom-call(s32[8]{0:T(128)S(1)} %copy-done.2, s32[4]{0:T(128)S(1)} %copy-done.3, bf16[512,256]{1,0:T(8,128)(2,1)S(1)} %copy-done.1, bf16[512,256]{1,0:T(8,128)(2,1)S(1)} %collective-permute-done.1.companion_ref.v_ref.va_ref), custom_call_target="tpu_custom_call" | custom-call | tf_op jit(solution)/shard_map/pallas_call | solution.py:297
  17.2 2.2 %collective-permute-start.3 = (bf16[512,256]{1,0:T(8,128)(2,1)S(1)}, bf16[512,256]{1,0:T(8,128)(2,1)S(1)}, u32[]{:S(2)}, u32[]{:S(2)}) collective-permute-start(bf16[512,256]{1,0:T(8,128)(2,1)S(1)} %shard_map.94), channel_id=1, source_target_pairs={{0,4},{2,6},{4,0},{6,2},{8,12},{10,14},{12,8},{14,10},{1,5},{3,7},... | collective-permute-start | bytes 786440 | tf_op jit(solution)/shard_map/ppermute | solution.py:25
  19.4 5.1 %shard_map.96 = (bf16[512,1280]{1,0:T(8,128)(2,1)S(1)}, f32[8,128]{1,0:T(8,128)S(1)}) custom-call(s32[8]{0:T(128)S(1)} %copy-done.2, f32[1,1280]{1,0:T(1,128)S(1)} %reshape.11.weight_ref, bf16[512,1280]{1,0:T(8,128)(2,1)S(1)} %copy-done.4, f32[512,1280]{1,0:T(8,128)S(1)} %get-tuple-element.18.o_ref, f32[512,1280]{1,0:T(8,128)S(1)} %get-tuple-element.19.sum_ref, ...), custom_call_target="tpu_custom_call" | custom-call | flops 2684354560 | bytes 10485760 | tf_op jit(solution)/shard_map/pallas_call | solution.py:297
  24.5 0.5 %collective-permute-done.5.piece_ref = bf16[256,768]{1,0:T(8,128)(2,1)S(1)} collective-permute-done((bf16[256,768]{1,0:T(8,128)(2,1)S(1)}, bf16[256,768]{1,0:T(8,128)(2,1)S(1)}, u32[]{:S(2)}, u32[]{:S(2)}) %collective-permute-start.5) | collective-permute-done | bytes 393248 | tf_op jit(solution)/shard_map/ppermute | solution.py:25
  25.0 0.6 %collective-permute-done.3.vb_ref = bf16[512,256]{1,0:T(8,128)(2,1)S(1)} collective-permute-done((bf16[512,256]{1,0:T(8,128)(2,1)S(1)}, bf16[512,256]{1,0:T(8,128)(2,1)S(1)}, u32[]{:S(2)}, u32[]{:S(2)}) %collective-permute-start.3) | collective-permute-done | bytes 262176 | tf_op jit(solution)/shard_map/ppermute | solution.py:25
  25.6 4.1 %shard_map.97 = (bf16[256,1280]{1,0:T(8,128)(2,1)S(1)}, f32[8,128]{1,0:T(8,128)S(1)}) custom-call(s32[8]{0:T(128)S(1)} %copy-done.2, s32[4]{0:T(128)S(1)} %copy-done.3, f32[1,1280]{1,0:T(1,128)S(1)} %reshape.11.weight_ref, bf16[512,1280]{1,0:T(8,128)(2,1)S(1)} %copy-done.4, f32[512,1280]{1,0:T(8,128)S(1)} %get-tuple-element.18.o_ref, ...), custom_call_target="tpu_custom_call" | custom-call | flops 8053063680 | bytes 31457280 | tf_op jit(solution)/shard_map/pallas_call | solution.py:297
  29.7 1.2 %collective-permute-start.7 = (f32[8,128]{1,0:T(8,128)S(1)}, f32[8,128]{1,0:T(8,128)S(1)}, u32[]{:S(2)}, u32[]{:S(2)}) collective-permute-start(f32[8,128]{1,0:T(8,128)S(1)} %get-tuple-element.27), channel_id=1, source_target_pairs={{0,2},{2,0},{4,6},{6,4},{8,10},{10,8},{12,14},{14,12},{1,3},{3,1},... | collective-permute-start | bytes 12296 | tf_op jit(solution)/shard_map/ppermute | solution.py:25
  30.9 0.0 collective-permute-start.8
  30.9 1.0 %collective-permute-start.6 = (f32[8,128]{1,0:T(8,128)S(1)}, f32[8,128]{1,0:T(8,128)S(1)}, u32[]{:S(2)}, u32[]{:S(2)}) collective-permute-start(f32[8,128]{1,0:T(8,128)S(1)} %get-tuple-element.27), channel_id=1, source_target_pairs={{0,1},{1,0},{2,3},{3,2},{4,5},{5,4},{6,7},{7,6},{8,9},{9,8},{10,11... | collective-permute-start | bytes 12296 | tf_op jit(solution)/shard_map/ppermute | solution.py:25
  31.9 1.9 %shard_map.98 = (bf16[512,1280]{1,0:T(8,128)(2,1)}, bf16[256,1280]{1,0:T(8,128)(2,1)}) custom-call(s32[8]{0:T(128)S(1)} %copy-done.2, s32[4]{0:T(128)S(1)} %copy-done.3, bf16[512,256]{1,0:T(8,128)(2,1)S(1)} %collective-permute-done.companion_ref.k_ref.ka_ref, bf16[512,256]{1,0:T(8,128)(2,1)S(1)} %collective-permute-done.1.companion_ref.v_ref.va_ref, ...), custom_call_target="tpu_custom_call" | custom-call | flops 83886080 | bytes 327680 | tf_op jit(solution)/shard_map/pallas_call | solution.py:297
  33.8 0.1 collective-permute-done.8
  33.9 0.0 collective-permute-done.6
  33.9 0.1 select_add_fusion
  34.0 0.5 %fusion = (f32[1,1]{1,0:T(1,128)}, f32[1,1]{1,0:T(1,128)}) fusion(f32[8,128]{1,0:T(8,128)S(1)} %select_add_fusion), kind=kLoop, calls=%fused_computation.2 | loop fusion | bytes 16 | tf_op jit(solution)/shard_map/slice | solution.py:397
  (16 shorter events, 0.0 us)
Async XLA Ops:
  0.6 11.5 %copy-start = (bf16[512,256]{1,0:T(8,128)(2,1)S(1)}, bf16[512,256]{1,0:T(8,128)(2,1)}, u32[]{:S(2)}) copy-start(bf16[512,256]{1,0:T(8,128)(2,1)} %k_hbm.1) | copy-start | bytes 786436
  0.6 16.0 %copy-start.1 = (bf16[512,256]{1,0:T(8,128)(2,1)S(1)}, bf16[512,256]{1,0:T(8,128)(2,1)}, u32[]{:S(2)}) copy-start(bf16[512,256]{1,0:T(8,128)(2,1)} %v_hbm.1) | copy-start | bytes 786436
  0.7 11.5 %collective-permute-start = (bf16[512,256]{1,0:T(8,128)(2,1)}, bf16[512,256]{1,0:T(8,128)(2,1)S(1)}, u32[]{:S(2)}, u32[]{:S(2)}) collective-permute-start(bf16[512,256]{1,0:T(8,128)(2,1)} %k_hbm.1), channel_id=1, source_target_pairs={{0,2},{2,0},{4,6},{6,4},{8,10},{10,8},{12,14},{14,12},{1,3},{3,1},... | collective-permute-start | bytes 786440 | tf_op jit(solution)/shard_map/ppermute | solution.py:25
  3.7 13.0 %collective-permute-start.1 = (bf16[512,256]{1,0:T(8,128)(2,1)}, bf16[512,256]{1,0:T(8,128)(2,1)S(1)}, u32[]{:S(2)}, u32[]{:S(2)}) collective-permute-start(bf16[512,256]{1,0:T(8,128)(2,1)} %v_hbm.1), channel_id=1, source_target_pairs={{0,2},{2,0},{4,6},{6,4},{8,10},{10,8},{12,14},{14,12},{1,3},{3,1},... | collective-permute-start | bytes 786440 | tf_op jit(solution)/shard_map/ppermute | solution.py:25
  3.7 0.7 %copy-start.2 = (s32[8]{0:T(128)S(1)}, s32[8]{0:T(128)}, u32[]{:S(2)}) copy-start(s32[8]{0:T(128)} %lengths_ref.11) | copy-start | bytes 100
  4.4 7.7 %copy-start.3 = (s32[4]{0:T(128)S(1)}, s32[4]{0:T(128)}, u32[]{:S(2)}) copy-start(s32[4]{0:T(128)} %winners_ref.7) | copy-start | bytes 52
  4.4 15.0 %copy-start.5 = (f32[1280]{0:T(1024)S(1)}, f32[1280]{0:T(1024)}, u32[]{:S(2)}) copy-start(f32[1280]{0:T(1024)} %param.11) | copy-start | bytes 15364
  4.4 15.0 %copy-start.4 = (bf16[512,1280]{1,0:T(8,128)(2,1)S(1)}, bf16[512,1280]{1,0:T(8,128)(2,1)}, u32[]{:S(2)}) copy-start(bf16[512,1280]{1,0:T(8,128)(2,1)} %q_ref.3) | copy-start | bytes 3932164
  10.0 15.0 %collective-permute-start.5 = (bf16[256,768]{1,0:T(8,128)(2,1)S(1)}, bf16[256,768]{1,0:T(8,128)(2,1)S(1)}, u32[]{:S(2)}, u32[]{:S(2)}) collective-permute-start(bf16[256,768]{1,0:T(8,128)(2,1)S(1)} %get-tuple-element.22), channel_id=1, source_target_pairs={{0,2},{2,0},{4,6},{6,4},{8,10},{10,8},{12,14},{14,12},{1,3},{3,1},... | collective-permute-start | bytes 1179656 | tf_op jit(solution)/shard_map/ppermute | solution.py:25
  12.0 19.9 %collective-permute-start.4 = (bf16[256,512]{1,0:T(8,128)(2,1)S(1)}, bf16[256,512]{1,0:T(8,128)(2,1)S(1)}, u32[]{:S(2)}, u32[]{:S(2)}) collective-permute-start(bf16[256,512]{1,0:T(8,128)(2,1)S(1)} %get-tuple-element.17), channel_id=1, source_target_pairs={{0,2},{2,0},{4,6},{6,4},{8,10},{10,8},{12,14},{14,12},{1,3},{3,1},... | collective-permute-start | bytes 786440 | tf_op jit(solution)/shard_map/ppermute | solution.py:25
  12.7 12.3 %collective-permute-start.2 = (bf16[512,256]{1,0:T(8,128)(2,1)S(1)}, bf16[512,256]{1,0:T(8,128)(2,1)S(1)}, u32[]{:S(2)}, u32[]{:S(2)}) collective-permute-start(bf16[512,256]{1,0:T(8,128)(2,1)S(1)} %shard_map.93), channel_id=1, source_target_pairs={{0,4},{2,6},{4,0},{6,2},{8,12},{10,14},{12,8},{14,10},{1,5},{3,7},... | collective-permute-start | bytes 786440 | tf_op jit(solution)/shard_map/ppermute | solution.py:25
  17.2 8.4 %collective-permute-start.3 = (bf16[512,256]{1,0:T(8,128)(2,1)S(1)}, bf16[512,256]{1,0:T(8,128)(2,1)S(1)}, u32[]{:S(2)}, u32[]{:S(2)}) collective-permute-start(bf16[512,256]{1,0:T(8,128)(2,1)S(1)} %shard_map.94), channel_id=1, source_target_pairs={{0,4},{2,6},{4,0},{6,2},{8,12},{10,14},{12,8},{14,10},{1,5},{3,7},... | collective-permute-start | bytes 786440 | tf_op jit(solution)/shard_map/ppermute | solution.py:25
  29.7 4.1 %collective-permute-start.7 = (f32[8,128]{1,0:T(8,128)S(1)}, f32[8,128]{1,0:T(8,128)S(1)}, u32[]{:S(2)}, u32[]{:S(2)}) collective-permute-start(f32[8,128]{1,0:T(8,128)S(1)} %get-tuple-element.27), channel_id=1, source_target_pairs={{0,2},{2,0},{4,6},{6,4},{8,10},{10,8},{12,14},{14,12},{1,3},{3,1},... | collective-permute-start | bytes 12296 | tf_op jit(solution)/shard_map/ppermute | solution.py:25
  30.9 3.0 %collective-permute-start.8 = (f32[8,128]{1,0:T(8,128)S(1)}, f32[8,128]{1,0:T(8,128)S(1)}, u32[]{:S(2)}, u32[]{:S(2)}) collective-permute-start(f32[8,128]{1,0:T(8,128)S(1)} %get-tuple-element.27), channel_id=1, source_target_pairs={{0,3},{1,2},{2,1},{3,0},{4,7},{5,6},{6,5},{7,4},{8,11},{9,10},{10,... | collective-permute-start | bytes 12296 | tf_op jit(solution)/shard_map/ppermute | solution.py:394
  30.9 3.0 %collective-permute-start.6 = (f32[8,128]{1,0:T(8,128)S(1)}, f32[8,128]{1,0:T(8,128)S(1)}, u32[]{:S(2)}, u32[]{:S(2)}) collective-permute-start(f32[8,128]{1,0:T(8,128)S(1)} %get-tuple-element.27), channel_id=1, source_target_pairs={{0,1},{1,0},{2,3},{3,2},{4,5},{5,4},{6,7},{7,6},{8,9},{9,8},{10,11... | collective-permute-start | bytes 12296 | tf_op jit(solution)/shard_map/ppermute | solution.py:25

commit v4 on v3

--- a/solution.py
+++ b/solution.py
@@ -12,30 +12,40 @@
 LOG2E = 1.4426950408889634
 FACTOR = HD ** (-0.5) * LOG2E
 BARRED = -1e30
-LAST_HEADS = 4
+LAST_HEADS = 5
 COST = 10
 VMEM_LIMIT = 12 * 1024 * 1024
 ANY = pl.BlockSpec(memory_space=pl.ANY)
 HBM = pl.BlockSpec(memory_space=pltpu.HBM)
 VMEM = pl.BlockSpec(memory_space=pltpu.VMEM)
-SMEM = pl.BlockSpec(memory_space=pltpu.SMEM)
 
 
 def from_partner(value, axis, stride):
     return lax.ppermute(value, axis, [(i, i ^ 1 << stride) for i in range(lax.axis_size(axis))])
 
 
-class Place:
-    def __init__(self, lengths_ref, winners_ref):
-        device = lax.axis_index("cand")
-        self.bit = device & 1
-        pair = device >> 1
-        self.winner = winners_ref[pair]
-        self.won = self.bit == self.winner
-        rival_pair = pair ^ 1
-        self.own_valid = lengths_ref[device]
-        self.partner_valid = lengths_ref[device ^ 1]
-        self.rival_valid = lengths_ref[2 * rival_pair + winners_ref[rival_pair]]
+OWN_VALID, PARTNER_VALID, RIVAL_VALID, WON = range(4)
+
+
+def gather_facts(lengths_ref, winners_ref):
+    device = lax.axis_index("cand")
+    pair = device >> 1
+    rival_pair = pair ^ 1
+    rival = 2 * rival_pair + winners_ref[rival_pair]
+    won = jnp.where(winners_ref[pair] == (device & 1), 1, 0)
+    row = lax.broadcasted_iota(jnp.int32, (8, LANES), 0)
+    facts = jnp.zeros((8, LANES), jnp.int32)
+    for index, number in enumerate((lengths_ref[device], lengths_ref[device ^ 1], lengths_ref[rival], won)):
+        facts = jnp.where(row == index, number, facts)
+    return facts.astype(jnp.float32)
+
+
+def valid_of(facts_ref, index):
+    return facts_ref[index : index + 1, :].astype(jnp.int32)
+
+
+def has_won(facts_ref):
+    return jnp.max(facts_ref[WON : WON + 1, :]) > 0.5
 
 
 def load_span(k_buf, v_buf, k_ref, v_ref, group, valid, start):
@@ -83,22 +93,29 @@
         scores = later
 
 
-def own_kernel(ratio, block, cuts, lengths_ref, q_hbm, k_hbm, v_hbm, o_ref, sum_ref, peak_ref, *rest):
-    piece_refs, (q_ref, k_ref, v_ref, k_buf, v_buf, sems) = rest[: len(cuts)], rest[len(cuts) :]
+def own_kernel(ratio, block, cuts, lengths_hbm, winners_hbm, q_hbm, k_hbm, v_hbm, o_ref, sum_ref, peak_ref, facts_ref, *rest):
+    piece_refs, (q_ref, k_ref, v_ref, lengths_ref, winners_ref, k_buf, v_buf, sems) = rest[: len(cuts)], rest[len(cuts) :]
     groups = k_ref.shape[1] // HD
+    lengths_copy = pltpu.make_async_copy(lengths_hbm, lengths_ref, sems.at[2 + groups])
+    winners_copy = pltpu.make_async_copy(winners_hbm, winners_ref, sems.at[3 + groups])
+    lengths_copy.start()
+    winners_copy.start()
     copies = [pltpu.make_async_copy(k_hbm, k_ref, sems.at[0]), pltpu.make_async_copy(v_hbm, v_ref, sems.at[1])]
     for group in range(groups):
         columns = pl.ds(group * ratio * HD, ratio * HD)
         copies.append(pltpu.make_async_copy(q_hbm.at[:, columns], q_ref.at[:, columns], sems.at[2 + group]))
     for copy in copies:
         copy.start()
+    lengths_copy.wait()
+    winners_copy.wait()
+    facts_ref[...] = gather_facts(lengths_ref, winners_ref)
     copies[0].wait()
     copies[1].wait()
     device = lax.axis_index("cand")
     half = q_ref.shape[0] // 2
     sent = pl.ds(pl.multiple_of((1 - (device & 1)) * half, half), half)
     for group in range(groups):
-        load_span(k_buf.at[group], v_buf.at[group], k_ref, v_ref, group, lengths_ref[device], 0)
+        load_span(k_buf.at[group], v_buf.at[group], k_ref, v_ref, group, valid_of(facts_ref, OWN_VALID), 0)
 
     def score(rows, columns, group):
         if rows.start == 0 and columns.start == group * ratio * HD:
@@ -120,15 +137,16 @@
         piece_ref[...] = q_ref[sent, low * HD : high * HD]
 
 
-def choose_kernel(lengths_ref, winners_ref, own_ref, companion_ref, *out_refs):
-    place = Place(lengths_ref, winners_ref)
-    for won, ref in ((True, own_ref), (False, companion_ref)):
-        @pl.when(place.won == won)
-        def _():
-            start = 0
-            for out_ref in out_refs:
-                out_ref[...] = ref[:, start : start + out_ref.shape[1]]
-                start += out_ref.shape[1]
+def choose_kernel(facts_ref, own_ref, companion_ref, out_ref):
+    won = has_won(facts_ref)
+
+    @pl.when(won)
+    def _():
+        out_ref[...] = own_ref[...]
+
+    @pl.when(jnp.logical_not(won))
+    def _():
+        out_ref[...] = companion_ref[...]
 
 
 def join_work(rows, first_row, columns, valid_rows, q_ref, own_refs, k_buf, v_buf, totals, keep_output):
@@ -155,21 +173,21 @@
     return jnp.sum(output.astype(jnp.float32).reshape(output.shape[0] // 8, 8, LANES), axis=0)
 
 
-def weigh_totals(totals, weight_ref, valid):
+def weigh_totals(totals, weight_ref, facts_ref, index):
+    valid = facts_ref[index : index + 1, :]
     score = jnp.zeros((8, LANES), jnp.float32)
     for columns, total in totals:
         score += total * weight_ref[:, columns]
-    return jnp.full((8, LANES), jnp.sum(score), jnp.float32) / valid.astype(jnp.float32)
+    return jnp.full((8, LANES), jnp.sum(score), jnp.float32) / valid
 
 
 def first_kernel(
-    ratio, block, lengths_ref, weight_ref, q_ref, o_ref, sum_ref, peak_ref, k_ref, v_ref, out_ref, part_ref, k_buf, v_buf
+    ratio, block, facts_ref, weight_ref, q_ref, o_ref, sum_ref, peak_ref, k_ref, v_ref, out_ref, part_ref, k_buf, v_buf
 ):
-    device = lax.axis_index("cand")
     span, heads = q_ref.shape[0], q_ref.shape[1] // HD
-    valid = lengths_ref[device]
+    valid = valid_of(facts_ref, OWN_VALID)
     for group in range(heads // ratio):
-        load_span(k_buf.at[group], v_buf.at[group], k_ref, v_ref, group, lengths_ref[device ^ 1], 0)
+        load_span(k_buf.at[group], v_buf.at[group], k_ref, v_ref, group, valid_of(facts_ref, PARTNER_VALID), 0)
 
     def keep(rows, columns, output):
         out_ref[rows, columns] = output
@@ -185,18 +203,18 @@
                 )
             )
     in_turn(works)
-    part_ref[...] = weigh_totals(totals, weight_ref, valid)
-
-
-def lose_works(place, low, high, ratio, q_ref, k_buf, v_buf, totals, out_ref):
+    part_ref[...] = weigh_totals(totals, weight_ref, facts_ref, OWN_VALID)
+
+
+def lose_works(facts_ref, low, high, ratio, q_ref, k_buf, v_buf, totals, out_ref):
     def score(head):
         return score_rows(q_ref[:, (head - low) * HD : (head - low + 1) * HD], k_buf.at[head // ratio])
 
     def attend(head, scores):
         columns = slice(head * HD, (head + 1) * HD)
         above, below = weigh(scores, peak_of(scores), v_buf.at[head // ratio])
-        first_row = place.bit * q_ref.shape[0]
-        output = finish(above, below, place.partner_valid, first_row, out_ref.dtype)
+        first_row = (lax.axis_index("cand") & 1) * q_ref.shape[0]
+        output = finish(above, below, valid_of(facts_ref, PARTNER_VALID), first_row, out_ref.dtype)
         totals.append((columns, sum_rows(output)))
         out_ref[:, columns] = output
 
@@ -204,20 +222,20 @@
 
 
 def second_kernel(
-    ratio, high, lengths_ref, winners_ref, weight_ref, q_ref, o_ref, sum_ref, peak_ref,
+    ratio, high, facts_ref, weight_ref, q_ref, o_ref, sum_ref, peak_ref,
     ka_ref, va_ref, kb_ref, vb_ref, piece_ref, first_ref, out_ref, part_ref, k_buf, v_buf,
 ):
-    place = Place(lengths_ref, winners_ref)
+    won = has_won(facts_ref)
     half, span, heads = piece_ref.shape[0], q_ref.shape[0], q_ref.shape[1] // HD
 
     def give_part(part):
         row = lax.broadcasted_iota(jnp.int32, part.shape, 0)
         part_ref[...] = jnp.where(row == 0, part, first_ref[...])
 
-    @pl.when(place.won)
+    @pl.when(won)
     def _():
         for group in range(heads // ratio):
-            load_span(k_buf.at[group, :span], v_buf.at[group, :span], kb_ref, vb_ref, group, place.rival_valid, 0)
+            load_span(k_buf.at[group, :span], v_buf.at[group, :span], kb_ref, vb_ref, group, valid_of(facts_ref, RIVAL_VALID), 0)
         works, totals = [], []
 
         def keep(head, output):
@@ -225,33 +243,33 @@
 
         def work(head, start, keep_output):
             return join_work(
-                pl.ds(start, half), start, slice(head * HD, (head + 1) * HD), place.own_valid, q_ref,
+                pl.ds(start, half), start, slice(head * HD, (head + 1) * HD), valid_of(facts_ref, OWN_VALID), q_ref,
                 (o_ref, sum_ref, peak_ref), k_buf.at[head // ratio, :span], v_buf.at[head // ratio, :span], totals,
                 keep_output,
             )
 
-        own_row = pl.multiple_of(place.bit * half, half)
+        own_row = pl.multiple_of((lax.axis_index("cand") & 1) * half, half)
         other_row = pl.multiple_of(half - own_row, half)
         works = [work(head, own_row, functools.partial(keep, head)) for head in range(heads)]
         works += [work(head, other_row, lambda output: None) for head in range(high, heads)]
         in_turn(works)
-        give_part(weigh_totals(totals, weight_ref, place.own_valid))
-
-    @pl.when(jnp.logical_not(place.won))
+        give_part(weigh_totals(totals, weight_ref, facts_ref, OWN_VALID))
+
+    @pl.when(jnp.logical_not(won))
     def _():
         for group in range((high - 1) // ratio + 1):
-            load_span(k_buf.at[group], v_buf.at[group], ka_ref, va_ref, group, place.partner_valid, 0)
-            load_span(k_buf.at[group], v_buf.at[group], kb_ref, vb_ref, group, place.rival_valid, span)
+            load_span(k_buf.at[group], v_buf.at[group], ka_ref, va_ref, group, valid_of(facts_ref, PARTNER_VALID), 0)
+            load_span(k_buf.at[group], v_buf.at[group], kb_ref, vb_ref, group, valid_of(facts_ref, RIVAL_VALID), span)
         totals = []
-        in_turn(lose_works(place, 0, high, ratio, piece_ref, k_buf, v_buf, totals, out_ref))
-        give_part(weigh_totals(totals, weight_ref, place.partner_valid))
+        in_turn(lose_works(facts_ref, 0, high, ratio, piece_ref, k_buf, v_buf, totals, out_ref))
+        give_part(weigh_totals(totals, weight_ref, facts_ref, PARTNER_VALID))
 
 
 def last_kernel(
-    ratio, low, lengths_ref, winners_ref, ka_ref, va_ref, kb_ref, vb_ref, piece_ref, first_ref, second_ref,
+    ratio, low, facts_ref, ka_ref, va_ref, kb_ref, vb_ref, piece_ref, first_ref, second_ref,
     first_out, second_out, k_buf, v_buf, out_buf, sems,
 ):
-    place = Place(lengths_ref, winners_ref)
+    won = has_won(facts_ref)
     heads, span = second_ref.shape[1] // HD, ka_ref.shape[0]
     before, after = pl.ds(0, low * HD), pl.ds(low * HD, (heads - low) * HD)
     first_copy = pltpu.make_async_copy(first_ref, first_out, sems.at[0])
@@ -265,19 +283,19 @@
     first_copy.start()
     before_copy.start()
 
-    @pl.when(place.won)
+    @pl.when(won)
     def _():
         won_copy.start()
         won_copy.wait()
 
-    @pl.when(jnp.logical_not(place.won))
+    @pl.when(jnp.logical_not(won))
     def _():
         for group in range(low // ratio, heads // ratio):
-            load_span(k_buf.at[group], v_buf.at[group], ka_ref, va_ref, group, place.partner_valid, 0)
-            load_span(k_buf.at[group], v_buf.at[group], kb_ref, vb_ref, group, place.rival_valid, span)
+            load_span(k_buf.at[group], v_buf.at[group], ka_ref, va_ref, group, valid_of(facts_ref, PARTNER_VALID), 0)
+            load_span(k_buf.at[group], v_buf.at[group], kb_ref, vb_ref, group, valid_of(facts_ref, RIVAL_VALID), span)
         works = []
         for head, (score, attend) in zip(
-            range(low, heads), lose_works(place, low, heads, ratio, piece_ref, k_buf, v_buf, [], out_buf)
+            range(low, heads), lose_works(facts_ref, low, heads, ratio, piece_ref, k_buf, v_buf, [], out_buf)
         ):
 
             def attend_and_copy(scores, head=head, attend=attend):
@@ -331,47 +349,46 @@
     partial = jax.ShapeDtypeStruct((span, width), jnp.float32)
     *own, sent = kernel_call(
         functools.partial(own_kernel, ratio, block, cuts),
-        (lengths, *[pltpu.with_memory_space_constraint(array, pltpu.HBM) for array in (queries, keys, values)]),
-        [SMEM, HBM, HBM, HBM],
-        (partial,) * 3 + piece_shapes,
-        (VMEM,) * (3 + len(cuts)),
+        [pltpu.with_memory_space_constraint(array, pltpu.HBM) for array in (lengths, winners, queries, keys, values)],
+        [HBM] * 5,
+        (partial,) * 3 + (part_shape,) + piece_shapes,
+        (VMEM,) * (4 + len(cuts)),
         [pltpu.VMEM(array.shape, dtype) for array in (queries, keys, values)]
+        + [pltpu.SMEM(array.shape, array.dtype) for array in (lengths, winners)]
         + buffers(1)
-        + [pltpu.SemaphoreType.DMA((2 + groups,))],
+        + [pltpu.SemaphoreType.DMA((4 + groups,))],
         share * heads,
     )
-    own, sent = own[:3], own[3:] + [sent]
+    own, facts, sent = own[:3], own[3], own[4:] + [sent]
 
     pieces = [from_partner(piece, "cand", 0) for piece in sent]
 
-    def choose(own, companion, parts):
-        shape = jax.ShapeDtypeStruct((span, own.shape[1] // parts), dtype)
-        return kernel_call(
-            choose_kernel, (lengths, winners, own, companion), [SMEM, SMEM, VMEM, VMEM], (shape,) * parts, (VMEM,) * parts
-        )
-
-    chosen_keys = choose(keys, companion_keys, 1)[0]
+    def choose(own, companion):
+        shape = jax.ShapeDtypeStruct(own.shape, dtype)
+        return kernel_call(choose_kernel, (facts, own, companion), [VMEM] * 3, shape, VMEM)
+
+    chosen_keys = choose(keys, companion_keys)
     rival_keys = from_partner(chosen_keys, "cand", 1)
     companion_values, _ = lax.optimization_barrier((companion_values, chosen_keys))
-    rival_values = from_partner(choose(values, companion_values, 1)[0], "cand", 1)
+    rival_values = from_partner(choose(values, companion_values), "cand", 1)
 
     first_shape = jax.ShapeDtypeStruct((span, width), dtype)
     first, first_part = kernel_call(
         functools.partial(first_kernel, ratio, block),
-        (lengths, weight, queries, *own, companion_keys, companion_values),
-        [SMEM] + [VMEM] * 7,
+        (facts, weight, queries, *own, companion_keys, companion_values),
+        [VMEM] * 8,
         (first_shape, part_shape),
         (VMEM, VMEM),
         buffers(1),
-        share * heads // 5,
+        share * heads // 6,
     )
     second, part = kernel_call(
         functools.partial(second_kernel, ratio, middle),
         (
-            lengths, winners, weight, queries, *own, companion_keys, companion_values, rival_keys, rival_values,
+            facts, weight, queries, *own, companion_keys, companion_values, rival_keys, rival_values,
             pieces[0], first_part,
         ),
-        [SMEM] * 2 + [VMEM] * 11,
+        [VMEM] * 12,
         (second_shape, part_shape),
         (VMEM, VMEM),
         buffers(2),
@@ -379,8 +396,8 @@
     )
     first, second = kernel_call(
         functools.partial(last_kernel, ratio, middle),
-        (lengths, winners, companion_keys, companion_values, rival_keys, rival_values, pieces[1], first, second),
-        [SMEM] * 2 + [VMEM] * 7,
+        (facts, companion_keys, companion_values, rival_keys, rival_values, pieces[1], first, second),
+        [VMEM] * 8,
         (first_shape, second_shape),
         (ANY, ANY),
         buffers(2) + [pltpu.VMEM((half, width), dtype), pltpu.SemaphoreType.DMA((3 + LAST_HEADS,))],

time: 35.1 us -> 32.6 us (0.929)
  Pallas kernels: 17.8 us -> 14.8 us
  waiting for transfers between devices: 3.03 us -> 4.08 us
  local copies, waits for them, and re-layouts: 1.2 us -> 0.54 us
    pallas_call x6, Pallas kernels: 17.8 us -> 14.8 us  [kernel_call(): pl.pallas_call(kernel, out_shape=out_shape, in_specs=in_specs, out_specs=...]
    ppermute x8, waiting for transfers between devices: 2.89 us -> 4 us  [from_partner(): lax.ppermute(value, axis, [(i, i ^ 1 << stride) for i in range(lax.axis_s...]
    unnamed x12 -> x8, local copies, waits for them, and re-layouts: 0.67 us -> 0.02 us
  transfers between devices with their start and end apart: 9 -> 9, of which waited for: 4 -> 5; matrix products, arithmetic and copies ran while one was open for 0% -> 0% of each run, Pallas kernels for 52% -> 46%
where the time goes in v4:
time: 32.6 us; the launch traced here: 32.1 us
  Pallas kernels  14.8 us (45%)
  starting transfers between devices  11.8 us (36%)
  waiting for transfers between devices  4.08 us (13%)
  between operations  0.73 us (2%)
  local copies, waits for them, and re-layouts  0.54 us (2%)
    pallas_call x6, Pallas kernels, kernel_call(): pl.pallas_call(kernel, out_shape=out_shape, in_specs=in_specs, out_specs=...  14.8 us
    ppermute x8, starting transfers between devices, from_partner(): lax.ppermute(value, axis, [(i, i ^ 1 << stride) for i in range(lax.axis_s...  11.8 us
    ppermute x8, waiting for transfers between devices, from_partner(): lax.ppermute(value, axis, [(i, i ^ 1 << stride) for i in range(lax.axis_s...  4 us
  transfers between devices with their start and end apart: 9, of which 5 were waited for; matrix products, arithmetic and copies ran while one was open for 0% of the time, Pallas kernels for 46%

profile of v4, /device:TPU:0, one launch (start us, length us, event | category | flops | bytes accessed | tf_op | source)
XLA Modules:
  0.0 32.1 jit_solution(2271224986573709423)
XLA Ops:
  0.7 3.0 %collective-permute-start = (bf16[512,256]{1,0:T(8,128)(2,1)}, bf16[512,256]{1,0:T(8,128)(2,1)S(1)}, u32[]{:S(2)}, u32[]{:S(2)}) collective-permute-start(bf16[512,256]{1,0:T(8,128)(2,1)} %own_ref.2), channel_id=1, source_target_pairs={{0,2},{2,0},{4,6},{6,4},{8,10},{10,8},{12,14},{14,12},{1,3},{3,1},... | collective-permute-start | bytes 786440 | tf_op jit(solution)/shard_map/ppermute | solution.py:24
  3.7 0.1 collective-permute-start.1
  3.8 5.1 %shard_map.93 = (f32[512,1280]{1,0:T(8,128)S(1)}, f32[512,1280]{1,0:T(8,128)S(1)}, f32[512,1280]{1,0:T(8,128)S(1)}, f32[8,128]{1,0:T(8,128)S(1)}, bf16[256,640]{...) custom-call(s32[8]{0:T(128)} %lengths_hbm.1, s32[4]{0:T(128)} %winners_hbm.1, bf16[512,1280]{1,0:T(8,128)(2,1)} %q_ref.3, ...), custom_call_target="tpu_custom_call" | custom-call | flops 13421772800 | bytes 52428800 | tf_op jit(solution)/shard_map/pallas_call | solution.py:315
  8.9 2.0 %collective-permute-start.5 = (bf16[256,640]{1,0:T(8,128)(2,1)S(1)}, bf16[256,640]{1,0:T(8,128)(2,1)S(1)}, u32[]{:S(2)}, u32[]{:S(2)}) collective-permute-start(bf16[256,640]{1,0:T(8,128)(2,1)S(1)} %get-tuple-element.24), channel_id=1, source_target_pairs={{0,2},{2,0},{4,6},{6,4},{8,10},{10,8},{12,14},{14,12},{1,3},{3,1},... | collective-permute-start | bytes 983048 | tf_op jit(solution)/shard_map/ppermute | solution.py:24
  10.9 0.1 collective-permute-start.4
  11.0 0.0 collective-permute-done.companion_ref.k_ref.ka_ref
  11.0 0.1 shard_map.94
  11.2 2.2 %collective-permute-start.2 = (bf16[512,256]{1,0:T(8,128)(2,1)S(1)}, bf16[512,256]{1,0:T(8,128)(2,1)S(1)}, u32[]{:S(2)}, u32[]{:S(2)}) collective-permute-start(bf16[512,256]{1,0:T(8,128)(2,1)S(1)} %shard_map.94), channel_id=1, source_target_pairs={{0,4},{2,6},{4,0},{6,2},{8,12},{10,14},{12,8},{14,10},{1,5},{3,7},... | collective-permute-start | bytes 786440 | tf_op jit(solution)/shard_map/ppermute | solution.py:24
  13.4 3.3 %collective-permute-done.1.companion_ref.v_ref.va_ref = bf16[512,256]{1,0:T(8,128)(2,1)S(1)} collective-permute-done((bf16[512,256]{1,0:T(8,128)(2,1)}, bf16[512,256]{1,0:T(8,128)(2,1)S(1)}, u32[]{:S(2)}, u32[]{:S(2)}) %collective-permute-start.1) | collective-permute-done | bytes 262176 | tf_op jit(solution)/shard_map/ppermute | solution.py:24
  16.6 0.1 shard_map.95
  16.8 2.2 %collective-permute-start.3 = (bf16[512,256]{1,0:T(8,128)(2,1)S(1)}, bf16[512,256]{1,0:T(8,128)(2,1)S(1)}, u32[]{:S(2)}, u32[]{:S(2)}) collective-permute-start(bf16[512,256]{1,0:T(8,128)(2,1)S(1)} %shard_map.95), channel_id=1, source_target_pairs={{0,4},{2,6},{4,0},{6,2},{8,12},{10,14},{12,8},{14,10},{1,5},{3,7},... | collective-permute-start | bytes 786440 | tf_op jit(solution)/shard_map/ppermute | solution.py:24
  19.0 4.4 %shard_map.96 = (bf16[512,1280]{1,0:T(8,128)(2,1)S(1)}, f32[8,128]{1,0:T(8,128)S(1)}) custom-call(f32[8,128]{1,0:T(8,128)S(1)} %get-tuple-element.17.facts_ref, f32[1,1280]{1,0:T(1,128)S(1)} %reshape.11.weight_ref, bf16[512,1280]{1,0:T(8,128)(2,1)S(1)} %copy-done, f32[512,1280]{1,0:T(8,128)S(1)} %get-tuple-element.20.o_ref, ...), custom_call_target="tpu_custom_call" | custom-call | flops 2236962048 | bytes 8738133 | tf_op jit(solution)/shard_map/pallas_call | solution.py:315
  23.5 0.2 collective-permute-done.5.piece_ref
  23.7 0.4 %collective-permute-done.3.vb_ref = bf16[512,256]{1,0:T(8,128)(2,1)S(1)} collective-permute-done((bf16[512,256]{1,0:T(8,128)(2,1)S(1)}, bf16[512,256]{1,0:T(8,128)(2,1)S(1)}, u32[]{:S(2)}, u32[]{:S(2)}) %collective-permute-start.3) | collective-permute-done | bytes 262176 | tf_op jit(solution)/shard_map/ppermute | solution.py:24
  24.0 3.7 %shard_map.97 = (bf16[256,1280]{1,0:T(8,128)(2,1)S(1)}, f32[8,128]{1,0:T(8,128)S(1)}) custom-call(f32[8,128]{1,0:T(8,128)S(1)} %get-tuple-element.17.facts_ref, f32[1,1280]{1,0:T(1,128)S(1)} %reshape.11.weight_ref, bf16[512,1280]{1,0:T(8,128)(2,1)S(1)} %copy-done, f32[512,1280]{1,0:T(8,128)S(1)} %get-tuple-element.20.o_ref, ...), custom_call_target="tpu_custom_call" | custom-call | flops 6710886400 | bytes 26214400 | tf_op jit(solution)/shard_map/pallas_call | solution.py:315
  27.7 0.7 %collective-permute-start.7 = (f32[8,128]{1,0:T(8,128)S(1)}, f32[8,128]{1,0:T(8,128)S(1)}, u32[]{:S(2)}, u32[]{:S(2)}) collective-permute-start(f32[8,128]{1,0:T(8,128)S(1)} %get-tuple-element.29), channel_id=1, source_target_pairs={{0,2},{2,0},{4,6},{6,4},{8,10},{10,8},{12,14},{14,12},{1,3},{3,1},... | collective-permute-start | bytes 12296 | tf_op jit(solution)/shard_map/ppermute | solution.py:24
  28.4 0.0 collective-permute-start.8
  28.4 1.5 %collective-permute-start.6 = (f32[8,128]{1,0:T(8,128)S(1)}, f32[8,128]{1,0:T(8,128)S(1)}, u32[]{:S(2)}, u32[]{:S(2)}) collective-permute-start(f32[8,128]{1,0:T(8,128)S(1)} %get-tuple-element.29), channel_id=1, source_target_pairs={{0,1},{1,0},{2,3},{3,2},{4,5},{5,4},{6,7},{7,6},{8,9},{9,8},{10,11... | collective-permute-start | bytes 12296 | tf_op jit(solution)/shard_map/ppermute | solution.py:24
  29.9 0.0 collective-permute-done.4.piece_ref
  29.9 1.3 %shard_map.98 = (bf16[512,1280]{1,0:T(8,128)(2,1)}, bf16[256,1280]{1,0:T(8,128)(2,1)}) custom-call(f32[8,128]{1,0:T(8,128)S(1)} %get-tuple-element.17.facts_ref, bf16[512,256]{1,0:T(8,128)(2,1)S(1)} %collective-permute-done.companion_ref.k_ref.ka_ref, bf16[512,256]{1,0:T(8,128)(2,1)S(1)} %collective-permute-done.1.companion_ref.v_ref.va_ref, ...), custom_call_target="tpu_custom_call" | custom-call | flops 83886080 | bytes 327680 | tf_op jit(solution)/shard_map/pallas_call | solution.py:315
  31.3 0.1 collective-permute-done.7
  31.4 0.1 collective-permute-done.8
  31.5 0.1 select_add_fusion
  31.6 0.5 %fusion = (f32[1,1]{1,0:T(1,128)}, f32[1,1]{1,0:T(1,128)}) fusion(f32[8,128]{1,0:T(8,128)S(1)} %select_add_fusion), kind=kLoop, calls=%fused_computation.2 | loop fusion | bytes 16 | tf_op jit(solution)/shard_map/slice | solution.py:414
  (12 shorter events, 0.0 us)
Async XLA Ops:
  0.6 10.4 %copy-start.1 = (bf16[512,256]{1,0:T(8,128)(2,1)S(1)}, bf16[512,256]{1,0:T(8,128)(2,1)}, u32[]{:S(2)}) copy-start(bf16[512,256]{1,0:T(8,128)(2,1)} %own_ref.2) | copy-start | bytes 786436
  0.6 16.0 %copy-start.2 = (bf16[512,256]{1,0:T(8,128)(2,1)S(1)}, bf16[512,256]{1,0:T(8,128)(2,1)}, u32[]{:S(2)}) copy-start(bf16[512,256]{1,0:T(8,128)(2,1)} %own_ref.3) | copy-start | bytes 786436
  0.7 18.4 %copy-start = (bf16[512,1280]{1,0:T(8,128)(2,1)S(1)}, bf16[512,1280]{1,0:T(8,128)(2,1)}, u32[]{:S(2)}) copy-start(bf16[512,1280]{1,0:T(8,128)(2,1)} %q_ref.3) | copy-start | bytes 3932164
  0.7 18.3 %copy-start.3 = (f32[1280]{0:T(1024)S(1)}, f32[1280]{0:T(1024)}, u32[]{:S(2)}) copy-start(f32[1280]{0:T(1024)} %param.11) | copy-start | bytes 15364
  0.7 10.3 %collective-permute-start = (bf16[512,256]{1,0:T(8,128)(2,1)}, bf16[512,256]{1,0:T(8,128)(2,1)S(1)}, u32[]{:S(2)}, u32[]{:S(2)}) collective-permute-start(bf16[512,256]{1,0:T(8,128)(2,1)} %own_ref.2), channel_id=1, source_target_pairs={{0,2},{2,0},{4,6},{6,4},{8,10},{10,8},{12,14},{14,12},{1,3},{3,1},... | collective-permute-start | bytes 786440 | tf_op jit(solution)/shard_map/ppermute | solution.py:24
  3.7 13.0 %collective-permute-start.1 = (bf16[512,256]{1,0:T(8,128)(2,1)}, bf16[512,256]{1,0:T(8,128)(2,1)S(1)}, u32[]{:S(2)}, u32[]{:S(2)}) collective-permute-start(bf16[512,256]{1,0:T(8,128)(2,1)} %own_ref.3), channel_id=1, source_target_pairs={{0,2},{2,0},{4,6},{6,4},{8,10},{10,8},{12,14},{14,12},{1,3},{3,1},... | collective-permute-start | bytes 786440 | tf_op jit(solution)/shard_map/ppermute | solution.py:24
  8.9 14.8 %collective-permute-start.5 = (bf16[256,640]{1,0:T(8,128)(2,1)S(1)}, bf16[256,640]{1,0:T(8,128)(2,1)S(1)}, u32[]{:S(2)}, u32[]{:S(2)}) collective-permute-start(bf16[256,640]{1,0:T(8,128)(2,1)S(1)} %get-tuple-element.24), channel_id=1, source_target_pairs={{0,2},{2,0},{4,6},{6,4},{8,10},{10,8},{12,14},{14,12},{1,3},{3,1},... | collective-permute-start | bytes 983048 | tf_op jit(solution)/shard_map/ppermute | solution.py:24
  10.9 19.0 %collective-permute-start.4 = (bf16[256,640]{1,0:T(8,128)(2,1)S(1)}, bf16[256,640]{1,0:T(8,128)(2,1)S(1)}, u32[]{:S(2)}, u32[]{:S(2)}) collective-permute-start(bf16[256,640]{1,0:T(8,128)(2,1)S(1)} %get-tuple-element.19), channel_id=1, source_target_pairs={{0,2},{2,0},{4,6},{6,4},{8,10},{10,8},{12,14},{14,12},{1,3},{3,1},... | collective-permute-start | bytes 983048 | tf_op jit(solution)/shard_map/ppermute | solution.py:24
  11.2 12.5 %collective-permute-start.2 = (bf16[512,256]{1,0:T(8,128)(2,1)S(1)}, bf16[512,256]{1,0:T(8,128)(2,1)S(1)}, u32[]{:S(2)}, u32[]{:S(2)}) collective-permute-start(bf16[512,256]{1,0:T(8,128)(2,1)S(1)} %shard_map.94), channel_id=1, source_target_pairs={{0,4},{2,6},{4,0},{6,2},{8,12},{10,14},{12,8},{14,10},{1,5},{3,7},... | collective-permute-start | bytes 786440 | tf_op jit(solution)/shard_map/ppermute | solution.py:24
  16.8 7.2 %collective-permute-start.3 = (bf16[512,256]{1,0:T(8,128)(2,1)S(1)}, bf16[512,256]{1,0:T(8,128)(2,1)S(1)}, u32[]{:S(2)}, u32[]{:S(2)}) collective-permute-start(bf16[512,256]{1,0:T(8,128)(2,1)S(1)} %shard_map.95), channel_id=1, source_target_pairs={{0,4},{2,6},{4,0},{6,2},{8,12},{10,14},{12,8},{14,10},{1,5},{3,7},... | collective-permute-start | bytes 786440 | tf_op jit(solution)/shard_map/ppermute | solution.py:24
  27.7 3.7 %collective-permute-start.7 = (f32[8,128]{1,0:T(8,128)S(1)}, f32[8,128]{1,0:T(8,128)S(1)}, u32[]{:S(2)}, u32[]{:S(2)}) collective-permute-start(f32[8,128]{1,0:T(8,128)S(1)} %get-tuple-element.29), channel_id=1, source_target_pairs={{0,2},{2,0},{4,6},{6,4},{8,10},{10,8},{12,14},{14,12},{1,3},{3,1},... | collective-permute-start | bytes 12296 | tf_op jit(solution)/shard_map/ppermute | solution.py:24
  28.4 3.1 %collective-permute-start.8 = (f32[8,128]{1,0:T(8,128)S(1)}, f32[8,128]{1,0:T(8,128)S(1)}, u32[]{:S(2)}, u32[]{:S(2)}) collective-permute-start(f32[8,128]{1,0:T(8,128)S(1)} %get-tuple-element.29), channel_id=1, source_target_pairs={{0,3},{1,2},{2,1},{3,0},{4,7},{5,6},{6,5},{7,4},{8,11},{9,10},{10,... | collective-permute-start | bytes 12296 | tf_op jit(solution)/shard_map/ppermute | solution.py:411
  28.4 3.1 %collective-permute-start.6 = (f32[8,128]{1,0:T(8,128)S(1)}, f32[8,128]{1,0:T(8,128)S(1)}, u32[]{:S(2)}, u32[]{:S(2)}) collective-permute-start(f32[8,128]{1,0:T(8,128)S(1)} %get-tuple-element.29), channel_id=1, source_target_pairs={{0,1},{1,0},{2,3},{3,2},{4,5},{5,4},{6,7},{7,6},{8,9},{9,8},{10,11... | collective-permute-start | bytes 12296 | tf_op jit(solution)/shard_map/ppermute | solution.py:24

commit v5 on v4

--- a/solution.py
+++ b/solution.py
@@ -13,6 +13,7 @@
 FACTOR = HD ** (-0.5) * LOG2E
 BARRED = -1e30
 LAST_HEADS = 5
+TAIL_HEADS = 3
 COST = 10
 VMEM_LIMIT = 12 * 1024 * 1024
 ANY = pl.BlockSpec(memory_space=pl.ANY)
@@ -206,37 +207,54 @@
     part_ref[...] = weigh_totals(totals, weight_ref, facts_ref, OWN_VALID)
 
 
-def lose_works(facts_ref, low, high, ratio, q_ref, k_buf, v_buf, totals, out_ref):
-    def score(head):
-        return score_rows(q_ref[:, (head - low) * HD : (head - low + 1) * HD], k_buf.at[head // ratio])
-
-    def attend(head, scores):
-        columns = slice(head * HD, (head + 1) * HD)
-        above, below = weigh(scores, peak_of(scores), v_buf.at[head // ratio])
-        first_row = (lax.axis_index("cand") & 1) * q_ref.shape[0]
-        output = finish(above, below, valid_of(facts_ref, PARTNER_VALID), first_row, out_ref.dtype)
-        totals.append((columns, sum_rows(output)))
-        out_ref[:, columns] = output
-
-    return [(functools.partial(score, head), functools.partial(attend, head)) for head in range(low, high)]
-
-
-def second_kernel(
-    ratio, high, facts_ref, weight_ref, q_ref, o_ref, sum_ref, peak_ref,
-    ka_ref, va_ref, kb_ref, vb_ref, piece_ref, first_ref, out_ref, part_ref, k_buf, v_buf,
+def lose_works(facts_ref, low, high, ratio, q_ref, k_buf, v_buf, totals, out_ref, then=None):
+    half, span = q_ref.shape[0], k_buf.shape[1] // 2
+    chunks, head = [], low
+    while head < high:
+        after = min(head + 2, high, (head // ratio + 1) * ratio)
+        chunks.append(range(head, after))
+        head = after
+
+    def score(chunk):
+        rows = jnp.concatenate([q_ref[:, (head - low) * HD : (head - low + 1) * HD] for head in chunk], axis=0)
+        k_wide = k_buf.at[chunk[0] // ratio]
+        return [score_rows(rows, k_wide.at[start : start + span]) for start in (0, span)]
+
+    def attend(chunk, scores):
+        v_wide = v_buf.at[chunk[0] // ratio]
+        peak = jnp.maximum(*(jnp.max(each, axis=1, keepdims=True) for each in scores))
+        both = 0.0
+        for each, start in zip(scores, (0, span)):
+            exps = jnp.exp2((each - peak) * FACTOR).astype(v_wide.dtype)
+            both += jnp.dot(exps, v_wide[start : start + span], preferred_element_type=jnp.float32)
+        first_row = (lax.axis_index("cand") & 1) * half
+        for index, head in enumerate(chunk):
+            columns = slice(head * HD, (head + 1) * HD)
+            rows = both[index * half : (index + 1) * half]
+            output = finish(rows[:, :HD], rows[:, HD:], valid_of(facts_ref, PARTNER_VALID), first_row, out_ref.dtype)
+            totals.append((columns, sum_rows(output)))
+            out_ref[:, columns] = output
+            if then is not None:
+                then(head)
+
+    return [(functools.partial(score, chunk), functools.partial(attend, chunk)) for chunk in chunks]
+
+
+def give_part(part_ref, part, first_ref):
+    row = lax.broadcasted_iota(jnp.int32, part.shape, 0)
+    part_ref[...] = jnp.where(row == 0, part, first_ref[...])
+
+
+def win_kernel(
+    ratio, low, facts_ref, weight_ref, q_ref, o_ref, sum_ref, peak_ref, k_ref, v_ref, first_ref, out_ref, part_ref, k_buf, v_buf
 ):
-    won = has_won(facts_ref)
-    half, span, heads = piece_ref.shape[0], q_ref.shape[0], q_ref.shape[1] // HD
-
-    def give_part(part):
-        row = lax.broadcasted_iota(jnp.int32, part.shape, 0)
-        part_ref[...] = jnp.where(row == 0, part, first_ref[...])
-
-    @pl.when(won)
+    half, heads = out_ref.shape[0], q_ref.shape[1] // HD
+
+    @pl.when(has_won(facts_ref))
     def _():
         for group in range(heads // ratio):
-            load_span(k_buf.at[group, :span], v_buf.at[group, :span], kb_ref, vb_ref, group, valid_of(facts_ref, RIVAL_VALID), 0)
-        works, totals = [], []
+            load_span(k_buf.at[group], v_buf.at[group], k_ref, v_ref, group, valid_of(facts_ref, RIVAL_VALID), 0)
+        totals = []
 
         def keep(head, output):
             out_ref[:, head * HD : (head + 1) * HD] = output
@@ -244,33 +262,39 @@
         def work(head, start, keep_output):
             return join_work(
                 pl.ds(start, half), start, slice(head * HD, (head + 1) * HD), valid_of(facts_ref, OWN_VALID), q_ref,
-                (o_ref, sum_ref, peak_ref), k_buf.at[head // ratio, :span], v_buf.at[head // ratio, :span], totals,
-                keep_output,
+                (o_ref, sum_ref, peak_ref), k_buf.at[head // ratio], v_buf.at[head // ratio], totals, keep_output,
             )
 
         own_row = pl.multiple_of((lax.axis_index("cand") & 1) * half, half)
         other_row = pl.multiple_of(half - own_row, half)
         works = [work(head, own_row, functools.partial(keep, head)) for head in range(heads)]
-        works += [work(head, other_row, lambda output: None) for head in range(high, heads)]
+        works += [work(head, other_row, lambda output: None) for head in range(low, heads)]
         in_turn(works)
-        give_part(weigh_totals(totals, weight_ref, facts_ref, OWN_VALID))
-
-    @pl.when(jnp.logical_not(won))
-    def _():
-        for group in range((high - 1) // ratio + 1):
-            load_span(k_buf.at[group], v_buf.at[group], ka_ref, va_ref, group, valid_of(facts_ref, PARTNER_VALID), 0)
-            load_span(k_buf.at[group], v_buf.at[group], kb_ref, vb_ref, group, valid_of(facts_ref, RIVAL_VALID), span)
+        give_part(part_ref, weigh_totals(totals, weight_ref, facts_ref, OWN_VALID), first_ref)
+
+
+def lose_kernel(
+    ratio, high, facts_ref, weight_ref, ka_ref, va_ref, kb_ref, vb_ref, piece_ref, first_ref, second_ref, won_part_ref,
+    out_ref, part_ref, k_wide, v_wide,
+):
+    span = ka_ref.shape[0]
+
+    @pl.when(jnp.logical_not(has_won(facts_ref)))
+    def _():
+        for group in range(k_wide.shape[0]):
+            own_k, own_v = k_wide.at[group], v_wide.at[group]
+            load_span(own_k, own_v, ka_ref, va_ref, group, valid_of(facts_ref, PARTNER_VALID), 0)
+            load_span(own_k, own_v, kb_ref, vb_ref, group, valid_of(facts_ref, RIVAL_VALID), span)
         totals = []
-        in_turn(lose_works(facts_ref, 0, high, ratio, piece_ref, k_buf, v_buf, totals, out_ref))
-        give_part(weigh_totals(totals, weight_ref, facts_ref, PARTNER_VALID))
+        in_turn(lose_works(facts_ref, 0, high, ratio, piece_ref, k_wide, v_wide, totals, out_ref))
+        give_part(part_ref, weigh_totals(totals, weight_ref, facts_ref, PARTNER_VALID), first_ref)
 
 
 def last_kernel(
-    ratio, low, facts_ref, ka_ref, va_ref, kb_ref, vb_ref, piece_ref, first_ref, second_ref,
-    first_out, second_out, k_buf, v_buf, out_buf, sems,
+    ratio, low, facts_ref, k_wide, v_wide, piece_ref, first_ref, second_ref, first_out, second_out, out_ref, sems
 ):
     won = has_won(facts_ref)
-    heads, span = second_ref.shape[1] // HD, ka_ref.shape[0]
+    heads = second_ref.shape[1] // HD
     before, after = pl.ds(0, low * HD), pl.ds(low * HD, (heads - low) * HD)
     first_copy = pltpu.make_async_copy(first_ref, first_out, sems.at[0])
     before_copy = pltpu.make_async_copy(second_ref.at[:, before], second_out.at[:, before], sems.at[1])
@@ -278,7 +302,7 @@
 
     def lost_copy(head):
         columns = pl.ds(head * HD, HD)
-        return pltpu.make_async_copy(out_buf.at[:, columns], second_out.at[:, columns], sems.at[3 + head - low])
+        return pltpu.make_async_copy(out_ref.at[:, columns], second_out.at[:, columns], sems.at[3 + head - low])
 
     first_copy.start()
     before_copy.start()
@@ -290,25 +314,46 @@
 
     @pl.when(jnp.logical_not(won))
     def _():
-        for group in range(low // ratio, heads // ratio):
-            load_span(k_buf.at[group], v_buf.at[group], ka_ref, va_ref, group, valid_of(facts_ref, PARTNER_VALID), 0)
-            load_span(k_buf.at[group], v_buf.at[group], kb_ref, vb_ref, group, valid_of(facts_ref, RIVAL_VALID), span)
-        works = []
-        for head, (score, attend) in zip(
-            range(low, heads), lose_works(facts_ref, low, heads, ratio, piece_ref, k_buf, v_buf, [], out_buf)
-        ):
-
-            def attend_and_copy(scores, head=head, attend=attend):
-                attend(scores)
+        def copy_out(head):
+            if head < heads - TAIL_HEADS:
                 lost_copy(head).start()
 
-            works.append((score, attend_and_copy))
-        in_turn(works)
-        for head in range(low, heads):
+        in_turn(lose_works(facts_ref, low, heads, ratio, piece_ref, k_wide, v_wide, [], out_ref, copy_out))
+        for head in range(low, heads - TAIL_HEADS):
             lost_copy(head).wait()
 
     first_copy.wait()
     before_copy.wait()
+
+
+def final_kernel(
+    facts_ref, part_ref, beside_ref, across_ref, diagonal_ref, lost_ref, _, second_out, first_score, final_score,
+    first_buf, final_buf, sems,
+):
+    won = has_won(facts_ref)
+    width = TAIL_HEADS * HD
+    columns = pl.ds(second_out.shape[1] - width, width)
+    tail_copy = pltpu.make_async_copy(lost_ref.at[:, columns], second_out.at[:, columns], sems.at[2])
+
+    @pl.when(jnp.logical_not(won))
+    def _():
+        tail_copy.start()
+
+    beside = part_ref[...] + beside_ref[...]
+    total = beside + (across_ref[...] + diagonal_ref[...])
+    score_copies = []
+    scores = ((beside[1:2, :], first_buf, first_score), (total[0:1, :], final_buf, final_score))
+    for index, (score, buf, out) in enumerate(scores):
+        buf[0] = jnp.max(score)
+        copy = pltpu.make_async_copy(buf, out, sems.at[index])
+        copy.start()
+        score_copies.append(copy)
+    for copy in score_copies:
+        copy.wait()
+
+    @pl.when(jnp.logical_not(won))
+    def _():
+        tail_copy.wait()
 
 
 def kernel_call(kernel, operands, in_specs, out_shape, out_specs, scratch=(), flops=0, aliases=None):
@@ -380,38 +425,55 @@
         (first_shape, part_shape),
         (VMEM, VMEM),
         buffers(1),
-        share * heads // 6,
+        share * heads // 2,
     )
     second, part = kernel_call(
-        functools.partial(second_kernel, ratio, middle),
-        (
-            facts, weight, queries, *own, companion_keys, companion_values, rival_keys, rival_values,
-            pieces[0], first_part,
-        ),
-        [VMEM] * 12,
+        functools.partial(win_kernel, ratio, middle),
+        (facts, weight, queries, *own, rival_keys, rival_values, first_part),
+        [VMEM] * 9,
         (second_shape, part_shape),
         (VMEM, VMEM),
-        buffers(2),
+        buffers(1),
         share * middle,
     )
-    first, second = kernel_call(
+    wide_shape = jax.ShapeDtypeStruct((groups, 2 * span, HD + LANES), dtype)
+    second, part, *wide = kernel_call(
+        functools.partial(lose_kernel, ratio, middle),
+        (facts, weight, companion_keys, companion_values, rival_keys, rival_values, pieces[0], first_part, second, part),
+        [VMEM] * 10,
+        (second_shape, part_shape, wide_shape, wide_shape),
+        (VMEM,) * 4,
+        (),
+        share * middle,
+        {8: 0, 9: 1},
+    )
+    first, second, lost = kernel_call(
         functools.partial(last_kernel, ratio, middle),
-        (facts, companion_keys, companion_values, rival_keys, rival_values, pieces[1], first, second),
-        [VMEM] * 8,
-        (first_shape, second_shape),
-        (ANY, ANY),
-        buffers(2) + [pltpu.VMEM((half, width), dtype), pltpu.SemaphoreType.DMA((3 + LAST_HEADS,))],
+        (facts, *wide, pieces[1], first, second),
+        [VMEM] * 6,
+        (first_shape, second_shape, second_shape),
+        (ANY, ANY, VMEM),
+        [pltpu.SemaphoreType.DMA((3 + LAST_HEADS,))],
         share // 16,
     )
 
     cores = lax.axis_size("head")
     devices = lax.axis_size("cand") * cores
     diagonal = [(i, i ^ (cores + 1)) for i in range(devices)]
+    across = from_partner(part, "cand", 0)
+    across_beside = lax.ppermute(part, ("cand", "head"), diagonal)
     beside = from_partner(part, "head", 0)
-    across = from_partner(part, "cand", 0) + lax.ppermute(part, ("cand", "head"), diagonal)
-    row = lax.broadcasted_iota(jnp.int32, part.shape, 0)
-    sums = lax.optimization_barrier(part + beside + jnp.where(row == 0, across, 0.0))
-    final_round_score, first_score = sums[0, :1], sums[1, :1]
+    score_shape = jax.ShapeDtypeStruct((1,), jnp.float32)
+    second, first_score, final_round_score = kernel_call(
+        final_kernel,
+        (facts, part, beside, across, across_beside, lost, second),
+        [VMEM] * 6 + [ANY],
+        (second_shape, score_shape, score_shape),
+        (ANY, ANY, ANY),
+        [pltpu.SMEM((1,), jnp.float32)] * 2 + [pltpu.SemaphoreType.DMA((3,))],
+        share // 16,
+        {6: 0},
+    )
     return first, second, first_score, final_round_score
 
 

time: 32.6 us -> 33 us (1.012)
  waiting for transfers between devices: 4.08 us -> 4.62 us
  local copies, waits for them, and re-layouts: 0.54 us -> 0.02 us
  Pallas kernels: 14.8 us -> 15.3 us
    ppermute x8, waiting for transfers between devices: 4 us -> 4.62 us  [from_partner(): lax.ppermute(value, axis, [(i, i ^ 1 << stride) for i in range(lax.axis_s...]
    slice x1 -> x0, local copies, waits for them, and re-layouts: 0.52 us -> none  [body(): final_round_score, first_score = (sums[0, :1], sums[1, :1])]
    pallas_call x6 -> x8, Pallas kernels: 14.8 us -> 15.3 us  [kernel_call(): pl.pallas_call(kernel, out_shape=out_shape, in_specs=in_specs, out_specs=...]
    ppermute x8, starting transfers between devices: 11.8 us -> 11.4 us  [from_partner(): lax.ppermute(value, axis, [(i, i ^ 1 << stride) for i in range(lax.axis_s...]
  transfers between devices with their start and end apart: 9 -> 9, of which waited for: 5 -> 4; matrix products, arithmetic and copies ran while one was open for 0% -> 0% of each run, Pallas kernels for 46% -> 45%
where the time goes in v5:
time: 33 us; the launch traced here: 32.3 us
  Pallas kernels  15.3 us (46%)
  starting transfers between devices  11.5 us (35%)
  waiting for transfers between devices  4.62 us (14%)
  between operations  0.91 us (3%)
    pallas_call x8, Pallas kernels, kernel_call(): pl.pallas_call(kernel, out_shape=out_shape, in_specs=in_specs, out_specs=...  15.3 us
    ppermute x8, starting transfers between devices, from_partner(): lax.ppermute(value, axis, [(i, i ^ 1 << stride) for i in range(lax.axis_s...  11.4 us
    ppermute x8, waiting for transfers between devices, from_partner(): lax.ppermute(value, axis, [(i, i ^ 1 << stride) for i in range(lax.axis_s...  4.62 us
  transfers between devices with their start and end apart: 9, of which 4 were waited for; matrix products, arithmetic and copies ran while one was open for 0% of the time, Pallas kernels for 45%

profile of v5, /device:TPU:0, one launch (start us, length us, event | category | flops | bytes accessed | tf_op | source)
XLA Modules:
  0.0 32.3 jit_solution(9506921112321621917)
XLA Ops:
  0.7 3.0 %collective-permute-start = (bf16[512,256]{1,0:T(8,128)(2,1)}, bf16[512,256]{1,0:T(8,128)(2,1)S(1)}, u32[]{:S(2)}, u32[]{:S(2)}) collective-permute-start(bf16[512,256]{1,0:T(8,128)(2,1)} %own_ref.2), channel_id=1, source_target_pairs={{0,2},{2,0},{4,6},{6,4},{8,10},{10,8},{12,14},{14,12},{1,3},{3,1},... | collective-permute-start | bytes 786440 | tf_op jit(solution)/shard_map/ppermute | solution.py:25
  3.7 0.1 collective-permute-start.1
  3.8 5.1 %shard_map.93 = (f32[512,1280]{1,0:T(8,128)S(1)}, f32[512,1280]{1,0:T(8,128)S(1)}, f32[512,1280]{1,0:T(8,128)S(1)}, f32[8,128]{1,0:T(8,128)S(1)}, bf16[256,640]{...) custom-call(s32[8]{0:T(128)} %lengths_hbm.1, s32[4]{0:T(128)} %winners_hbm.1, bf16[512,1280]{1,0:T(8,128)(2,1)} %q_ref.3, ...), custom_call_target="tpu_custom_call" | custom-call | flops 13421772800 | bytes 52428800 | tf_op jit(solution)/shard_map/pallas_call | solution.py:360
  8.9 2.0 %collective-permute-start.4 = (bf16[256,640]{1,0:T(8,128)(2,1)S(1)}, bf16[256,640]{1,0:T(8,128)(2,1)S(1)}, u32[]{:S(2)}, u32[]{:S(2)}) collective-permute-start(bf16[256,640]{1,0:T(8,128)(2,1)S(1)} %get-tuple-element.27), channel_id=1, source_target_pairs={{0,2},{2,0},{4,6},{6,4},{8,10},{10,8},{12,14},{14,12},{1,3},{3,1},... | collective-permute-start | bytes 983048 | tf_op jit(solution)/shard_map/ppermute | solution.py:25
  10.9 0.1 collective-permute-start.5
  11.0 0.0 collective-permute-done.companion_ref.k_ref.ka_ref
  11.0 0.1 shard_map.94
  11.2 2.2 %collective-permute-start.2 = (bf16[512,256]{1,0:T(8,128)(2,1)S(1)}, bf16[512,256]{1,0:T(8,128)(2,1)S(1)}, u32[]{:S(2)}, u32[]{:S(2)}) collective-permute-start(bf16[512,256]{1,0:T(8,128)(2,1)S(1)} %shard_map.94), channel_id=1, source_target_pairs={{0,4},{2,6},{4,0},{6,2},{8,12},{10,14},{12,8},{14,10},{1,5},{3,7},... | collective-permute-start | bytes 786440 | tf_op jit(solution)/shard_map/ppermute | solution.py:25
  13.4 3.3 %collective-permute-done.1.companion_ref.v_ref.va_ref = bf16[512,256]{1,0:T(8,128)(2,1)S(1)} collective-permute-done((bf16[512,256]{1,0:T(8,128)(2,1)}, bf16[512,256]{1,0:T(8,128)(2,1)S(1)}, u32[]{:S(2)}, u32[]{:S(2)}) %collective-permute-start.1) | collective-permute-done | bytes 262176 | tf_op jit(solution)/shard_map/ppermute | solution.py:25
  16.6 0.1 shard_map.95
  16.8 2.2 %collective-permute-start.3 = (bf16[512,256]{1,0:T(8,128)(2,1)S(1)}, bf16[512,256]{1,0:T(8,128)(2,1)S(1)}, u32[]{:S(2)}, u32[]{:S(2)}) collective-permute-start(bf16[512,256]{1,0:T(8,128)(2,1)S(1)} %shard_map.95), channel_id=1, source_target_pairs={{0,4},{2,6},{4,0},{6,2},{8,12},{10,14},{12,8},{14,10},{1,5},{3,7},... | collective-permute-start | bytes 786440 | tf_op jit(solution)/shard_map/ppermute | solution.py:25
  19.0 4.2 %shard_map.96 = (bf16[512,1280]{1,0:T(8,128)(2,1)S(1)}, f32[8,128]{1,0:T(8,128)S(1)}) custom-call(f32[8,128]{1,0:T(8,128)S(1)} %get-tuple-element.25.facts_ref, f32[1,1280]{1,0:T(1,128)S(1)} %reshape.11.weight_ref, bf16[512,1280]{1,0:T(8,128)(2,1)S(1)} %copy-done.2, f32[512,1280]{1,0:T(8,128)S(1)} %get-tuple-element.28.o_ref, ...), custom_call_target="tpu_custom_call" | custom-call | flops 6710886400 | bytes 26214400 | tf_op jit(solution)/shard_map/pallas_call | solution.py:360
  23.2 0.8 %collective-permute-done.3.v_ref.vb_ref = bf16[512,256]{1,0:T(8,128)(2,1)S(1)} collective-permute-done((bf16[512,256]{1,0:T(8,128)(2,1)S(1)}, bf16[512,256]{1,0:T(8,128)(2,1)S(1)}, u32[]{:S(2)}, u32[]{:S(2)}) %collective-permute-start.3) | collective-permute-done | bytes 262176 | tf_op jit(solution)/shard_map/ppermute | solution.py:25
  24.0 0.0 collective-permute-done.2.k_ref.kb_ref
  24.0 3.4 %shard_map.97 = (bf16[256,1280]{1,0:T(8,128)(2,1)S(1)}, f32[8,128]{1,0:T(8,128)S(1)}) custom-call(f32[8,128]{1,0:T(8,128)S(1)} %get-tuple-element.25.facts_ref, f32[1,1280]{1,0:T(1,128)S(1)} %reshape.11.weight_ref, bf16[512,1280]{1,0:T(8,128)(2,1)S(1)} %copy-done.2, f32[512,1280]{1,0:T(8,128)S(1)} %get-tuple-element.28.o_ref, ...), custom_call_target="tpu_custom_call" | custom-call | flops 6710886400 | bytes 26214400 | tf_op jit(solution)/shard_map/pallas_call | solution.py:360
  27.4 0.3 shard_map.98
  27.7 0.1 collective-permute-start.8
  27.8 0.8 %collective-permute-start.7 = (f32[8,128]{1,0:T(8,128)S(1)}, f32[8,128]{1,0:T(8,128)S(1)}, u32[]{:S(2)}, u32[]{:S(2)}) collective-permute-start(f32[8,128]{1,0:T(8,128)S(1)} %get-tuple-element.40.part_ref), channel_id=1, source_target_pairs={{0,2},{2,0},{4,6},{6,4},{8,10},{10,8},{12,14},{14,12},{1,3},{3,1},... | collective-permute-start | bytes 12296 | tf_op jit(solution)/shard_map/ppermute | solution.py:25
  28.6 1.1 %collective-permute-start.6 = (f32[8,128]{1,0:T(8,128)S(1)}, f32[8,128]{1,0:T(8,128)S(1)}, u32[]{:S(2)}, u32[]{:S(2)}) collective-permute-start(f32[8,128]{1,0:T(8,128)S(1)} %get-tuple-element.40.part_ref), channel_id=1, source_target_pairs={{0,1},{1,0},{2,3},{3,2},{4,5},{5,4},{6,7},{7,6},{8,9},{9,8},{10,11... | collective-permute-start | bytes 12296 | tf_op jit(solution)/shard_map/ppermute | solution.py:25
  29.7 0.2 collective-permute-done.5.piece_ref
  29.9 1.3 %shard_map.99 = (bf16[512,1280]{1,0:T(8,128)(2,1)}, bf16[256,1280]{1,0:T(8,128)(2,1)}, bf16[256,1280]{1,0:T(8,128)(2,1)S(1)}) custom-call(f32[8,128]{1,0:T(8,128)S(1)} %get-tuple-element.25.facts_ref, bf16[2,1024,256]{2,1,0:T(8,128)(2,1)S(1)} %get-tuple-element.34.k_wide, bf16[2,1024,256]{2,1,0:T(8,128)(2,1)S(1)} %get-tuple-element.35.v_wide, ...), custom_call_target="tpu_custom_call" | custom-call | flops 83886080 | bytes 327680 | tf_op jit(solution)/shard_map/pallas_call | solution.py:360
  31.2 0.0 collective-permute-done.8.diagonal_ref
  31.2 0.3 collective-permute-done.7.across_ref
  31.5 0.7 %shard_map.100 = (bf16[256,1280]{1,0:T(8,128)(2,1)}, f32[1]{0:T(128)}, f32[1]{0:T(128)}) custom-call(f32[8,128]{1,0:T(8,128)S(1)} %get-tuple-element.25.facts_ref, f32[8,128]{1,0:T(8,128)S(1)} %get-tuple-element.40.part_ref, f32[8,128]{1,0:T(8,128)S(1)} %collective-permute-done.6.beside_ref, ...), custom_call_target="tpu_custom_call", output_to_operand_aliasing={{0}: (6, {})} | custom-call | flops 83886080 | bytes 327680 | tf_op jit(solution)/shard_map/pallas_call | solution.py:360
  (11 shorter events, 0.0 us)
Async XLA Ops:
  0.6 10.4 %copy-start = (bf16[512,256]{1,0:T(8,128)(2,1)S(1)}, bf16[512,256]{1,0:T(8,128)(2,1)}, u32[]{:S(2)}) copy-start(bf16[512,256]{1,0:T(8,128)(2,1)} %own_ref.2) | copy-start | bytes 786436
  0.6 16.0 %copy-start.1 = (bf16[512,256]{1,0:T(8,128)(2,1)S(1)}, bf16[512,256]{1,0:T(8,128)(2,1)}, u32[]{:S(2)}) copy-start(bf16[512,256]{1,0:T(8,128)(2,1)} %own_ref.3) | copy-start | bytes 786436
  0.7 18.3 %copy-start.2 = (bf16[512,1280]{1,0:T(8,128)(2,1)S(1)}, bf16[512,1280]{1,0:T(8,128)(2,1)}, u32[]{:S(2)}) copy-start(bf16[512,1280]{1,0:T(8,128)(2,1)} %q_ref.3) | copy-start | bytes 3932164
  0.7 10.3 %copy-start.3 = (f32[1280]{0:T(1024)S(1)}, f32[1280]{0:T(1024)}, u32[]{:S(2)}) copy-start(f32[1280]{0:T(1024)} %param.11) | copy-start | bytes 15364
  0.7 10.3 %collective-permute-start = (bf16[512,256]{1,0:T(8,128)(2,1)}, bf16[512,256]{1,0:T(8,128)(2,1)S(1)}, u32[]{:S(2)}, u32[]{:S(2)}) collective-permute-start(bf16[512,256]{1,0:T(8,128)(2,1)} %own_ref.2), channel_id=1, source_target_pairs={{0,2},{2,0},{4,6},{6,4},{8,10},{10,8},{12,14},{14,12},{1,3},{3,1},... | collective-permute-start | bytes 786440 | tf_op jit(solution)/shard_map/ppermute | solution.py:25
  3.7 13.0 %collective-permute-start.1 = (bf16[512,256]{1,0:T(8,128)(2,1)}, bf16[512,256]{1,0:T(8,128)(2,1)S(1)}, u32[]{:S(2)}, u32[]{:S(2)}) collective-permute-start(bf16[512,256]{1,0:T(8,128)(2,1)} %own_ref.3), channel_id=1, source_target_pairs={{0,2},{2,0},{4,6},{6,4},{8,10},{10,8},{12,14},{14,12},{1,3},{3,1},... | collective-permute-start | bytes 786440 | tf_op jit(solution)/shard_map/ppermute | solution.py:25
  8.9 18.5 %collective-permute-start.4 = (bf16[256,640]{1,0:T(8,128)(2,1)S(1)}, bf16[256,640]{1,0:T(8,128)(2,1)S(1)}, u32[]{:S(2)}, u32[]{:S(2)}) collective-permute-start(bf16[256,640]{1,0:T(8,128)(2,1)S(1)} %get-tuple-element.27), channel_id=1, source_target_pairs={{0,2},{2,0},{4,6},{6,4},{8,10},{10,8},{12,14},{14,12},{1,3},{3,1},... | collective-permute-start | bytes 983048 | tf_op jit(solution)/shard_map/ppermute | solution.py:25
  10.9 19.0 %collective-permute-start.5 = (bf16[256,640]{1,0:T(8,128)(2,1)S(1)}, bf16[256,640]{1,0:T(8,128)(2,1)S(1)}, u32[]{:S(2)}, u32[]{:S(2)}) collective-permute-start(bf16[256,640]{1,0:T(8,128)(2,1)S(1)} %get-tuple-element.36), channel_id=1, source_target_pairs={{0,2},{2,0},{4,6},{6,4},{8,10},{10,8},{12,14},{14,12},{1,3},{3,1},... | collective-permute-start | bytes 983048 | tf_op jit(solution)/shard_map/ppermute | solution.py:25
  11.2 12.9 %collective-permute-start.2 = (bf16[512,256]{1,0:T(8,128)(2,1)S(1)}, bf16[512,256]{1,0:T(8,128)(2,1)S(1)}, u32[]{:S(2)}, u32[]{:S(2)}) collective-permute-start(bf16[512,256]{1,0:T(8,128)(2,1)S(1)} %shard_map.94), channel_id=1, source_target_pairs={{0,4},{2,6},{4,0},{6,2},{8,12},{10,14},{12,8},{14,10},{1,5},{3,7},... | collective-permute-start | bytes 786440 | tf_op jit(solution)/shard_map/ppermute | solution.py:25
  16.8 7.3 %collective-permute-start.3 = (bf16[512,256]{1,0:T(8,128)(2,1)S(1)}, bf16[512,256]{1,0:T(8,128)(2,1)S(1)}, u32[]{:S(2)}, u32[]{:S(2)}) collective-permute-start(bf16[512,256]{1,0:T(8,128)(2,1)S(1)} %shard_map.95), channel_id=1, source_target_pairs={{0,4},{2,6},{4,0},{6,2},{8,12},{10,14},{12,8},{14,10},{1,5},{3,7},... | collective-permute-start | bytes 786440 | tf_op jit(solution)/shard_map/ppermute | solution.py:25
  27.7 3.5 %collective-permute-start.8 = (f32[8,128]{1,0:T(8,128)S(1)}, f32[8,128]{1,0:T(8,128)S(1)}, u32[]{:S(2)}, u32[]{:S(2)}) collective-permute-start(f32[8,128]{1,0:T(8,128)S(1)} %get-tuple-element.40.part_ref), channel_id=1, source_target_pairs={{0,3},{1,2},{2,1},{3,0},{4,7},{5,6},{6,5},{7,4},{8,11},{9,10},{10,... | collective-permute-start | bytes 12296 | tf_op jit(solution)/shard_map/ppermute | solution.py:464
  27.8 3.7 %collective-permute-start.7 = (f32[8,128]{1,0:T(8,128)S(1)}, f32[8,128]{1,0:T(8,128)S(1)}, u32[]{:S(2)}, u32[]{:S(2)}) collective-permute-start(f32[8,128]{1,0:T(8,128)S(1)} %get-tuple-element.40.part_ref), channel_id=1, source_target_pairs={{0,2},{2,0},{4,6},{6,4},{8,10},{10,8},{12,14},{14,12},{1,3},{3,1},... | collective-permute-start | bytes 12296 | tf_op jit(solution)/shard_map/ppermute | solution.py:25
  28.6 2.9 %collective-permute-start.6 = (f32[8,128]{1,0:T(8,128)S(1)}, f32[8,128]{1,0:T(8,128)S(1)}, u32[]{:S(2)}, u32[]{:S(2)}) collective-permute-start(f32[8,128]{1,0:T(8,128)S(1)} %get-tuple-element.40.part_ref), channel_id=1, source_target_pairs={{0,1},{1,0},{2,3},{3,2},{4,5},{5,4},{6,7},{7,6},{8,9},{9,8},{10,11... | collective-permute-start | bytes 12296 | tf_op jit(solution)/shard_map/ppermute | solution.py:25

commit v6 on v5

--- a/solution.py
+++ b/solution.py
@@ -13,7 +13,6 @@
 FACTOR = HD ** (-0.5) * LOG2E
 BARRED = -1e30
 LAST_HEADS = 5
-TAIL_HEADS = 3
 COST = 10
 VMEM_LIMIT = 12 * 1024 * 1024
 ANY = pl.BlockSpec(memory_space=pl.ANY)
@@ -183,15 +182,22 @@
 
 
 def first_kernel(
-    ratio, block, facts_ref, weight_ref, q_ref, o_ref, sum_ref, peak_ref, k_ref, v_ref, out_ref, part_ref, k_buf, v_buf
+    ratio, block, facts_ref, weight_ref, q_ref, o_ref, sum_ref, peak_ref, k_ref, v_ref,
+    out_ref, part_ref, k_buf, v_buf, out_buf, sems,
 ):
     span, heads = q_ref.shape[0], q_ref.shape[1] // HD
     valid = valid_of(facts_ref, OWN_VALID)
     for group in range(heads // ratio):
         load_span(k_buf.at[group], v_buf.at[group], k_ref, v_ref, group, valid_of(facts_ref, PARTNER_VALID), 0)
 
+    def out_copy(head):
+        columns = pl.ds(head * HD, HD)
+        return pltpu.make_async_copy(out_buf.at[:, columns], out_ref.at[:, columns], sems.at[head])
+
     def keep(rows, columns, output):
-        out_ref[rows, columns] = output
+        out_buf[rows, columns] = output
+        if rows.stop == span:
+            out_copy(columns.start // HD).start()
 
     works, totals = [], []
     for head in range(heads):
@@ -205,6 +211,8 @@
             )
     in_turn(works)
     part_ref[...] = weigh_totals(totals, weight_ref, facts_ref, OWN_VALID)
+    for head in range(heads):
+        out_copy(head).wait()
 
 
 def lose_works(facts_ref, low, high, ratio, q_ref, k_buf, v_buf, totals, out_ref, then=None):
@@ -275,9 +283,13 @@
 
 def lose_kernel(
     ratio, high, facts_ref, weight_ref, ka_ref, va_ref, kb_ref, vb_ref, piece_ref, first_ref, second_ref, won_part_ref,
-    out_ref, part_ref, k_wide, v_wide,
+    out_ref, part_ref, second_out, k_wide, v_wide, sems,
 ):
     span = ka_ref.shape[0]
+
+    def lost_copy(head):
+        columns = pl.ds(head * HD, HD)
+        return pltpu.make_async_copy(out_ref.at[:, columns], second_out.at[:, columns], sems.at[head])
 
     @pl.when(jnp.logical_not(has_won(facts_ref)))
     def _():
@@ -286,44 +298,30 @@
             load_span(own_k, own_v, ka_ref, va_ref, group, valid_of(facts_ref, PARTNER_VALID), 0)
             load_span(own_k, own_v, kb_ref, vb_ref, group, valid_of(facts_ref, RIVAL_VALID), span)
         totals = []
-        in_turn(lose_works(facts_ref, 0, high, ratio, piece_ref, k_wide, v_wide, totals, out_ref))
+        works = lose_works(
+            facts_ref, 0, high, ratio, piece_ref, k_wide, v_wide, totals, out_ref, lambda head: lost_copy(head).start()
+        )
+        in_turn(works)
         give_part(part_ref, weigh_totals(totals, weight_ref, facts_ref, PARTNER_VALID), first_ref)
+        for head in range(high):
+            lost_copy(head).wait()
 
 
 def last_kernel(
-    ratio, low, facts_ref, k_wide, v_wide, piece_ref, first_ref, second_ref, first_out, second_out, out_ref, sems
+    ratio, low, facts_ref, k_wide, v_wide, piece_ref, second_ref, before_ref, second_out, out_ref, sem
 ):
     won = has_won(facts_ref)
-    heads = second_ref.shape[1] // HD
-    before, after = pl.ds(0, low * HD), pl.ds(low * HD, (heads - low) * HD)
-    first_copy = pltpu.make_async_copy(first_ref, first_out, sems.at[0])
-    before_copy = pltpu.make_async_copy(second_ref.at[:, before], second_out.at[:, before], sems.at[1])
-    won_copy = pltpu.make_async_copy(second_ref.at[:, after], second_out.at[:, after], sems.at[2])
-
-    def lost_copy(head):
-        columns = pl.ds(head * HD, HD)
-        return pltpu.make_async_copy(out_ref.at[:, columns], second_out.at[:, columns], sems.at[3 + head - low])
-
-    first_copy.start()
-    before_copy.start()
 
     @pl.when(won)
     def _():
+        won_copy = pltpu.make_async_copy(second_ref, second_out, sem)
         won_copy.start()
         won_copy.wait()
 
     @pl.when(jnp.logical_not(won))
     def _():
-        def copy_out(head):
-            if head < heads - TAIL_HEADS:
-                lost_copy(head).start()
-
-        in_turn(lose_works(facts_ref, low, heads, ratio, piece_ref, k_wide, v_wide, [], out_ref, copy_out))
-        for head in range(low, heads - TAIL_HEADS):
-            lost_copy(head).wait()
-
-    first_copy.wait()
-    before_copy.wait()
+        heads = out_ref.shape[1] // HD
+        in_turn(lose_works(facts_ref, low, heads, ratio, piece_ref, k_wide, v_wide, [], out_ref))
 
 
 def final_kernel(
@@ -331,7 +329,7 @@
     first_buf, final_buf, sems,
 ):
     won = has_won(facts_ref)
-    width = TAIL_HEADS * HD
+    width = LAST_HEADS * HD
     columns = pl.ds(second_out.shape[1] - width, width)
     tail_copy = pltpu.make_async_copy(lost_ref.at[:, columns], second_out.at[:, columns], sems.at[2])
 
@@ -423,8 +421,8 @@
         (facts, weight, queries, *own, companion_keys, companion_values),
         [VMEM] * 8,
         (first_shape, part_shape),
-        (VMEM, VMEM),
-        buffers(1),
+        (ANY, VMEM),
+        buffers(1) + [pltpu.VMEM((span, width), dtype), pltpu.SemaphoreType.DMA((heads,))],
         share * heads // 2,
     )
     second, part = kernel_call(
@@ -437,24 +435,25 @@
         share * middle,
     )
     wide_shape = jax.ShapeDtypeStruct((groups, 2 * span, HD + LANES), dtype)
-    second, part, *wide = kernel_call(
+    second, part, before, *wide = kernel_call(
         functools.partial(lose_kernel, ratio, middle),
         (facts, weight, companion_keys, companion_values, rival_keys, rival_values, pieces[0], first_part, second, part),
         [VMEM] * 10,
-        (second_shape, part_shape, wide_shape, wide_shape),
-        (VMEM,) * 4,
-        (),
+        (second_shape, part_shape, second_shape, wide_shape, wide_shape),
+        (VMEM, VMEM, ANY, VMEM, VMEM),
+        [pltpu.SemaphoreType.DMA((middle,))],
         share * middle,
         {8: 0, 9: 1},
     )
-    first, second, lost = kernel_call(
+    second, lost = kernel_call(
         functools.partial(last_kernel, ratio, middle),
-        (facts, *wide, pieces[1], first, second),
-        [VMEM] * 6,
-        (first_shape, second_shape, second_shape),
-        (ANY, ANY, VMEM),
-        [pltpu.SemaphoreType.DMA((3 + LAST_HEADS,))],
+        (facts, *wide, pieces[1], second, before),
+        [VMEM] * 5 + [ANY],
+        (second_shape, second_shape),
+        (ANY, VMEM),
+        [pltpu.SemaphoreType.DMA(())],
         share // 16,
+        {5: 0},
     )
 
     cores = lax.axis_size("head")

time: 33 us -> 32.8 us (level)
  transfers between devices with their start and end apart: 9 -> 9, of which waited for: 4 -> 5; matrix products, arithmetic and copies ran while one was open for 0% -> 0% of each run, Pallas kernels for 45% -> 46%
where the time goes in v6:
time: 32.8 us; the launch traced here: 32.4 us
  Pallas kernels  15.5 us (47%)
  starting transfers between devices  11.5 us (35%)
  waiting for transfers between devices  4.38 us (13%)
  between operations  0.91 us (3%)
    pallas_call x8, Pallas kernels, kernel_call(): pl.pallas_call(kernel, out_shape=out_shape, in_specs=in_specs, out_specs=...  15.5 us
    ppermute x8, starting transfers between devices, from_partner(): lax.ppermute(value, axis, [(i, i ^ 1 << stride) for i in range(lax.axis_s...  11.4 us
    ppermute x8, waiting for transfers between devices, from_partner(): lax.ppermute(value, axis, [(i, i ^ 1 << stride) for i in range(lax.axis_s...  4.33 us
  transfers between devices with their start and end apart: 9, of which 5 were waited for; matrix products, arithmetic and copies ran while one was open for 0% of the time, Pallas kernels for 46%

profile of v6, /device:TPU:0, one launch (start us, length us, event | category | flops | bytes accessed | tf_op | source)
XLA Modules:
  0.0 32.4 jit_solution(11394003858711101509)
XLA Ops:
  0.7 3.0 %collective-permute-start = (bf16[512,256]{1,0:T(8,128)(2,1)}, bf16[512,256]{1,0:T(8,128)(2,1)S(1)}, u32[]{:S(2)}, u32[]{:S(2)}) collective-permute-start(bf16[512,256]{1,0:T(8,128)(2,1)} %own_ref.2), channel_id=1, source_target_pairs={{0,2},{2,0},{4,6},{6,4},{8,10},{10,8},{12,14},{14,12},{1,3},{3,1},... | collective-permute-start | bytes 786440 | tf_op jit(solution)/shard_map/ppermute | solution.py:24
  3.7 0.1 collective-permute-start.1
  3.8 5.1 %shard_map.93 = (f32[512,1280]{1,0:T(8,128)S(1)}, f32[512,1280]{1,0:T(8,128)S(1)}, f32[512,1280]{1,0:T(8,128)S(1)}, f32[8,128]{1,0:T(8,128)S(1)}, bf16[256,640]{...) custom-call(s32[8]{0:T(128)} %lengths_hbm.1, s32[4]{0:T(128)} %winners_hbm.1, bf16[512,1280]{1,0:T(8,128)(2,1)} %q_ref.3, ...), custom_call_target="tpu_custom_call" | custom-call | flops 13421772800 | bytes 52428800 | tf_op jit(solution)/shard_map/pallas_call | solution.py:358
  8.9 2.0 %collective-permute-start.4 = (bf16[256,640]{1,0:T(8,128)(2,1)S(1)}, bf16[256,640]{1,0:T(8,128)(2,1)S(1)}, u32[]{:S(2)}, u32[]{:S(2)}) collective-permute-start(bf16[256,640]{1,0:T(8,128)(2,1)S(1)} %get-tuple-element.31), channel_id=1, source_target_pairs={{0,2},{2,0},{4,6},{6,4},{8,10},{10,8},{12,14},{14,12},{1,3},{3,1},... | collective-permute-start | bytes 983048 | tf_op jit(solution)/shard_map/ppermute | solution.py:24
  10.9 0.1 collective-permute-start.8
  11.0 0.0 collective-permute-done.companion_ref.k_ref.ka_ref
  11.0 0.1 shard_map.94
  11.2 2.2 %collective-permute-start.2 = (bf16[512,256]{1,0:T(8,128)(2,1)S(1)}, bf16[512,256]{1,0:T(8,128)(2,1)S(1)}, u32[]{:S(2)}, u32[]{:S(2)}) collective-permute-start(bf16[512,256]{1,0:T(8,128)(2,1)S(1)} %shard_map.94), channel_id=1, source_target_pairs={{0,4},{2,6},{4,0},{6,2},{8,12},{10,14},{12,8},{14,10},{1,5},{3,7},... | collective-permute-start | bytes 786440 | tf_op jit(solution)/shard_map/ppermute | solution.py:24
  13.4 3.3 %collective-permute-done.1.v_ref.companion_ref.va_ref = bf16[512,256]{1,0:T(8,128)(2,1)S(1)} collective-permute-done((bf16[512,256]{1,0:T(8,128)(2,1)}, bf16[512,256]{1,0:T(8,128)(2,1)S(1)}, u32[]{:S(2)}, u32[]{:S(2)}) %collective-permute-start.1) | collective-permute-done | bytes 262176 | tf_op jit(solution)/shard_map/ppermute | solution.py:24
  16.6 0.1 shard_map.96
  16.8 2.2 %collective-permute-start.3 = (bf16[512,256]{1,0:T(8,128)(2,1)S(1)}, bf16[512,256]{1,0:T(8,128)(2,1)S(1)}, u32[]{:S(2)}, u32[]{:S(2)}) collective-permute-start(bf16[512,256]{1,0:T(8,128)(2,1)S(1)} %shard_map.96), channel_id=1, source_target_pairs={{0,4},{2,6},{4,0},{6,2},{8,12},{10,14},{12,8},{14,10},{1,5},{3,7},... | collective-permute-start | bytes 786440 | tf_op jit(solution)/shard_map/ppermute | solution.py:24
  19.0 4.8 %shard_map.95 = (bf16[512,1280]{1,0:T(8,128)(2,1)}, f32[8,128]{1,0:T(8,128)S(1)}) custom-call(f32[8,128]{1,0:T(8,128)S(1)} %get-tuple-element.25.facts_ref, f32[1,1280]{1,0:T(1,128)S(1)} %reshape.11.weight_ref, bf16[512,1280]{1,0:T(8,128)(2,1)S(1)} %copy-done.2, f32[512,1280]{1,0:T(8,128)S(1)} %get-tuple-element.26.o_ref, ...), custom_call_target="tpu_custom_call" | custom-call | flops 6710886400 | bytes 26214400 | tf_op jit(solution)/shard_map/pallas_call | solution.py:358
  23.8 0.2 collective-permute-done.3.v_ref.vb_ref
  24.0 3.5 %shard_map.97 = (bf16[256,1280]{1,0:T(8,128)(2,1)S(1)}, f32[8,128]{1,0:T(8,128)S(1)}) custom-call(f32[8,128]{1,0:T(8,128)S(1)} %get-tuple-element.25.facts_ref, f32[1,1280]{1,0:T(1,128)S(1)} %reshape.11.weight_ref, bf16[512,1280]{1,0:T(8,128)(2,1)S(1)} %copy-done.2, f32[512,1280]{1,0:T(8,128)S(1)} %get-tuple-element.26.o_ref, ...), custom_call_target="tpu_custom_call" | custom-call | flops 6710886400 | bytes 26214400 | tf_op jit(solution)/shard_map/pallas_call | solution.py:358
  27.6 0.2 shard_map.98
  27.8 0.1 collective-permute-start.7
  27.9 1.3 %collective-permute-start.6 = (f32[8,128]{1,0:T(8,128)S(1)}, f32[8,128]{1,0:T(8,128)S(1)}, u32[]{:S(2)}, u32[]{:S(2)}) collective-permute-start(f32[8,128]{1,0:T(8,128)S(1)} %get-tuple-element.35.part_ref), channel_id=1, source_target_pairs={{0,2},{2,0},{4,6},{6,4},{8,10},{10,8},{12,14},{14,12},{1,3},{3,1},... | collective-permute-start | bytes 12296 | tf_op jit(solution)/shard_map/ppermute | solution.py:24
  29.2 0.6 %collective-permute-start.5 = (f32[8,128]{1,0:T(8,128)S(1)}, f32[8,128]{1,0:T(8,128)S(1)}, u32[]{:S(2)}, u32[]{:S(2)}) collective-permute-start(f32[8,128]{1,0:T(8,128)S(1)} %get-tuple-element.35.part_ref), channel_id=1, source_target_pairs={{0,1},{1,0},{2,3},{3,2},{4,5},{5,4},{6,7},{7,6},{8,9},{9,8},{10,11... | collective-permute-start | bytes 12296 | tf_op jit(solution)/shard_map/ppermute | solution.py:24
  29.7 0.1 collective-permute-done.8.piece_ref
  29.9 1.0 %shard_map.99 = (bf16[256,1280]{1,0:T(8,128)(2,1)}, bf16[256,1280]{1,0:T(8,128)(2,1)S(1)}) custom-call(f32[8,128]{1,0:T(8,128)S(1)} %get-tuple-element.25.facts_ref, bf16[2,1024,256]{2,1,0:T(8,128)(2,1)S(1)} %get-tuple-element.36.k_wide, bf16[2,1024,256]{2,1,0:T(8,128)(2,1)S(1)} %get-tuple-element.37.v_wide, ...), custom_call_target="tpu_custom_call", output_to_operand_aliasing={{0}: (5, {})} | custom-call | flops 83886080 | bytes 327680 | tf_op jit(solution)/shard_map/pallas_call | solution.py:358
  30.8 0.1 collective-permute-done.7.diagonal_ref
  30.9 0.7 %collective-permute-done.6.across_ref = f32[8,128]{1,0:T(8,128)S(1)} collective-permute-done((f32[8,128]{1,0:T(8,128)S(1)}, f32[8,128]{1,0:T(8,128)S(1)}, u32[]{:S(2)}, u32[]{:S(2)}) %collective-permute-start.6) | collective-permute-done | bytes 4128 | tf_op jit(solution)/shard_map/ppermute | solution.py:24
  31.5 0.0 collective-permute-done.5.beside_ref
  31.5 0.7 %shard_map.100 = (bf16[256,1280]{1,0:T(8,128)(2,1)}, f32[1]{0:T(128)}, f32[1]{0:T(128)}) custom-call(f32[8,128]{1,0:T(8,128)S(1)} %get-tuple-element.25.facts_ref, f32[8,128]{1,0:T(8,128)S(1)} %get-tuple-element.35.part_ref, f32[8,128]{1,0:T(8,128)S(1)} %collective-permute-done.5.beside_ref, ...), custom_call_target="tpu_custom_call", output_to_operand_aliasing={{0}: (6, {})} | custom-call | flops 83886080 | bytes 327680 | tf_op jit(solution)/shard_map/pallas_call | solution.py:358
  (11 shorter events, 0.0 us)
Async XLA Ops:
  0.6 10.4 %copy-start = (bf16[512,256]{1,0:T(8,128)(2,1)S(1)}, bf16[512,256]{1,0:T(8,128)(2,1)}, u32[]{:S(2)}) copy-start(bf16[512,256]{1,0:T(8,128)(2,1)} %own_ref.2) | copy-start | bytes 786436
  0.6 16.0 %copy-start.1 = (bf16[512,256]{1,0:T(8,128)(2,1)S(1)}, bf16[512,256]{1,0:T(8,128)(2,1)}, u32[]{:S(2)}) copy-start(bf16[512,256]{1,0:T(8,128)(2,1)} %own_ref.3) | copy-start | bytes 786436
  0.7 18.3 %copy-start.2 = (bf16[512,1280]{1,0:T(8,128)(2,1)S(1)}, bf16[512,1280]{1,0:T(8,128)(2,1)}, u32[]{:S(2)}) copy-start(bf16[512,1280]{1,0:T(8,128)(2,1)} %q_ref.3) | copy-start | bytes 3932164
  0.7 10.3 %copy-start.3 = (f32[1280]{0:T(1024)S(1)}, f32[1280]{0:T(1024)}, u32[]{:S(2)}) copy-start(f32[1280]{0:T(1024)} %param.11) | copy-start | bytes 15364
  0.7 10.3 %collective-permute-start = (bf16[512,256]{1,0:T(8,128)(2,1)}, bf16[512,256]{1,0:T(8,128)(2,1)S(1)}, u32[]{:S(2)}, u32[]{:S(2)}) collective-permute-start(bf16[512,256]{1,0:T(8,128)(2,1)} %own_ref.2), channel_id=1, source_target_pairs={{0,2},{2,0},{4,6},{6,4},{8,10},{10,8},{12,14},{14,12},{1,3},{3,1},... | collective-permute-start | bytes 786440 | tf_op jit(solution)/shard_map/ppermute | solution.py:24
  3.7 13.0 %collective-permute-start.1 = (bf16[512,256]{1,0:T(8,128)(2,1)}, bf16[512,256]{1,0:T(8,128)(2,1)S(1)}, u32[]{:S(2)}, u32[]{:S(2)}) collective-permute-start(bf16[512,256]{1,0:T(8,128)(2,1)} %own_ref.3), channel_id=1, source_target_pairs={{0,2},{2,0},{4,6},{6,4},{8,10},{10,8},{12,14},{14,12},{1,3},{3,1},... | collective-permute-start | bytes 786440 | tf_op jit(solution)/shard_map/ppermute | solution.py:24
  8.9 18.7 %collective-permute-start.4 = (bf16[256,640]{1,0:T(8,128)(2,1)S(1)}, bf16[256,640]{1,0:T(8,128)(2,1)S(1)}, u32[]{:S(2)}, u32[]{:S(2)}) collective-permute-start(bf16[256,640]{1,0:T(8,128)(2,1)S(1)} %get-tuple-element.31), channel_id=1, source_target_pairs={{0,2},{2,0},{4,6},{6,4},{8,10},{10,8},{12,14},{14,12},{1,3},{3,1},... | collective-permute-start | bytes 983048 | tf_op jit(solution)/shard_map/ppermute | solution.py:24
  10.9 19.0 %collective-permute-start.8 = (bf16[256,640]{1,0:T(8,128)(2,1)S(1)}, bf16[256,640]{1,0:T(8,128)(2,1)S(1)}, u32[]{:S(2)}, u32[]{:S(2)}) collective-permute-start(bf16[256,640]{1,0:T(8,128)(2,1)S(1)} %get-tuple-element.38), channel_id=1, source_target_pairs={{0,2},{2,0},{4,6},{6,4},{8,10},{10,8},{12,14},{14,12},{1,3},{3,1},... | collective-permute-start | bytes 983048 | tf_op jit(solution)/shard_map/ppermute | solution.py:24
  11.2 12.9 %collective-permute-start.2 = (bf16[512,256]{1,0:T(8,128)(2,1)S(1)}, bf16[512,256]{1,0:T(8,128)(2,1)S(1)}, u32[]{:S(2)}, u32[]{:S(2)}) collective-permute-start(bf16[512,256]{1,0:T(8,128)(2,1)S(1)} %shard_map.94), channel_id=1, source_target_pairs={{0,4},{2,6},{4,0},{6,2},{8,12},{10,14},{12,8},{14,10},{1,5},{3,7},... | collective-permute-start | bytes 786440 | tf_op jit(solution)/shard_map/ppermute | solution.py:24
  16.8 7.3 %collective-permute-start.3 = (bf16[512,256]{1,0:T(8,128)(2,1)S(1)}, bf16[512,256]{1,0:T(8,128)(2,1)S(1)}, u32[]{:S(2)}, u32[]{:S(2)}) collective-permute-start(bf16[512,256]{1,0:T(8,128)(2,1)S(1)} %shard_map.96), channel_id=1, source_target_pairs={{0,4},{2,6},{4,0},{6,2},{8,12},{10,14},{12,8},{14,10},{1,5},{3,7},... | collective-permute-start | bytes 786440 | tf_op jit(solution)/shard_map/ppermute | solution.py:24
  27.8 3.1 %collective-permute-start.7 = (f32[8,128]{1,0:T(8,128)S(1)}, f32[8,128]{1,0:T(8,128)S(1)}, u32[]{:S(2)}, u32[]{:S(2)}) collective-permute-start(f32[8,128]{1,0:T(8,128)S(1)} %get-tuple-element.35.part_ref), channel_id=1, source_target_pairs={{0,3},{1,2},{2,1},{3,0},{4,7},{5,6},{6,5},{7,4},{8,11},{9,10},{10,... | collective-permute-start | bytes 12296 | tf_op jit(solution)/shard_map/ppermute | solution.py:463
  27.9 3.7 %collective-permute-start.6 = (f32[8,128]{1,0:T(8,128)S(1)}, f32[8,128]{1,0:T(8,128)S(1)}, u32[]{:S(2)}, u32[]{:S(2)}) collective-permute-start(f32[8,128]{1,0:T(8,128)S(1)} %get-tuple-element.35.part_ref), channel_id=1, source_target_pairs={{0,2},{2,0},{4,6},{6,4},{8,10},{10,8},{12,14},{14,12},{1,3},{3,1},... | collective-permute-start | bytes 12296 | tf_op jit(solution)/shard_map/ppermute | solution.py:24
  29.2 2.4 %collective-permute-start.5 = (f32[8,128]{1,0:T(8,128)S(1)}, f32[8,128]{1,0:T(8,128)S(1)}, u32[]{:S(2)}, u32[]{:S(2)}) collective-permute-start(f32[8,128]{1,0:T(8,128)S(1)} %get-tuple-element.35.part_ref), channel_id=1, source_target_pairs={{0,1},{1,0},{2,3},{3,2},{4,5},{5,4},{6,7},{7,6},{8,9},{9,8},{10,11... | collective-permute-start | bytes 12296 | tf_op jit(solution)/shard_map/ppermute | solution.py:24

commit v7 on v6

--- a/solution.py
+++ b/solution.py
@@ -85,8 +85,8 @@
     return jnp.where(row < valid_rows, above / below, 0.0).astype(dtype)
 
 
-def in_turn(works):
-    scores = works[0][0]()
+def in_turn(works, scores=None):
+    scores = works[0][0]() if scores is None else scores
     for index, (_, finish_work) in enumerate(works):
         later = works[index + 1][0]() if index + 1 < len(works) else None
         finish_work(scores)
@@ -310,6 +310,8 @@
 def last_kernel(
     ratio, low, facts_ref, k_wide, v_wide, piece_ref, second_ref, before_ref, second_out, out_ref, sem
 ):
+    works = lose_works(facts_ref, low, out_ref.shape[1] // HD, ratio, piece_ref, k_wide, v_wide, [], out_ref)
+    scores = works[0][0]()
     won = has_won(facts_ref)
 
     @pl.when(won)
@@ -320,8 +322,7 @@
 
     @pl.when(jnp.logical_not(won))
     def _():
-        heads = out_ref.shape[1] // HD
-        in_turn(lose_works(facts_ref, low, heads, ratio, piece_ref, k_wide, v_wide, [], out_ref))
+        in_turn(works, scores)
 
 
 def final_kernel(

time: 32.8 us -> 33.1 us (level)
  Pallas kernels: 15.5 us -> 16.4 us
  waiting for transfers between devices: 4.38 us -> 3.77 us
    pallas_call x8, Pallas kernels: 15.5 us -> 16.4 us  [kernel_call(): pl.pallas_call(kernel, out_shape=out_shape, in_specs=in_specs, out_specs=...]
    ppermute x8, waiting for transfers between devices: 4.33 us -> 3.77 us  [from_partner(): lax.ppermute(value, axis, [(i, i ^ 1 << stride) for i in range(lax.axis_s...]
  transfers between devices with their start and end apart: 9 -> 9, of which waited for: 5 -> 3; matrix products, arithmetic and copies ran while one was open for 0% -> 0% of each run, Pallas kernels for 46% -> 47%
where the time goes in v7:
time: 33.1 us; the launch traced here: 33 us
  Pallas kernels  16.4 us (50%)
  starting transfers between devices  11.8 us (36%)
  waiting for transfers between devices  3.77 us (11%)
  between operations  0.93 us (3%)
    pallas_call x8, Pallas kernels, kernel_call(): pl.pallas_call(kernel, out_shape=out_shape, in_specs=in_specs, out_specs=...  16.4 us
    ppermute x8, starting transfers between devices, from_partner(): lax.ppermute(value, axis, [(i, i ^ 1 << stride) for i in range(lax.axis_s...  11.8 us
    ppermute x8, waiting for transfers between devices, from_partner(): lax.ppermute(value, axis, [(i, i ^ 1 << stride) for i in range(lax.axis_s...  3.77 us
  transfers between devices with their start and end apart: 9, of which 3 were waited for; matrix products, arithmetic and copies ran while one was open for 0% of the time, Pallas kernels for 47%

profile of v7, /device:TPU:0, one launch (start us, length us, event | category | flops | bytes accessed | tf_op | source)
XLA Modules:
  0.0 33.0 jit_solution(3249846248468376934)
XLA Ops:
  0.7 3.0 %collective-permute-start = (bf16[512,256]{1,0:T(8,128)(2,1)}, bf16[512,256]{1,0:T(8,128)(2,1)S(1)}, u32[]{:S(2)}, u32[]{:S(2)}) collective-permute-start(bf16[512,256]{1,0:T(8,128)(2,1)} %own_ref.2), channel_id=1, source_target_pairs={{0,2},{2,0},{4,6},{6,4},{8,10},{10,8},{12,14},{14,12},{1,3},{3,1},... | collective-permute-start | bytes 786440 | tf_op jit(solution)/shard_map/ppermute | solution.py:24
  3.7 0.1 collective-permute-start.1
  3.8 5.1 %shard_map.93 = (f32[512,1280]{1,0:T(8,128)S(1)}, f32[512,1280]{1,0:T(8,128)S(1)}, f32[512,1280]{1,0:T(8,128)S(1)}, f32[8,128]{1,0:T(8,128)S(1)}, bf16[256,640]{...) custom-call(s32[8]{0:T(128)} %lengths_hbm.1, s32[4]{0:T(128)} %winners_hbm.1, bf16[512,1280]{1,0:T(8,128)(2,1)} %q_ref.3, ...), custom_call_target="tpu_custom_call" | custom-call | flops 13421772800 | bytes 52428800 | tf_op jit(solution)/shard_map/pallas_call | solution.py:359
  8.9 2.0 %collective-permute-start.4 = (bf16[256,640]{1,0:T(8,128)(2,1)S(1)}, bf16[256,640]{1,0:T(8,128)(2,1)S(1)}, u32[]{:S(2)}, u32[]{:S(2)}) collective-permute-start(bf16[256,640]{1,0:T(8,128)(2,1)S(1)} %get-tuple-element.31), channel_id=1, source_target_pairs={{0,2},{2,0},{4,6},{6,4},{8,10},{10,8},{12,14},{14,12},{1,3},{3,1},... | collective-permute-start | bytes 983048 | tf_op jit(solution)/shard_map/ppermute | solution.py:24
  10.9 0.1 collective-permute-start.8
  11.0 0.0 collective-permute-done.companion_ref.k_ref.ka_ref
  11.0 0.1 shard_map.94
  11.2 2.2 %collective-permute-start.2 = (bf16[512,256]{1,0:T(8,128)(2,1)S(1)}, bf16[512,256]{1,0:T(8,128)(2,1)S(1)}, u32[]{:S(2)}, u32[]{:S(2)}) collective-permute-start(bf16[512,256]{1,0:T(8,128)(2,1)S(1)} %shard_map.94), channel_id=1, source_target_pairs={{0,4},{2,6},{4,0},{6,2},{8,12},{10,14},{12,8},{14,10},{1,5},{3,7},... | collective-permute-start | bytes 786440 | tf_op jit(solution)/shard_map/ppermute | solution.py:24
  13.4 3.3 %collective-permute-done.1.v_ref.companion_ref.va_ref = bf16[512,256]{1,0:T(8,128)(2,1)S(1)} collective-permute-done((bf16[512,256]{1,0:T(8,128)(2,1)}, bf16[512,256]{1,0:T(8,128)(2,1)S(1)}, u32[]{:S(2)}, u32[]{:S(2)}) %collective-permute-start.1) | collective-permute-done | bytes 262176 | tf_op jit(solution)/shard_map/ppermute | solution.py:24
  16.6 0.1 shard_map.96
  16.8 2.2 %collective-permute-start.3 = (bf16[512,256]{1,0:T(8,128)(2,1)S(1)}, bf16[512,256]{1,0:T(8,128)(2,1)S(1)}, u32[]{:S(2)}, u32[]{:S(2)}) collective-permute-start(bf16[512,256]{1,0:T(8,128)(2,1)S(1)} %shard_map.96), channel_id=1, source_target_pairs={{0,4},{2,6},{4,0},{6,2},{8,12},{10,14},{12,8},{14,10},{1,5},{3,7},... | collective-permute-start | bytes 786440 | tf_op jit(solution)/shard_map/ppermute | solution.py:24
  19.0 4.8 %shard_map.95 = (bf16[512,1280]{1,0:T(8,128)(2,1)}, f32[8,128]{1,0:T(8,128)S(1)}) custom-call(f32[8,128]{1,0:T(8,128)S(1)} %get-tuple-element.25.facts_ref, f32[1,1280]{1,0:T(1,128)S(1)} %reshape.11.weight_ref, bf16[512,1280]{1,0:T(8,128)(2,1)S(1)} %copy-done.2, f32[512,1280]{1,0:T(8,128)S(1)} %get-tuple-element.26.o_ref, ...), custom_call_target="tpu_custom_call" | custom-call | flops 6710886400 | bytes 26214400 | tf_op jit(solution)/shard_map/pallas_call | solution.py:359
  23.8 0.2 collective-permute-done.3.v_ref.vb_ref
  24.0 0.0 collective-permute-done.2.k_ref.kb_ref
  24.0 0.3 shard_map.97
  24.4 0.0 collective-permute-done.4.piece_ref
  24.4 3.0 %shard_map.98 = (bf16[256,1280]{1,0:T(8,128)(2,1)S(1)}, f32[8,128]{1,0:T(8,128)S(1)}, bf16[256,1280]{1,0:T(8,128)(2,1)}, bf16[2,1024,256]{2,1,0:T(8,128)(2,1)S(1)}, bf16[2,1024,256]{2,1,0:T(8,128)(2,1)S(1)}) custom-call(f32[8,128]{1,0:T(8,128)S(1)} %get-tuple-element.25.facts_ref, ...), custom_call_target="tpu_custom_call", output_to_operand_aliasing={{0}: (8, {}), {1}: (9, {})} | custom-call | flops 6710886400 | bytes 26214400 | tf_op jit(solution)/shard_map/pallas_call | solution.py:359
  27.4 0.1 collective-permute-start.7
  27.4 2.1 %collective-permute-start.6 = (f32[8,128]{1,0:T(8,128)S(1)}, f32[8,128]{1,0:T(8,128)S(1)}, u32[]{:S(2)}, u32[]{:S(2)}) collective-permute-start(f32[8,128]{1,0:T(8,128)S(1)} %get-tuple-element.35.part_ref), channel_id=1, source_target_pairs={{0,2},{2,0},{4,6},{6,4},{8,10},{10,8},{12,14},{14,12},{1,3},{3,1},... | collective-permute-start | bytes 12296 | tf_op jit(solution)/shard_map/ppermute | solution.py:24
  29.6 0.0 collective-permute-start.5
  29.6 0.2 collective-permute-done.8.piece_ref
  29.9 2.1 %shard_map.99 = (bf16[256,1280]{1,0:T(8,128)(2,1)}, bf16[256,1280]{1,0:T(8,128)(2,1)S(1)}) custom-call(f32[8,128]{1,0:T(8,128)S(1)} %get-tuple-element.25.facts_ref, bf16[2,1024,256]{2,1,0:T(8,128)(2,1)S(1)} %get-tuple-element.36.k_wide, bf16[2,1024,256]{2,1,0:T(8,128)(2,1)S(1)} %get-tuple-element.37.v_wide, ...), custom_call_target="tpu_custom_call", output_to_operand_aliasing={{0}: (5, {})} | custom-call | flops 83886080 | bytes 327680 | tf_op jit(solution)/shard_map/pallas_call | solution.py:359
  31.9 0.0 collective-permute-done.6.across_ref
  31.9 0.9 %shard_map.100 = (bf16[256,1280]{1,0:T(8,128)(2,1)}, f32[1]{0:T(128)}, f32[1]{0:T(128)}) custom-call(f32[8,128]{1,0:T(8,128)S(1)} %get-tuple-element.25.facts_ref, f32[8,128]{1,0:T(8,128)S(1)} %get-tuple-element.35.part_ref, f32[8,128]{1,0:T(8,128)S(1)} %collective-permute-done.5.beside_ref, ...), custom_call_target="tpu_custom_call", output_to_operand_aliasing={{0}: (6, {})} | custom-call | flops 83886080 | bytes 327680 | tf_op jit(solution)/shard_map/pallas_call | solution.py:359
  (11 shorter events, 0.0 us)
Async XLA Ops:
  0.6 10.4 %copy-start = (bf16[512,256]{1,0:T(8,128)(2,1)S(1)}, bf16[512,256]{1,0:T(8,128)(2,1)}, u32[]{:S(2)}) copy-start(bf16[512,256]{1,0:T(8,128)(2,1)} %own_ref.2) | copy-start | bytes 786436
  0.6 16.0 %copy-start.1 = (bf16[512,256]{1,0:T(8,128)(2,1)S(1)}, bf16[512,256]{1,0:T(8,128)(2,1)}, u32[]{:S(2)}) copy-start(bf16[512,256]{1,0:T(8,128)(2,1)} %own_ref.3) | copy-start | bytes 786436
  0.7 18.3 %copy-start.2 = (bf16[512,1280]{1,0:T(8,128)(2,1)S(1)}, bf16[512,1280]{1,0:T(8,128)(2,1)}, u32[]{:S(2)}) copy-start(bf16[512,1280]{1,0:T(8,128)(2,1)} %q_ref.3) | copy-start | bytes 3932164
  0.7 10.3 %copy-start.3 = (f32[1280]{0:T(1024)S(1)}, f32[1280]{0:T(1024)}, u32[]{:S(2)}) copy-start(f32[1280]{0:T(1024)} %param.11) | copy-start | bytes 15364
  0.7 10.3 %collective-permute-start = (bf16[512,256]{1,0:T(8,128)(2,1)}, bf16[512,256]{1,0:T(8,128)(2,1)S(1)}, u32[]{:S(2)}, u32[]{:S(2)}) collective-permute-start(bf16[512,256]{1,0:T(8,128)(2,1)} %own_ref.2), channel_id=1, source_target_pairs={{0,2},{2,0},{4,6},{6,4},{8,10},{10,8},{12,14},{14,12},{1,3},{3,1},... | collective-permute-start | bytes 786440 | tf_op jit(solution)/shard_map/ppermute | solution.py:24
  3.7 13.0 %collective-permute-start.1 = (bf16[512,256]{1,0:T(8,128)(2,1)}, bf16[512,256]{1,0:T(8,128)(2,1)S(1)}, u32[]{:S(2)}, u32[]{:S(2)}) collective-permute-start(bf16[512,256]{1,0:T(8,128)(2,1)} %own_ref.3), channel_id=1, source_target_pairs={{0,2},{2,0},{4,6},{6,4},{8,10},{10,8},{12,14},{14,12},{1,3},{3,1},... | collective-permute-start | bytes 786440 | tf_op jit(solution)/shard_map/ppermute | solution.py:24
  8.9 15.5 %collective-permute-start.4 = (bf16[256,640]{1,0:T(8,128)(2,1)S(1)}, bf16[256,640]{1,0:T(8,128)(2,1)S(1)}, u32[]{:S(2)}, u32[]{:S(2)}) collective-permute-start(bf16[256,640]{1,0:T(8,128)(2,1)S(1)} %get-tuple-element.31), channel_id=1, source_target_pairs={{0,2},{2,0},{4,6},{6,4},{8,10},{10,8},{12,14},{14,12},{1,3},{3,1},... | collective-permute-start | bytes 983048 | tf_op jit(solution)/shard_map/ppermute | solution.py:24
  10.9 19.0 %collective-permute-start.8 = (bf16[256,640]{1,0:T(8,128)(2,1)S(1)}, bf16[256,640]{1,0:T(8,128)(2,1)S(1)}, u32[]{:S(2)}, u32[]{:S(2)}) collective-permute-start(bf16[256,640]{1,0:T(8,128)(2,1)S(1)} %get-tuple-element.38), channel_id=1, source_target_pairs={{0,2},{2,0},{4,6},{6,4},{8,10},{10,8},{12,14},{14,12},{1,3},{3,1},... | collective-permute-start | bytes 983048 | tf_op jit(solution)/shard_map/ppermute | solution.py:24
  11.2 12.9 %collective-permute-start.2 = (bf16[512,256]{1,0:T(8,128)(2,1)S(1)}, bf16[512,256]{1,0:T(8,128)(2,1)S(1)}, u32[]{:S(2)}, u32[]{:S(2)}) collective-permute-start(bf16[512,256]{1,0:T(8,128)(2,1)S(1)} %shard_map.94), channel_id=1, source_target_pairs={{0,4},{2,6},{4,0},{6,2},{8,12},{10,14},{12,8},{14,10},{1,5},{3,7},... | collective-permute-start | bytes 786440 | tf_op jit(solution)/shard_map/ppermute | solution.py:24
  16.8 7.3 %collective-permute-start.3 = (bf16[512,256]{1,0:T(8,128)(2,1)S(1)}, bf16[512,256]{1,0:T(8,128)(2,1)S(1)}, u32[]{:S(2)}, u32[]{:S(2)}) collective-permute-start(bf16[512,256]{1,0:T(8,128)(2,1)S(1)} %shard_map.96), channel_id=1, source_target_pairs={{0,4},{2,6},{4,0},{6,2},{8,12},{10,14},{12,8},{14,10},{1,5},{3,7},... | collective-permute-start | bytes 786440 | tf_op jit(solution)/shard_map/ppermute | solution.py:24
  27.4 4.6 %collective-permute-start.7 = (f32[8,128]{1,0:T(8,128)S(1)}, f32[8,128]{1,0:T(8,128)S(1)}, u32[]{:S(2)}, u32[]{:S(2)}) collective-permute-start(f32[8,128]{1,0:T(8,128)S(1)} %get-tuple-element.35.part_ref), channel_id=1, source_target_pairs={{0,3},{1,2},{2,1},{3,0},{4,7},{5,6},{6,5},{7,4},{8,11},{9,10},{10,... | collective-permute-start | bytes 12296 | tf_op jit(solution)/shard_map/ppermute | solution.py:464
  27.4 4.5 %collective-permute-start.6 = (f32[8,128]{1,0:T(8,128)S(1)}, f32[8,128]{1,0:T(8,128)S(1)}, u32[]{:S(2)}, u32[]{:S(2)}) collective-permute-start(f32[8,128]{1,0:T(8,128)S(1)} %get-tuple-element.35.part_ref), channel_id=1, source_target_pairs={{0,2},{2,0},{4,6},{6,4},{8,10},{10,8},{12,14},{14,12},{1,3},{3,1},... | collective-permute-start | bytes 12296 | tf_op jit(solution)/shard_map/ppermute | solution.py:24
  29.6 2.4 %collective-permute-start.5 = (f32[8,128]{1,0:T(8,128)S(1)}, f32[8,128]{1,0:T(8,128)S(1)}, u32[]{:S(2)}, u32[]{:S(2)}) collective-permute-start(f32[8,128]{1,0:T(8,128)S(1)} %get-tuple-element.35.part_ref), channel_id=1, source_target_pairs={{0,1},{1,0},{2,3},{3,2},{4,5},{5,4},{6,7},{7,6},{8,9},{9,8},{10,11... | collective-permute-start | bytes 12296 | tf_op jit(solution)/shard_map/ppermute | solution.py:24
